TPU v7x, 32 devices: a whole 2x2x4 slice. The times are simulated.
32 devices in a mesh: dp: 8 (over z, x), tensor: 4 (over y, core).
Axes of the slice: x: 2, y: 2, z: 4, core: 2. Of those that a mesh axis runs over, the one named last changes fastest.
Arguments:
- images: bfloat16 [24, 729, 1152], P('dp', None, 'tensor'), may hold values from -6 to 6
- image_count: int32 [8], P('dp'), may hold values from 2 to 3, as said below
- attn_gain: float32 [1152], replicated, may hold values from 0.5 to 1.5
- attn_shift: float32 [1152], replicated, may hold values from -1.8 to 1.8
- query_weight: bfloat16 [1152, 1152], P('dp', 'tensor'), may hold values from -0.25 to 0.25
- query_bias: float32 [1152], P('tensor'), may hold values from -3 to 3
- key_weight: bfloat16 [1152, 1152], P('dp', 'tensor'), may hold values from -0.25 to 0.25
- value_weight: bfloat16 [1152, 1152], P('dp', 'tensor'), may hold values from -0.1875 to 0.1875
- value_bias: float32 [1152], P('tensor'), may hold values from -3 to 3
- output_weight: bfloat16 [1152, 1152], P('tensor', 'dp'), may hold values from -1 to 1
- output_bias: float32 [1152], P('tensor'), may hold values from -3 to 3
- mlp_gain: float32 [1152], replicated, may hold values from 0.5 to 1.5
- mlp_shift: float32 [1152], replicated, may hold values from -1.8 to 1.8
- up_weight: bfloat16 [1152, 4304], P('dp', 'tensor'), may hold values from -0.1875 to 0.1875
- up_bias: float32 [4304], P('tensor'), may hold values from -3 to 3
- down_weight: bfloat16 [4304, 1152], P('tensor', 'dp'), may hold values from -0.125 to 0.125
- down_bias: float32 [1152], P('tensor'), may hold values from -3 to 3
- cotangent: bfloat16 [24, 729, 1152], P('dp', None, 'tensor'), may hold values from -6 to 6
Outputs:
- layer_out: bfloat16 [24, 729, 1152], P('dp', None, 'tensor')
- image_grad: bfloat16 [24, 729, 1152], P('dp', None, 'tensor')
- attn_gain_grad: float32 [1152], P('tensor')
- attn_shift_grad: float32 [1152], P('tensor')
- query_weight_grad: float32 [1152, 1152], P('dp', 'tensor')
- query_bias_grad: float32 [1152], P('tensor')
- key_weight_grad: float32 [1152, 1152], P('dp', 'tensor')
- value_weight_grad: float32 [1152, 1152], P('dp', 'tensor')
- value_bias_grad: float32 [1152], P('tensor')
- output_weight_grad: float32 [1152, 1152], P('tensor', 'dp')
- output_bias_grad: float32 [1152], P('tensor')
- mlp_gain_grad: float32 [1152], P('tensor')
- mlp_shift_grad: float32 [1152], P('tensor')
- up_weight_grad: float32 [1152, 4304], P('dp', 'tensor')
- up_bias_grad: float32 [4304], P('tensor')
- down_weight_grad: float32 [4304, 1152], P('tensor', 'dp')
- down_bias_grad: float32 [1152], P('tensor')
Inputs may be any that keep to these rules, and one draw needn't show every extreme that they name: Slots 0 to image_count - 1 of a data position hold its images; some position has 3 images and some has 2.
All inputs are finite; a program needn't handle non-finite values.
Results may differ from a plain program's by a relative error of at most 0.017.
Values may be sent and summed in bfloat16 or wider, within the bound.
No kernel may reach another device: no remote copies, remote signals or barrier semaphores. Data moves between devices by JAX's collectives and lax.ppermute only.
A program may use at most 256 MiB of HBM per device.

v0:
```python
import math

import jax
import jax.numpy as jnp
from jax import lax
from jax.sharding import PartitionSpec as P

HDIM = 72


EPSILON = 1e-06


def gelu_tanh(value):
    return jax.nn.gelu(value, approximate=True)


def fetch_weights(query_weight, key_weight, value_weight, up_weight, output_weight, down_weight):
    row_parts = (
        lax.all_gather(query_weight, "dp", axis=0, tiled=True),
        lax.all_gather(key_weight, "dp", axis=0, tiled=True),
        lax.all_gather(value_weight, "dp", axis=0, tiled=True),
        lax.all_gather(up_weight, "dp", axis=0, tiled=True),
    )
    col_parts = (
        lax.all_gather(output_weight, "dp", axis=1, tiled=True),
        lax.all_gather(down_weight, "dp", axis=1, tiled=True),
    )
    return tuple(row_parts) + tuple(col_parts)


def normalize(rows):
    centred = rows - jnp.mean(rows, axis=1, keepdims=True)
    inverse = lax.rsqrt(jnp.mean(centred * centred, axis=1, keepdims=True) + EPSILON)
    return (centred * inverse, inverse)


def norm_back(grad_share, normed_share, inverse, gain_share):
    scaled = grad_share * gain_share
    totals = lax.psum((jnp.sum(scaled, axis=1), jnp.sum(scaled * normed_share, axis=1)), "tensor")
    width = grad_share.shape[1] * lax.axis_size("tensor")
    first_mean = totals[0][:, None] / width
    second_mean = totals[1][:, None] / width
    return inverse * (scaled - first_mean - normed_share * second_mean)


def split_heads(rows):
    return rows.reshape(rows.shape[0], -1, HDIM).transpose(1, 0, 2)


def merge_heads(blocks):
    return blocks.transpose(1, 0, 2).reshape(blocks.shape[1], -1)


def column_share(whole, start, width):
    return lax.dynamic_slice_in_dim(whole, start, width, whole.ndim - 1)


def local(
    images,
    image_count,
    attn_gain,
    attn_shift,
    query_weight,
    query_bias,
    key_weight,
    value_weight,
    value_bias,
    output_weight,
    output_bias,
    mlp_gain,
    mlp_shift,
    up_weight,
    up_bias,
    down_weight,
    down_bias,
    cotangent,
):
    share_width = images.shape[2]
    share_start = lax.axis_index("tensor") * share_width
    attn_gain_share = column_share(attn_gain, share_start, share_width)
    mlp_gain_share = column_share(mlp_gain, share_start, share_width)
    score_scale = 1.0 / math.sqrt(HDIM)
    grads_sum = None
    out_slots = []
    grad_slots = []
    for slot_index in range(images.shape[0]):
        weights_now = fetch_weights(
            query_weight, key_weight, value_weight, up_weight, output_weight, down_weight
        )
        query_full, key_full, value_full, up_full, output_full, down_full = weights_now
        live_flag = (image_count[0] > slot_index).astype(jnp.float32)
        rows_pair = (
            lax.all_gather(images[slot_index], "tensor", axis=1, tiled=True),
            lax.all_gather(cotangent[slot_index], "tensor", axis=1, tiled=True),
        )
        input_full = rows_pair[0].astype(jnp.float32)
        grad_full = rows_pair[1].astype(jnp.float32) * live_flag
        grad_low = grad_full.astype(jnp.bfloat16)
        input_share = images[slot_index].astype(jnp.float32)
        grad_share = cotangent[slot_index].astype(jnp.float32) * live_flag
        normed1, inverse1 = normalize(input_full)
        attn_in = (normed1 * attn_gain + attn_shift).astype(jnp.bfloat16)
        query_low = (
            jnp.dot(attn_in, query_full, preferred_element_type=jnp.float32) + query_bias
        ).astype(jnp.bfloat16)
        key_low = jnp.dot(attn_in, key_full, preferred_element_type=jnp.float32).astype(
            jnp.bfloat16
        )
        value_low = (
            jnp.dot(attn_in, value_full, preferred_element_type=jnp.float32) + value_bias
        ).astype(jnp.bfloat16)
        query_heads = split_heads(query_low)
        key_heads = split_heads(key_low)
        value_heads = split_heads(value_low)
        scores = (
            jnp.einsum("hqd,hkd->hqk", query_heads, key_heads, preferred_element_type=jnp.float32)
            * score_scale
        )
        row_max = jnp.max(scores, axis=-1, keepdims=True)
        expo = jnp.exp(scores - row_max)
        prob_total = jnp.sum(expo, axis=-1, keepdims=True)
        log_total = row_max + jnp.log(prob_total)
        probs_low = (expo / prob_total).astype(jnp.bfloat16)
        mixed_heads = jnp.einsum(
            "hqk,hkd->hqd", probs_low, value_heads, preferred_element_type=jnp.float32
        )
        mixed_low = merge_heads(mixed_heads).astype(jnp.bfloat16)
        attn_partial = jnp.dot(mixed_low, output_full, preferred_element_type=jnp.float32)
        attn_share = lax.psum_scatter(attn_partial, "tensor", scatter_dimension=1, tiled=True)
        hidden1_share = input_share + attn_share + output_bias
        hidden1_full = lax.all_gather(hidden1_share, "tensor", axis=1, tiled=True)
        normed2, inverse2 = normalize(hidden1_full)
        mlp_in = (normed2 * mlp_gain + mlp_shift).astype(jnp.bfloat16)
        pre_act = jnp.dot(mlp_in, up_full, preferred_element_type=jnp.float32) + up_bias
        activ, gelu_pull = jax.vjp(gelu_tanh, pre_act)
        activ_low = activ.astype(jnp.bfloat16)
        mlp_partial = jnp.dot(activ_low, down_full, preferred_element_type=jnp.float32)
        mlp_share = lax.psum_scatter(
            mlp_partial.astype(jnp.bfloat16), "tensor", scatter_dimension=1, tiled=True
        ).astype(jnp.float32)
        out_slots.append(((hidden1_share + mlp_share + down_bias) * live_flag).astype(jnp.bfloat16))
        down_grad = jnp.einsum("sf,sd->fd", activ_low, grad_low, preferred_element_type=jnp.float32)
        hidden_grad = jnp.einsum(
            "sd,fd->sf", grad_low, down_full, preferred_element_type=jnp.float32
        )
        pre_grad = gelu_pull(hidden_grad)[0].astype(jnp.bfloat16)
        up_grad = jnp.einsum("sd,sf->df", mlp_in, pre_grad, preferred_element_type=jnp.float32)
        norm2_partial = jnp.einsum(
            "sf,df->sd", pre_grad, up_full, preferred_element_type=jnp.float32
        )
        normed2_share = column_share(normed2, share_start, share_width)
        norm2_share = lax.psum_scatter(norm2_partial, "tensor", scatter_dimension=1, tiled=True)
        hidden1_grad = grad_share + norm_back(norm2_share, normed2_share, inverse2, mlp_gain_share)
        branch_low = lax.all_gather(hidden1_grad.astype(jnp.bfloat16), "tensor", axis=1, tiled=True)
        output_grad = jnp.einsum(
            "sh,sd->hd", mixed_low, branch_low, preferred_element_type=jnp.float32
        )
        mixed_grad = split_heads(
            jnp.einsum(
                "sd,hd->sh", branch_low, output_full, preferred_element_type=jnp.float32
            ).astype(jnp.bfloat16)
        )
        scores_again = (
            jnp.einsum("hqd,hkd->hqk", query_heads, key_heads, preferred_element_type=jnp.float32)
            * score_scale
        )
        probs_again = jnp.exp(scores_again - log_total)
        probs_again_low = probs_again.astype(jnp.bfloat16)
        prob_grad = jnp.einsum(
            "hqd,hkd->hqk", mixed_grad, value_heads, preferred_element_type=jnp.float32
        )
        row_delta = jnp.sum(probs_again * prob_grad, axis=-1, keepdims=True)
        score_grad = (probs_again * (prob_grad - row_delta)).astype(jnp.bfloat16)
        query_grad = merge_heads(
            jnp.einsum("hqk,hkd->hqd", score_grad, key_heads, preferred_element_type=jnp.float32)
            * score_scale
        ).astype(jnp.bfloat16)
        key_grad = merge_heads(
            jnp.einsum("hqk,hqd->hkd", score_grad, query_heads, preferred_element_type=jnp.float32)
            * score_scale
        ).astype(jnp.bfloat16)
        value_grad = merge_heads(
            jnp.einsum(
                "hqk,hqd->hkd", probs_again_low, mixed_grad, preferred_element_type=jnp.float32
            )
        ).astype(jnp.bfloat16)
        query_w_grad = jnp.einsum(
            "sd,sh->dh", attn_in, query_grad, preferred_element_type=jnp.float32
        )
        key_w_grad = jnp.einsum("sd,sh->dh", attn_in, key_grad, preferred_element_type=jnp.float32)
        value_w_grad = jnp.einsum(
            "sd,sh->dh", attn_in, value_grad, preferred_element_type=jnp.float32
        )
        norm1_partial = jnp.einsum(
            "sh,dh->sd", query_grad, query_full, preferred_element_type=jnp.float32
        )
        norm1_partial = norm1_partial + jnp.einsum(
            "sh,dh->sd", key_grad, key_full, preferred_element_type=jnp.float32
        )
        norm1_partial = norm1_partial + jnp.einsum(
            "sh,dh->sd", value_grad, value_full, preferred_element_type=jnp.float32
        )
        norm1_share = lax.psum_scatter(
            norm1_partial.astype(jnp.bfloat16), "tensor", scatter_dimension=1, tiled=True
        ).astype(jnp.float32)
        normed1_share = column_share(normed1, share_start, share_width)
        grad_slots.append(
            (
                hidden1_grad + norm_back(norm1_share, normed1_share, inverse1, attn_gain_share)
            ).astype(jnp.bfloat16)
        )
        slot_grads = (
            query_w_grad,
            key_w_grad,
            value_w_grad,
            up_grad,
            output_grad,
            down_grad,
            jnp.sum(norm1_share * normed1_share, axis=0),
            jnp.sum(norm1_share, axis=0),
            jnp.sum(query_grad.astype(jnp.float32), axis=0),
            jnp.sum(value_grad.astype(jnp.float32), axis=0),
            jnp.sum(hidden1_grad, axis=0),
            jnp.sum(norm2_share * normed2_share, axis=0),
            jnp.sum(norm2_share, axis=0),
            jnp.sum(pre_grad.astype(jnp.float32), axis=0),
            jnp.sum(grad_share, axis=0),
        )
        grads_sum = (
            slot_grads if grads_sum is None else jax.tree.map(jnp.add, grads_sum, slot_grads)
        )
    row_grads = (
        lax.psum_scatter(grads_sum[0], "dp", scatter_dimension=0, tiled=True),
        lax.psum_scatter(grads_sum[1], "dp", scatter_dimension=0, tiled=True),
        lax.psum_scatter(grads_sum[2], "dp", scatter_dimension=0, tiled=True),
        lax.psum_scatter(grads_sum[3], "dp", scatter_dimension=0, tiled=True),
    )
    col_grads = (
        lax.psum_scatter(grads_sum[4], "dp", scatter_dimension=1, tiled=True),
        lax.psum_scatter(grads_sum[5], "dp", scatter_dimension=1, tiled=True),
    )
    small = lax.psum(
        (
            grads_sum[6],
            grads_sum[7],
            grads_sum[8],
            grads_sum[9],
            grads_sum[10],
            grads_sum[11],
            grads_sum[12],
            grads_sum[13],
            grads_sum[14],
        ),
        "dp",
    )
    return (
        jnp.stack(out_slots),
        jnp.stack(grad_slots),
        small[0],
        small[1],
        row_grads[0],
        small[2],
        row_grads[1],
        row_grads[2],
        small[3],
        col_grads[0],
        small[4],
        small[5],
        small[6],
        row_grads[3],
        small[7],
        col_grads[1],
        small[8],
    )


def solution(mesh):
    in_specs = (
        P("dp", None, "tensor"),
        P("dp"),
        P(),
        P(),
        P("dp", "tensor"),
        P("tensor"),
        P("dp", "tensor"),
        P("dp", "tensor"),
        P("tensor"),
        P("tensor", "dp"),
        P("tensor"),
        P(),
        P(),
        P("dp", "tensor"),
        P("tensor"),
        P("tensor", "dp"),
        P("tensor"),
        P("dp", None, "tensor"),
    )
    out_specs = (
        P("dp", None, "tensor"),
        P("dp", None, "tensor"),
        P("tensor"),
        P("tensor"),
        P("dp", "tensor"),
        P("tensor"),
        P("dp", "tensor"),
        P("dp", "tensor"),
        P("tensor"),
        P("tensor", "dp"),
        P("tensor"),
        P("tensor"),
        P("tensor"),
        P("dp", "tensor"),
        P("tensor"),
        P("tensor", "dp"),
        P("tensor"),
    )
    return jax.shard_map(local, mesh=mesh, in_specs=in_specs, out_specs=out_specs, check_vma=False)
```

profile of v0, /device:TPU:8, one launch (start us, length us, event | category | flops | bytes accessed | tf_op | source)
XLA Modules:
  0.0 1478.9 jit_solution(229131202090913659)
XLA Ops:
  11.3 30.3 %all_gather.67 = bf16[1152,288]{1,0:T(8,128)(2,1)S(1)} all-gather(bf16[144,288]{1,0:T(8,128)(2,1)S(1)} %copy-done.91), channel_id=1, replica_groups=mesh['dp'=8,'tensor'=4] {'dp'}, dimensions={0}, use_global_device_ids=true | all-gather | bytes 746496 | tf_op jit(solution)/shard_map/all_gather | solution.py:20
  41.6 32.5 %all_gather.68 = bf16[1152,288]{1,0:T(8,128)(2,1)S(1)} all-gather(bf16[144,288]{1,0:T(8,128)(2,1)S(1)} %copy-done.92), channel_id=1, replica_groups=mesh['dp'=8,'tensor'=4] {'dp'}, dimensions={0}, use_global_device_ids=true | all-gather | bytes 746496 | tf_op jit(solution)/shard_map/all_gather | solution.py:21
  74.1 32.6 %all_gather.69 = bf16[1152,288]{1,0:T(8,128)(2,1)S(1)} all-gather(bf16[144,288]{1,0:T(8,128)(2,1)S(1)} %copy-done.93), channel_id=1, replica_groups=mesh['dp'=8,'tensor'=4] {'dp'}, dimensions={0}, use_global_device_ids=true | all-gather | bytes 746496 | tf_op jit(solution)/shard_map/all_gather | solution.py:22
  106.7 32.0 %all_gather.70 = bf16[288,1152]{0,1:T(8,128)(2,1)S(1)} all-gather(bf16[288,144]{0,1:T(8,128)(2,1)} %param.27), channel_id=1, replica_groups=mesh['dp'=8,'tensor'=4] {'dp'}, dimensions={1}, use_global_device_ids=true | all-gather | bytes 746496 | tf_op jit(solution)/shard_map/all_gather | solution.py:26
  155.2 2.9 fusion.152
  175.9 2.8 fusion.153
  195.9 2.9 fusion.151
  198.9 3.8 reduce-scatter.23.cloned.1.call-done
  202.7 43.1 %reduce-scatter.27.cloned.1.call-done = f32[729,288]{0,1:T(8,128)} async-done(((f32[729,1152]{0,1:T(8,128)}), f32[729,288]{0,1:T(8,128)}) %reduce-scatter.27.cloned.1.call-update) | async-done | bytes 839824 | tf_op jit(solution)/shard_map/reduce_scatter | solution.py:130
  245.8 42.9 %reduce-scatter.19.cloned.1.call-done = f32[729,288]{0,1:T(8,128)} async-done(((f32[729,1152]{0,1:T(8,128)}), f32[729,288]{0,1:T(8,128)}) %reduce-scatter.19.cloned.1.call-update) | async-done | bytes 839824 | tf_op jit(solution)/shard_map/reduce_scatter | solution.py:130
  288.7 3.6 fusion.129
  298.5 24.7 %all-gather.29.cloned.1.call-done = f32[729,1152]{0,1:T(8,128)} async-done(((f32[729,288]{0,1:T(8,128)}), f32[729,1152]{0,1:T(8,128)}) %all-gather.29.cloned.1.call-update) | async-done | bytes 3359248 | tf_op jit(solution)/shard_map/all_gather | solution.py:132
  328.8 51.8 %all-gather.23.cloned.1.call-done = bf16[1152,1076]{1,0:T(8,128)(2,1)} async-done(((bf16[144,1076]{1,0:T(8,128)(2,1)}), bf16[1152,1076]{1,0:T(8,128)(2,1)}) %all-gather.23.cloned.1.call-update) | async-done | bytes 2479120 | tf_op jit(solution)/shard_map/all_gather | solution.py:23
  380.6 5.4 convolution_add_fusion.10
  386.1 16.2 %all-gather.47.cloned.1.call-done = bf16[1,729,1152]{1,2,0:T(8,128)(2,1)} async-done(((bf16[1,729,288]{1,2,0:T(8,128)(2,1)}), bf16[1,729,1152]{1,2,0:T(8,128)(2,1)}) %all-gather.47.cloned.1.call-update) | async-done | bytes 1679632 | tf_op jit(solution)/shard_map/all_gather | solution.py:95
  402.2 57.3 %all-gather.25.cloned.1.call-done = bf16[1076,1152]{0,1:T(8,128)(2,1)} async-done(((bf16[1076,144]{0,1:T(8,128)(2,1)}), bf16[1076,1152]{0,1:T(8,128)(2,1)}) %all-gather.25.cloned.1.call-update) | async-done | bytes 2479120 | tf_op jit(solution)/shard_map/all_gather | solution.py:27
  459.5 7.4 convert_reduce_fusion.3
  468.2 4.3 fusion.158
  472.7 18.4 %all-gather.27.cloned.1.call-done = f32[729,1152]{0,1:T(8,128)} async-done(((f32[729,288]{0,1:T(8,128)}), f32[729,1152]{0,1:T(8,128)}) %all-gather.27.cloned.1.call-update) | async-done | bytes 3359248 | tf_op jit(solution)/shard_map/all_gather | solution.py:132
  497.6 4.3 convolution_add_fusion.11
  501.8 11.6 all-gather.45.cloned.1.call-done
  513.4 7.6 convert_reduce_fusion.4
  522.3 4.4 fusion.156
  527.0 19.5 %all-gather.21.cloned.1.call-done = f32[729,1152]{0,1:T(8,128)} async-done(((f32[729,288]{0,1:T(8,128)}), f32[729,1152]{0,1:T(8,128)}) %all-gather.21.cloned.1.call-update) | async-done | bytes 3359248 | tf_op jit(solution)/shard_map/all_gather | solution.py:132
  552.9 4.4 convolution_add_fusion.12
  557.3 12.0 all-gather.43.cloned.1.call-done
  569.3 7.6 convert_reduce_fusion.5
  578.1 4.4 fusion.154
  583.5 28.9 %reduce-scatter.39.cloned.1.call-done = f32[729,288]{0,1:T(8,128)} async-done(((f32[729,1152]{0,1:T(8,128)}), f32[729,288]{0,1:T(8,128)}) %reduce-scatter.39.cloned.1.call-update) | async-done | bytes 839824 | tf_op jit(solution)/shard_map/reduce_scatter | solution.py:153
  612.3 42.9 %reduce-scatter.35.cloned.1.call-done = f32[729,288]{0,1:T(8,128)} async-done(((f32[729,1152]{0,1:T(8,128)}), f32[729,288]{0,1:T(8,128)}) %reduce-scatter.35.cloned.1.call-update) | async-done | bytes 839824 | tf_op jit(solution)/shard_map/reduce_scatter | solution.py:153
  655.2 43.0 %reduce-scatter.31.cloned.1.call-done = f32[729,288]{0,1:T(8,128)} async-done(((f32[729,1152]{0,1:T(8,128)}), f32[729,288]{0,1:T(8,128)}) %reduce-scatter.31.cloned.1.call-update) | async-done | bytes 839824 | tf_op jit(solution)/shard_map/reduce_scatter | solution.py:153
  698.3 4.0 multiply_reduce_fusion.11
  702.3 10.9 all-reduce.2
  713.2 3.0 fusion.147
  722.9 6.7 convolution_convert_fusion.2
  729.7 6.6 convolution_convert_fusion.1
  737.1 6.7 convolution_convert_fusion
  746.5 7.4 multiply_reduce_fusion.2
  753.9 10.2 multiply_convert_fusion.2
  764.1 4.0 convert_reduce_fusion.14
  781.2 7.7 multiply_reduce_fusion
  788.9 10.6 multiply_convert_fusion
  799.5 4.1 convert_reduce_fusion.12
  816.5 7.0 multiply_reduce_fusion.1
  823.6 11.1 multiply_convert_fusion.1
  834.6 4.2 convert_reduce_fusion.13
  848.8 4.8 fusion.70
  853.7 2.8 convolution_add_fusion.1
  856.5 5.1 convolution_add_fusion
  862.3 5.4 fusion.145
  867.8 2.9 convolution_add_fusion.3
  870.7 5.3 convolution_add_fusion.2
  910.9 2.7 fusion.161
  917.1 28.1 %reduce-scatter.41.cloned.1.call-done = bf16[729,288]{0,1:T(8,128)(2,1)} async-done(((bf16[729,1152]{0,1:T(8,128)(2,1)}), bf16[729,288]{0,1:T(8,128)(2,1)}) %reduce-scatter.41.cloned.1.call-update) | async-done | bytes 419920 | tf_op jit(solution)/shard_map/reduce_scatter | solution.py:204
  945.2 32.0 %reduce-scatter.37.cloned.1.call-done = bf16[729,288]{0,1:T(8,128)(2,1)} async-done(((bf16[729,1152]{0,1:T(8,128)(2,1)}), bf16[729,288]{0,1:T(8,128)(2,1)}) %reduce-scatter.37.cloned.1.call-update) | async-done | bytes 419920 | tf_op jit(solution)/shard_map/reduce_scatter | solution.py:204
  977.3 3.7 fusion.124
  982.2 37.6 %all-reduce = (f32[288]{0:T(512)}, f32[288]{0:T(512)}, f32[288]{0:T(512)}, f32[288]{0:T(512)}, f32[288]{0:T(512)}, /*index=5*/f32[288]{0:T(512)}, f32[288]{0:T(512)}, f32[1076]{0:T(1024)}, f32[288]{0:T(512)}) all-reduce(f32[288]{0:T(512)} %add_add_fusion.8, f32[288]{0:T(512)} %add_add_fusion.7, ...), channel_id=1, replica_groups=mesh['dp'=8,'tensor'=4] {'dp'}, use_global_device_ids=true, to_apply=%region_60.0 | all-reduce | flops 3380 | bytes 27040 | tf_op jit(solution)/shard_map/psum | solution.py:243
  1019.8 12.2 all-reduce.1
  1040.9 45.0 %reduce-scatter.53.cloned.1.call-done = f32[1076,144]{0,1:T(8,128)} async-done(((f32[1076,1152]{0,1:T(8,128)}), f32[1076,144]{0,1:T(8,128)}) %reduce-scatter.53.cloned.1.call-update) | async-done | bytes 619792 | tf_op jit(solution)/shard_map/reduce_scatter | solution.py:241
  1085.9 108.5 %reduce-scatter.51.cloned.1.call-done = f32[144,1076]{1,0:T(8,128)} async-done(((f32[1152,1076]{1,0:T(8,128)}), f32[144,1076]{1,0:T(8,128)}) %reduce-scatter.51.cloned.1.call-update) | async-done | bytes 619792 | tf_op jit(solution)/shard_map/reduce_scatter | solution.py:237
  1194.4 69.4 %reduce-scatter.49.cloned.1.call-done = f32[288,144]{0,1:T(8,128)} async-done(((f32[288,1152]{0,1:T(8,128)}), f32[288,144]{0,1:T(8,128)}) %reduce-scatter.49.cloned.1.call-update) | async-done | bytes 165904 | tf_op jit(solution)/shard_map/reduce_scatter | solution.py:240
  1263.8 69.5 %reduce-scatter.47.cloned.1.call-done = f32[144,288]{1,0:T(8,128)} async-done(((f32[1152,288]{1,0:T(8,128)}), f32[144,288]{1,0:T(8,128)}) %reduce-scatter.47.cloned.1.call-update) | async-done | bytes 165904 | tf_op jit(solution)/shard_map/reduce_scatter | solution.py:236
  1333.3 69.2 %reduce-scatter.43.cloned.1.call-done = f32[144,288]{1,0:T(8,128)} async-done(((f32[1152,288]{1,0:T(8,128)}), f32[144,288]{1,0:T(8,128)}) %reduce-scatter.43.cloned.1.call-update) | async-done | bytes 165904 | tf_op jit(solution)/shard_map/reduce_scatter | solution.py:234
  1402.5 69.4 %reduce-scatter.45.cloned.1.call-done = f32[144,288]{1,0:T(8,128)} async-done(((f32[1152,288]{1,0:T(8,128)}), f32[144,288]{1,0:T(8,128)}) %reduce-scatter.45.cloned.1.call-update) | async-done | bytes 165904 | tf_op jit(solution)/shard_map/reduce_scatter | solution.py:235
  (510 shorter events, 178.3 us)
Async XLA Ops:
  7.2 34.3 %copy-start.92 = (bf16[144,288]{1,0:T(8,128)(2,1)S(1)}, bf16[144,288]{1,0:T(8,128)(2,1)}, u32[]{:S(2)}) copy-start(bf16[144,288]{1,0:T(8,128)(2,1)} %param.24) | copy-start | bytes 248836
  7.2 66.9 %copy-start.93 = (bf16[144,288]{1,0:T(8,128)(2,1)S(1)}, bf16[144,288]{1,0:T(8,128)(2,1)}, u32[]{:S(2)}) copy-start(bf16[144,288]{1,0:T(8,128)(2,1)} %param.25) | copy-start | bytes 248836
  7.2 131.5 %all-gather.39.cloned.1.call-start = ((), (), s32[]{:S(2)}) async-start(), calls=%async_computation.45 | async-start | bytes 2211840 | tf_op jit(solution)/shard_map/all_gather | solution.py:94
  9.7 148.7 %all-gather.41.cloned.1.call-start = ((), (), s32[]{:S(2)}) async-start(), calls=%async_computation.46 | async-start | bytes 2211840 | tf_op jit(solution)/shard_map/all_gather | solution.py:94
  10.5 168.5 %all-gather.37.cloned.1.call-start = ((), (), s32[]{:S(2)}) async-start(), calls=%async_computation.44 | async-start | bytes 2211840 | tf_op jit(solution)/shard_map/all_gather | solution.py:94
  11.2 191.5 %reduce-scatter.23.cloned.1.call-start = ((), (), s32[]{:S(2)}) async-start(), calls=%async_computation.23 | async-start | bytes 4423680 | tf_op jit(solution)/shard_map/reduce_scatter | solution.py:130
  41.5 145.6 %copy-start.15 = (bf16[1152,288]{1,0:T(8,128)(2,1)}, bf16[1152,288]{1,0:T(8,128)(2,1)S(1)}, u32[]{:S(2)}) copy-start(bf16[1152,288]{1,0:T(8,128)(2,1)S(1)} %all_gather.67) | copy-start | bytes 1990660
  41.5 101.4 %copy-start.100 = (f32[1152]{0:T(1024)S(1)}, f32[1152]{0:T(1024)}, u32[]{:S(2)}) copy-start(f32[1152]{0:T(1024)} %param.20) | copy-start | bytes 13828
  41.5 101.4 %copy-start.101 = (f32[1152]{0:T(1024)S(1)}, f32[1152]{0:T(1024)}, u32[]{:S(2)}) copy-start(f32[1152]{0:T(1024)} %param.21) | copy-start | bytes 13828
  74.1 111.4 %copy-start.19 = (bf16[1152,288]{1,0:T(8,128)(2,1)}, bf16[1152,288]{1,0:T(8,128)(2,1)S(1)}, u32[]{:S(2)}) copy-start(bf16[1152,288]{1,0:T(8,128)(2,1)S(1)} %all_gather.68) | copy-start | bytes 1990660
  106.7 79.6 %copy-start.13 = (bf16[1152,288]{1,0:T(8,128)(2,1)}, bf16[1152,288]{1,0:T(8,128)(2,1)S(1)}, u32[]{:S(2)}) copy-start(bf16[1152,288]{1,0:T(8,128)(2,1)S(1)} %all_gather.69) | copy-start | bytes 1990660
  138.7 56.4 %copy-start.17 = (bf16[288,1152]{0,1:T(8,128)(2,1)}, bf16[288,1152]{0,1:T(8,128)(2,1)S(1)}, u32[]{:S(2)}) copy-start(bf16[288,1152]{0,1:T(8,128)(2,1)S(1)} %all_gather.70) | copy-start | bytes 1990660
  158.2 87.6 %reduce-scatter.27.cloned.1.call-start = ((), (), s32[]{:S(2)}) async-start(), calls=%async_computation.26 | async-start | bytes 4423680 | tf_op jit(solution)/shard_map/reduce_scatter | solution.py:130
  178.7 110.0 %reduce-scatter.19.cloned.1.call-start = ((), (), s32[]{:S(2)}) async-start(), calls=%async_computation.18 | async-start | bytes 4423680 | tf_op jit(solution)/shard_map/reduce_scatter | solution.py:130
  198.8 89.8 %copy-start.33 = (bf16[3,729,288]{1,2,0:T(8,128)(2,1)S(1)}, bf16[3,729,288]{1,2,0:T(8,128)(2,1)}, u32[]{:S(2)}) copy-start(bf16[3,729,288]{1,2,0:T(8,128)(2,1)} %param.18) | copy-start | bytes 3779140
  198.8 89.8 %copy-start.118 = (f32[288]{0:T(512)S(1)}, f32[288]{0:T(512)}, u32[]{:S(2)}) copy-start(f32[288]{0:T(512)} %param.28) | copy-start | bytes 3460
  198.9 94.2 %copy-start.21 = (bf16[3,729,288]{1,2,0:T(8,128)(2,1)S(1)}, bf16[3,729,288]{1,2,0:T(8,128)(2,1)}, u32[]{:S(2)}) copy-start(bf16[3,729,288]{1,2,0:T(8,128)(2,1)} %param.35) | copy-start | bytes 3779140
  198.9 124.3 %all-gather.29.cloned.1.call-start = ((), (), s32[]{:S(2)}) async-start(), calls=%async_computation.27 | async-start | bytes 4423680 | tf_op jit(solution)/shard_map/all_gather | solution.py:132
  292.3 88.4 %all-gather.23.cloned.1.call-start = ((), (), s32[]{:S(2)}) async-start(), calls=%async_computation.20 | async-start | bytes 2985984 | tf_op jit(solution)/shard_map/all_gather | solution.py:23
  293.0 109.2 %all-gather.47.cloned.1.call-start = ((), (), s32[]{:S(2)}) async-start(), calls=%async_computation.49 | async-start | bytes 2211840 | tf_op jit(solution)/shard_map/all_gather | solution.py:95
  294.2 165.4 %all-gather.25.cloned.1.call-start = ((), (), s32[]{:S(2)}) async-start(), calls=%async_computation.21 | async-start | bytes 2985984 | tf_op jit(solution)/shard_map/all_gather | solution.py:27
  294.8 196.4 %all-gather.27.cloned.1.call-start = ((), (), s32[]{:S(2)}) async-start(), calls=%async_computation.24 | async-start | bytes 4423680 | tf_op jit(solution)/shard_map/all_gather | solution.py:132
  295.5 217.9 %all-gather.45.cloned.1.call-start = ((), (), s32[]{:S(2)}) async-start(), calls=%async_computation.48 | async-start | bytes 2211840 | tf_op jit(solution)/shard_map/all_gather | solution.py:95
  296.1 250.4 %all-gather.21.cloned.1.call-start = ((), (), s32[]{:S(2)}) async-start(), calls=%async_computation.19 | async-start | bytes 4423680 | tf_op jit(solution)/shard_map/all_gather | solution.py:132
  296.8 272.5 %all-gather.43.cloned.1.call-start = ((), (), s32[]{:S(2)}) async-start(), calls=%async_computation.47 | async-start | bytes 2211840 | tf_op jit(solution)/shard_map/all_gather | solution.py:95
  297.4 314.9 %reduce-scatter.39.cloned.1.call-start = ((), (), s32[]{:S(2)}) async-start(), calls=%async_computation.35 | async-start | bytes 4423680 | tf_op jit(solution)/shard_map/reduce_scatter | solution.py:153
  326.7 53.9 %copy-start.119 = (f32[1152]{0:T(1024)S(1)}, f32[1152]{0:T(1024)}, u32[]{:S(2)}) copy-start(f32[1152]{0:T(1024)} %param.29) | copy-start | bytes 13828
  386.0 80.9 %copy-start.147 = (f32[729,1076]{0,1:T(8,128)}, f32[729,1076]{0,1:T(8,128)S(1)}, u32[]{:S(2)}) copy-start(f32[729,1076]{0,1:T(8,128)S(1)} %convolution_add_fusion.10) | copy-start | bytes 9412852
  459.5 8.7 copy-start.124
  472.5 182.7 %reduce-scatter.35.cloned.1.call-start = ((), (), s32[]{:S(2)}) async-start(), calls=%async_computation.32 | async-start | bytes 4423680 | tf_op jit(solution)/shard_map/reduce_scatter | solution.py:153
  497.6 15.9 %copy-start.122 = (bf16[1076,1152]{0,1:T(8,128)(2,1)S(1)}, bf16[1076,1152]{0,1:T(8,128)(2,1)}, u32[]{:S(2)}) copy-start(bf16[1076,1152]{0,1:T(8,128)(2,1)} %all-gather.25.cloned.1.call-done) | copy-start | bytes 7437316
  513.4 8.9 copy-start.126
  526.7 171.6 %reduce-scatter.31.cloned.1.call-start = ((), (), s32[]{:S(2)}) async-start(), calls=%async_computation.29 | async-start | bytes 4423680 | tf_op jit(solution)/shard_map/reduce_scatter | solution.py:153
  552.9 16.4 %copy-start.123 = (bf16[1076,1152]{0,1:T(8,128)(2,1)S(1)}, bf16[1076,1152]{0,1:T(8,128)(2,1)}, u32[]{:S(2)}) copy-start(bf16[1076,1152]{0,1:T(8,128)(2,1)} %all-gather.25.cloned.1.call-done) | copy-start | bytes 7437316
  569.3 8.8 copy-start.128
  582.5 130.7 %copy-start.22 = (bf16[3,729,288]{1,2,0:T(8,128)(2,1)S(1)}, bf16[3,729,288]{1,2,0:T(8,128)(2,1)}, u32[]{:S(2)}) copy-start(bf16[3,729,288]{1,2,0:T(8,128)(2,1)} %param.35) | copy-start | bytes 3779140
  582.5 161.6 %all-gather.31.cloned.1.call-start = ((), (), s32[]{:S(2)}) async-start(), calls=%async_computation.30 | async-start | bytes 2211840 | tf_op jit(solution)/shard_map/all_gather | solution.py:155
  612.3 100.9 %copy-start.45 = (f32[729,288]{0,1:T(8,128)S(1)}, f32[729,288]{0,1:T(8,128)}, u32[]{:S(2)}) copy-start(f32[729,288]{0,1:T(8,128)} %reduce-scatter.39.cloned.1.call-done) | copy-start | bytes 2519428
  717.9 60.8 %all-gather.35.cloned.1.call-start = ((), (), s32[]{:S(2)}) async-start(), calls=%async_computation.36 | async-start | bytes 2211840 | tf_op jit(solution)/shard_map/all_gather | solution.py:155
  718.8 95.3 %all-gather.33.cloned.1.call-start = ((), (), s32[]{:S(2)}) async-start(), calls=%async_computation.33 | async-start | bytes 2211840 | tf_op jit(solution)/shard_map/all_gather | solution.py:155
  722.8 178.9 %reduce-scatter.21.cloned.1.call-start = ((), (), s32[]{:S(2)}) async-start(), calls=%async_computation.22 | async-start | bytes 2211840 | tf_op jit(solution)/shard_map/reduce_scatter | solution.py:139
  729.7 7.5 copy-start.99
  729.7 172.1 %reduce-scatter.25.cloned.1.call-start = ((), (), s32[]{:S(2)}) async-start(), calls=%async_computation.25 | async-start | bytes 2211840 | tf_op jit(solution)/shard_map/reduce_scatter | solution.py:139
  736.4 165.4 %reduce-scatter.29.cloned.1.call-start = ((), (), s32[]{:S(2)}) async-start(), calls=%async_computation.28 | async-start | bytes 2211840 | tf_op jit(solution)/shard_map/reduce_scatter | solution.py:139
  737.1 16.7 %copy-start.89 = (f32[4,729]{1,0:T(4,128)}, f32[4,729]{1,0:T(4,128)S(1)}, u32[]{:S(2)}) copy-start(f32[4,729]{1,0:T(4,128)S(1)} %log_add_fusion.2) | copy-start | bytes 34996
  743.9 173.2 %reduce-scatter.33.cloned.1.call-start = ((), (), s32[]{:S(2)}) async-start(), calls=%async_computation.31 | async-start | bytes 2211840 | tf_op jit(solution)/shard_map/reduce_scatter | solution.py:204
  753.9 10.2 copy-start.86
  778.5 166.7 %reduce-scatter.41.cloned.1.call-start = ((), (), s32[]{:S(2)}) async-start(), calls=%async_computation.37 | async-start | bytes 2211840 | tf_op jit(solution)/shard_map/reduce_scatter | solution.py:204
  781.1 7.7 copy-start.54
  813.7 163.6 %reduce-scatter.37.cloned.1.call-start = ((), (), s32[]{:S(2)}) async-start(), calls=%async_computation.34 | async-start | bytes 2211840 | tf_op jit(solution)/shard_map/reduce_scatter | solution.py:204
  848.6 237.3 %reduce-scatter.53.cloned.1.call-start = ((), (), s32[]{:S(2)}) async-start(), calls=%async_computation.43 | async-start | bytes 5971968 | tf_op jit(solution)/shard_map/reduce_scatter | solution.py:241
  861.6 332.7 %reduce-scatter.51.cloned.1.call-start = ((), (), s32[]{:S(2)}) async-start(), calls=%async_computation.42 | async-start | bytes 5971968 | tf_op jit(solution)/shard_map/reduce_scatter | solution.py:237
  876.0 387.8 %reduce-scatter.49.cloned.1.call-start = ((), (), s32[]{:S(2)}) async-start(), calls=%async_computation.41 | async-start | bytes 1990656 | tf_op jit(solution)/shard_map/reduce_scatter | solution.py:240
  883.5 449.8 %reduce-scatter.47.cloned.1.call-start = ((), (), s32[]{:S(2)}) async-start(), calls=%async_computation.40 | async-start | bytes 1990656 | tf_op jit(solution)/shard_map/reduce_scatter | solution.py:236
  890.8 511.7 %reduce-scatter.43.cloned.1.call-start = ((), (), s32[]{:S(2)}) async-start(), calls=%async_computation.38 | async-start | bytes 1990656 | tf_op jit(solution)/shard_map/reduce_scatter | solution.py:234
  900.4 571.6 %reduce-scatter.45.cloned.1.call-start = ((), (), s32[]{:S(2)}) async-start(), calls=%async_computation.39 | async-start | bytes 1990656 | tf_op jit(solution)/shard_map/reduce_scatter | solution.py:235
  917.1 119.0 %copy-start.30 = (f32[729,288]{0,1:T(8,128)S(1)}, f32[729,288]{0,1:T(8,128)}, u32[]{:S(2)}) copy-start(f32[729,288]{0,1:T(8,128)} %copy-done.29) | copy-start | bytes 2519428
  917.1 119.0 %copy-start.111 = (f32[729]{0:T(1024)S(1)}, f32[729]{0:T(1024)}, u32[]{:S(2)}) copy-start(f32[729]{0:T(1024)} %copy-done.110) | copy-start | bytes 8752
  977.3 60.3 %copy-start.24 = (f32[729,288]{0,1:T(8,128)S(1)}, f32[729,288]{0,1:T(8,128)}, u32[]{:S(2)}) copy-start(f32[729,288]{0,1:T(8,128)} %copy-done.23) | copy-start | bytes 2519428
  977.3 60.4 %copy-start.28 = (f32[729,288]{0,1:T(8,128)S(1)}, f32[729,288]{0,1:T(8,128)}, u32[]{:S(2)}) copy-start(f32[729,288]{0,1:T(8,128)} %copy-done.27) | copy-start | bytes 2519428
  977.3 60.4 %copy-start.56 = (bf16[729,288]{0,1:T(8,128)(2,1)S(1)}, bf16[729,288]{0,1:T(8,128)(2,1)}, u32[]{:S(2)}) copy-start(bf16[729,288]{0,1:T(8,128)(2,1)} %reduce-scatter.33.cloned.1.call-done) | copy-start | bytes 1259716
  977.3 60.4 %copy-start.57 = (bf16[729,288]{0,1:T(8,128)(2,1)S(1)}, bf16[729,288]{0,1:T(8,128)(2,1)}, u32[]{:S(2)}) copy-start(bf16[729,288]{0,1:T(8,128)(2,1)} %reduce-scatter.37.cloned.1.call-done) | copy-start | bytes 1259716
  977.3 60.4 %copy-start.109 = (f32[729]{0:T(1024)S(1)}, f32[729]{0:T(1024)}, u32[]{:S(2)}) copy-start(f32[729]{0:T(1024)} %copy-done.108) | copy-start | bytes 8752
  977.3 60.4 %copy-start.113 = (f32[729]{0:T(1024)S(1)}, f32[729]{0:T(1024)}, u32[]{:S(2)}) copy-start(f32[729]{0:T(1024)} %copy-done.112) | copy-start | bytes 8752
  (128 other events, 376.2 us)
Sparse Core Ops, SparseCore 0:
  10.2 21.9 all-gather.38
  34.3 20.7 all-gather.40
  57.2 20.7 all-gather.36
  158.3 44.3 reduce-scatter.22
  205.3 40.4 reduce-scatter.26
  248.2 40.4 reduce-scatter.18
  292.4 30.7 all-gather.28
  325.6 55.0 all-gather.22
  382.9 19.3 all-gather.46
  404.5 55.0 all-gather.24
  461.8 29.3 all-gather.26
  492.6 20.7 all-gather.44
  515.6 30.7 all-gather.20
  548.5 20.7 all-gather.42
  571.9 40.4 reduce-scatter.38
  614.8 40.4 reduce-scatter.34
  657.8 40.4 reduce-scatter.30
  718.1 21.6 all-gather.30
  741.9 20.7 all-gather.34
  764.1 20.7 all-gather.32
  787.5 29.4 reduce-scatter.20
  819.7 29.3 reduce-scatter.24
  851.7 29.3 reduce-scatter.28
  883.8 29.4 reduce-scatter.32
  915.8 29.3 reduce-scatter.40
  947.8 29.3 reduce-scatter.36
  981.3 104.5 reduce-scatter.52
  1090.5 103.8 reduce-scatter.50
  1198.4 65.3 reduce-scatter.48
  1268.1 65.1 reduce-scatter.46
  1337.4 65.1 reduce-scatter.42
  1407.0 64.9 reduce-scatter.44
where the time goes:
time: 1490 us; the launch traced here: 1480 us
  waiting for transfers between devices  913 us (61%)
  matrix products  214 us (14%)
  blocking collectives  188 us (13%)
  other arithmetic  108 us (7%)
  local copies, waits for them, and re-layouts  34.8 us (2%)
  between operations  17.2 us (1%)
    reduce_scatter x3, waiting for transfers between devices, local(): lax.psum_scatter(norm2_partial, 'tensor', scatter_dimension=1, tiled=True)  115 us
    reduce_scatter x1, waiting for transfers between devices, local(): lax.psum_scatter(grads_sum[3], 'dp', scatter_dimension=0, tiled=True)  109 us
    reduce_scatter x3, waiting for transfers between devices, local(): lax.psum_scatter(attn_partial, 'tensor', scatter_dimension=1, tiled=True)  89.8 us
    reduce_scatter x1, waiting for transfers between devices, local(): lax.psum_scatter(grads_sum[2], 'dp', scatter_dimension=0, tiled=True)  69.5 us
    reduce_scatter x1, waiting for transfers between devices, local(): lax.psum_scatter(grads_sum[4], 'dp', scatter_dimension=1, tiled=True)  69.4 us
    reduce_scatter x1, waiting for transfers between devices, local(): lax.psum_scatter(grads_sum[1], 'dp', scatter_dimension=0, tiled=True)  69.4 us
    reduce_scatter x1, waiting for transfers between devices, local(): lax.psum_scatter(grads_sum[0], 'dp', scatter_dimension=0, tiled=True)  69.2 us
    all_gather x3, waiting for transfers between devices, local(): hidden1_full = lax.all_gather(hidden1_share, 'tensor', axis=1, tiled=True)  62.6 us
  transfers between devices with their start and end apart: 32, of which 22 were waited for; matrix products, arithmetic and copies ran while one was open for 21% of the time, Pallas kernels for 0%

commit v1 on v0

v1 whole, which is shorter than its diff:
```python
import functools
import math

import jax
import jax.numpy as jnp
from jax import lax
from jax.experimental import pallas as pl
from jax.experimental.pallas import tpu as pltpu
from jax.sharding import PartitionSpec as P

HDIM = 72
EPSILON = 1e-06
LOG2E = 1.4426950408889634
MASKED = -1e30
GELU_A = math.sqrt(2.0 / math.pi)
GELU_B = 0.044715
TILE = 256
VMEM_LIMIT = 56 * 2**20
F32 = jnp.float32
LOW = jnp.bfloat16
Y_SWAP = [(0, 2), (2, 0), (1, 3), (3, 1)]
CORE_SWAP = [(0, 1), (1, 0), (2, 3), (3, 2)]


def y_swap(value):
    return lax.ppermute(value, "tensor", Y_SWAP)


def core_swap(value):
    return lax.ppermute(value, "tensor", CORE_SWAP)


def dot_nn(a, b):
    return lax.dot_general(a, b, (((1,), (0,)), ((), ())), preferred_element_type=F32)


def dot_nt(a, b):
    return lax.dot_general(a, b, (((1,), (1,)), ((), ())), preferred_element_type=F32)


def dot_tn(a, b):
    return lax.dot_general(a, b, (((0,), (0,)), ((), ())), preferred_element_type=F32)


def rel_blocks(value, t):
    width = value.shape[0] // 4
    return jnp.concatenate(
        [lax.dynamic_slice_in_dim(value, (t ^ m) * width, width, 0) for m in (0, 2, 1, 3)], axis=0
    )


def rows4(a, b, c, d):
    return jnp.concatenate([a, b, c, d], axis=0)


def lanes(count):
    return [slice(at, at + TILE) for at in range(0, count, TILE)]


def column(sums):
    pad = jnp.zeros((sums[0].shape[0], 8 - len(sums)), F32)
    return jnp.concatenate([*sums, pad], axis=1)


def prepare_kernel(x, bias, out):
    slots, share, seq = x.shape
    high = bias[:, 0:1].astype(LOW)
    rest = bias[:, 0:1] - high.astype(F32)
    mid = rest.astype(LOW)
    for i in range(slots):
        out[i] = jnp.zeros(out.shape[1:], LOW)
        out[i, :, :seq] = x[i]
        out[i, :, seq : seq + 1] = high
        out[i, :, seq + 1 : seq + 2] = mid
        out[i, :, seq + 2 : seq + 3] = (rest - mid.astype(F32)).astype(LOW)


def prepare_grad_kernel(live, x, out, sums):
    slots, share, seq = x.shape
    total = 0.0
    for i in range(slots):
        out[i] = jnp.zeros(out.shape[1:], LOW)
        out[i, :, :seq] = (x[i].astype(F32) * live[i]).astype(LOW)
        total = total + dot_nt(jnp.ones((8, out.shape[2]), LOW), out[i])
    sums[...] = total


def place_kernel(pos, *refs):
    count = len(refs) - 3
    far, out, turned = refs[count:]
    for m in range(count):
        out[pos[2 * m]] = refs[m][...]
        out[pos[2 * m + 1]] = far[m]
    rows = out.shape[0] * out.shape[1]
    turned[...] = out[...].reshape(rows, out.shape[2]).T


def join_kernel(near, far, out, turned):
    rows, half = near.shape
    out[:, :half] = near[...]
    out[: rows // 2, half:] = far[rows // 2 :]
    out[rows // 2 :, half:] = far[: rows // 2]
    turned[...] = near[:, : half // 2].T


def attn_fwd_kernel(seq, xo, xy, xc, xd, vec, w, bias, attn_in, qkv, mixed, stats, lse):
    share, count = xo.shape
    heads = share // HDIM
    gain, shift = vec[:, 0:1], vec[:, 1:2]
    for at in lanes(count):
        x = rows4(xo[:, at], xy[:, at], xc[:, at], xd[:, at]).astype(F32)
        mean = jnp.mean(x, axis=0, keepdims=True)
        centred = x - mean
        inverse = lax.rsqrt(jnp.mean(centred * centred, axis=0, keepdims=True) + EPSILON)
        low = (centred * inverse * gain + shift).astype(LOW)
        attn_in[:, at] = low
        stats[0:1, at] = mean
        stats[1:2, at] = inverse
        part = dot_nn(w[...], low) + bias[:, 0:1]
        for i in range(3 * heads):
            qkv[i, :, at] = part[i * HDIM : (i + 1) * HDIM].astype(LOW)
    c = LOG2E / math.sqrt(HDIM)
    mask = lax.broadcasted_iota(jnp.int32, (count, 1), 0) < seq
    out = []
    for h in range(heads):
        q, k, v = qkv[h], qkv[heads + h], qkv[2 * heads + h]
        s = jnp.where(mask, dot_tn(k, q), MASKED)
        top = jnp.max(s, axis=0, keepdims=True)
        e = jnp.exp2((s - top) * c)
        total = jnp.sum(e, axis=0, keepdims=True)
        lse[h : h + 1, :] = top * c + jnp.log2(total)
        out.append(dot_nn(v, e.astype(LOW)) * (1.0 / total))
    mixed[...] = jnp.concatenate(out, axis=0).astype(LOW)


def mlp_fwd_kernel(
    seq, xo, xy, xc, xd, mo, my, mc, md, vec, w_out, up, up_bias, down,
    mlp_in, norm2, activ, slope, base, stats, keep, send,
):
    share, count = xo.shape
    gain, shift = vec[:, 3:4], vec[:, 4:5]
    tail = rows4(xo[:, seq:], xy[:, seq:], xc[:, seq:], xd[:, seq:]).astype(F32)
    o_bias = tail[:, 0:1] + tail[:, 1:2] + tail[:, 2:3]
    for at in lanes(count):
        mixed = rows4(mo[:, at], my[:, at], mc[:, at], md[:, at])
        x = rows4(xo[:, at], xy[:, at], xc[:, at], xd[:, at]).astype(F32)
        hidden = x + dot_nn(w_out[...], mixed) + o_bias
        mean = jnp.mean(hidden, axis=0, keepdims=True)
        centred = hidden - mean
        inverse = lax.rsqrt(jnp.mean(centred * centred, axis=0, keepdims=True) + EPSILON)
        normed = centred * inverse
        stats[0:1, at] = inverse
        norm2[:, at] = normed.astype(LOW)
        low = (normed * gain + shift).astype(LOW)
        mlp_in[:, at] = low
        v = dot_nn(up[...], low) + up_bias[:, 0:1]
        square = v * v
        tanh = jnp.tanh(v * (GELU_A + GELU_A * GELU_B * square))
        gate = 0.5 + 0.5 * tanh
        act = (v * gate).astype(LOW)
        activ[:, at] = act
        slope[:, at] = (
            gate + v * (0.5 - 0.5 * tanh * tanh) * (GELU_A + 3.0 * GELU_A * GELU_B * square)
        ).astype(LOW)
        part = dot_nn(down[...], act)
        base[:, at] = hidden[:share] + part[:share] + vec[:share, 5:6]
        keep[:, at] = part[share : 2 * share]
        send[0, :, at] = part[2 * share : 3 * share].astype(LOW)
        send[1, :, at] = part[3 * share :].astype(LOW)


def mlp_bwd_kernel(co, cy, cc, cd, slope, down, up, cot, pre_grad, keep, send, sums):
    share, count = co.shape
    for at in lanes(count):
        c = rows4(co[:, at], cy[:, at], cc[:, at], cd[:, at])
        cot[:, at] = c
        low = (dot_nn(down[...], c) * slope[:, at].astype(F32)).astype(LOW)
        pre_grad[:, at] = low
        part = dot_nn(up[...], low)
        keep[0, :, at] = part[:share]
        keep[1, :, at] = part[share : 2 * share]
        send[0, :, at] = part[2 * share : 3 * share].astype(LOW)
        send[1, :, at] = part[3 * share :].astype(LOW)
    sums[...] = dot_nt(jnp.ones((8, count), LOW), pre_grad[...])


def attn_bwd_kernel(
    seq, half, across, far, cot, norm2, stats2, vec, w_out, qkv, lse, w, attn_in,
    branch, h_grad, dqkv, keep_o, keep_y, send, stats, sums_own, sums_qkv,
    dmix,
):
    width, count = cot.shape
    share = width // 4
    heads = share // HDIM
    gain2 = vec[:, 3:4]
    sums = [0.0, 0.0, 0.0]
    for at in lanes(count):
        near = half[:, :, at] + across[:, :, at].astype(F32)
        ng = rows4(near[0], near[1], far[0, :, at].astype(F32), far[1, :, at].astype(F32))
        n2 = norm2[:, at].astype(F32)
        g = ng * gain2
        first = jnp.mean(g, axis=0, keepdims=True)
        second = jnp.mean(g * n2, axis=0, keepdims=True)
        hg = cot[:, at].astype(F32) + stats2[0:1, at] * (g - first - n2 * second)
        h_grad[:, at] = hg[:share]
        low = hg.astype(LOW)
        branch[:, at] = low
        dm = dot_nn(w_out[...], low)
        for h in range(heads):
            dmix[h, :, at] = dm[h * HDIM : (h + 1) * HDIM].astype(LOW)
        own = ng[:share]
        now = [hg[:share], own * n2[:share], own]
        sums = [a + jnp.sum(b, axis=1, keepdims=True) for a, b in zip(sums, now)]
    sums_own[...] = column(sums)
    scale = 1.0 / math.sqrt(HDIM)
    c = LOG2E * scale
    mask = lax.broadcasted_iota(jnp.int32, (count, 1), 0) < seq
    dq, dk, dv = [], [], []
    for h in range(heads):
        q, k, v, dm = qkv[h], qkv[heads + h], qkv[2 * heads + h], dmix[h]
        p = jnp.where(mask, jnp.exp2(dot_tn(k, q) * c - lse[h : h + 1, :]), 0.0)
        dp = dot_tn(v, dm)
        delta = jnp.sum(p * dp, axis=0, keepdims=True)
        ds = (p * (dp - delta)).astype(LOW)
        dq.append(dot_nn(k, ds) * scale)
        dk.append(dot_nt(q, ds) * scale)
        dv.append(dot_nt(dm, p.astype(LOW)))
    for j, part in enumerate((dq, dk, dv)):
        dqkv[j * share : (j + 1) * share, :] = jnp.concatenate(part, axis=0).astype(LOW)
    gain1, shift1 = vec[:, 0:1], vec[:, 1:2]
    for at in lanes(count):
        part = dot_nn(w[...], dqkv[:, at])
        keep_o[:, at] = part[:share]
        keep_y[:, at] = part[share : 2 * share]
        send[0, :, at] = part[2 * share : 3 * share].astype(LOW)
        send[1, :, at] = part[3 * share :].astype(LOW)
        stats[0:1, at] = jnp.sum(part * gain1, axis=0, keepdims=True)
        stats[1:2, at] = jnp.sum(part * (attn_in[:, at].astype(F32) - shift1), axis=0, keepdims=True)
    sums_qkv[...] = dot_nt(jnp.ones((8, count), LOW), dqkv[...])


def out_kernel(live, base, came, across, out):
    seq = out.shape[2]
    rows = base[0] + came[0, 0].astype(F32) + across[0].astype(F32)
    out[0] = (rows * live[pl.program_id(0)])[:, :seq].astype(LOW)


def grad_kernel(h_grad, keep, came, across, x_own, stats1, stats, vec, _, out, sums):
    share, seq = out.shape
    ng = keep[...] + came[0].astype(F32) + across[...].astype(F32)
    inverse = stats1[1:2, :]
    n1 = (x_own[...].astype(F32) - stats1[0:1, :]) * inverse
    mean = stats[...] * (1.0 / (4 * share))
    rows = h_grad[...] + inverse * (ng * vec[:, 0:1] - mean[0:1] - n1 * mean[1:2])
    out[...] = rows[:, :seq].astype(LOW)
    sums[...] = column(
        [jnp.sum(ng * n1, axis=1, keepdims=True), jnp.sum(ng, axis=1, keepdims=True)]
    )


def weight_grad_kernel(count, *refs):
    a, b, out = refs[1 : count + 1], refs[count + 1 : 2 * count + 1], refs[-1]
    total = dot_nt(a[0][...], b[0][...])
    for i in range(1, count):
        total = total + dot_nt(a[i][...], b[i][...])
    out[0] = total.astype(LOW)


def weight_split_kernel(count, *refs):
    odd, a, b = refs[1][0] == 1, refs[2 : count + 2], refs[count + 2 : 2 * count + 2]
    keep, send = refs[-2:]
    total = dot_nt(a[0][...], b[0][...])
    for i in range(1, count):
        total = total + dot_nt(a[i][...], b[i][...])
    half = total.shape[0] // 2
    top, low = total[:half], total[half:]
    keep[0] = jnp.where(odd, low, top)
    send[0] = jnp.where(odd, top, low).astype(LOW)


def shaped(*dims, dtype=LOW):
    return jax.ShapeDtypeStruct(dims, dtype)


def spec_of(array):
    if isinstance(array, tuple):
        array, i = array
        zeros = (0,) * (len(array.shape) - 1)
        return pl.BlockSpec(
            (None, *array.shape[1:]), lambda _: (i, *zeros), pipeline_mode=pl.Buffered(1)
        )
    zeros = (0,) * len(array.shape)
    return pl.BlockSpec(array.shape, lambda _: zeros, pipeline_mode=pl.Buffered(1))


SCALARS = pl.BlockSpec(memory_space=pltpu.SMEM)
LEFT = pl.BlockSpec(memory_space=pl.ANY)


def array_of(array):
    return array[0] if isinstance(array, tuple) else array


def run(kernel, outs, args, name, flops, scratch=(), after=(), scalars=0, buffers=None):
    arrays = [array_of(a) for a in args]
    shapes = [array_of(o) for o in outs]
    moved = sum(math.prod(a.shape) * a.dtype.itemsize for a in [*arrays, *shapes])
    buffers = buffers or {}
    used, extra = len(args), len(buffers) + len(after)

    def body(*refs):
        kernel(*refs[:used], *refs[used + extra :])

    return pl.pallas_call(
        body,
        grid=(1,),
        out_shape=tuple(shapes),
        in_specs=[*[SCALARS] * scalars, *map(spec_of, args[scalars:]), *[LEFT] * extra],
        out_specs=tuple(map(spec_of, outs)),
        input_output_aliases={used + j: o for j, o in enumerate(buffers)},
        scratch_shapes=scratch,
        compiler_params=pltpu.CompilerParams(vmem_limit_bytes=VMEM_LIMIT),
        cost_estimate=pl.CostEstimate(flops=flops, bytes_accessed=moved, transcendentals=0),
        name=name,
    )(*arrays, *buffers.values(), *after)


def prepare(array, bias, count):
    slots, share, _ = array.shape
    return run(prepare_kernel, [shaped(slots, share, count)], [array, bias], "prepare", 10**6)[0]


def prepare_grad(array, live, count, after=()):
    slots, share, _ = array.shape
    outs = [shaped(slots, share, count), shaped(8, share, dtype=F32)]
    return run(
        prepare_grad_kernel, outs, [live, array], "prepare", 10**6, after=after, scalars=1
    )


def attn_fwd(x, i, vec, w, bias, seq, after=()):
    slots, share, count = x[0].shape
    outs = [
        shaped(4 * share, count),
        shaped(3 * share // HDIM, HDIM, count),
        shaped(share, count),
        shaped(8, count, dtype=F32),
        shaped(8, count, dtype=F32),
    ]
    flops = 2 * count * 12 * share * share + 8 * count * count * 256
    return run(
        functools.partial(attn_fwd_kernel, seq), outs, [*[(a, i) for a in x], vec, w, bias],
        "attn_fwd", flops, after=after,
    )


def mlp_fwd(x, m, i, vec, w_out, up, up_bias, down, seq, buffers, after=()):
    slots, share, count = x[0].shape
    hidden = up.shape[0]
    outs = [
        shaped(4 * share, count),
        shaped(4 * share, count),
        shaped(hidden, count),
        shaped(hidden, count),
        (shaped(slots, share, count, dtype=F32), i),
        shaped(8, count, dtype=F32),
        (shaped(slots, share, count, dtype=F32), i),
        (shaped(slots, 2, share, count), i),
    ]
    flops = 2 * count * 4 * share * (4 * share + 2 * hidden)
    args = [*[(a, i) for a in x], *m, vec, w_out, up, up_bias, down]
    return run(
        functools.partial(mlp_fwd_kernel, seq), outs, args, "mlp_fwd", flops,
        after=after, buffers=buffers,
    )


def mlp_bwd(c, i, slope, down, up, after=()):
    _, share, count = c[0].shape
    hidden = up.shape[1]
    outs = [
        shaped(4 * share, count),
        shaped(hidden, count),
        shaped(2, share, count, dtype=F32),
        shaped(2, share, count),
        shaped(8, hidden, dtype=F32),
    ]
    flops = 2 * count * 4 * share * 2 * hidden
    args = [*[(a, i) for a in c], slope, down, up]
    return run(mlp_bwd_kernel, outs, args, "mlp_bwd", flops, after=after)


def attn_bwd(ng, cot, norm2, stats2, vec, w_out, qkv, lse, w, attn_in, seq, after=()):
    width, count = cot.shape
    share = width // 4
    outs = [
        shaped(width, count),
        shaped(share, count, dtype=F32),
        shaped(3 * share, count),
        shaped(share, count, dtype=F32),
        shaped(share, count, dtype=F32),
        shaped(2, share, count),
        shaped(8, count, dtype=F32),
        shaped(share, 8, dtype=F32),
        shaped(8, 3 * share, dtype=F32),
    ]
    flops = 2 * count * 16 * share * share + 20 * count * count * 256
    args = [*ng, cot, norm2, stats2, vec, w_out, qkv, lse, w, attn_in]
    scratch = (pltpu.VMEM((share // HDIM, HDIM, count), LOW),)
    return run(
        functools.partial(attn_bwd_kernel, seq), outs, args, "attn_bwd", flops, scratch, after
    )


def finish_grad(args, i, buffer, slots, seq):
    share = args[0].shape[0]
    outs = [(shaped(slots, share, seq), i), shaped(share, 8, dtype=F32)]
    buffers = {} if buffer is None else {0: buffer}

    def kernel(*refs):
        grad_kernel(*refs[:8], None, *refs[8:])

    return run(kernel, outs, args, "grad", 10**6, buffers=buffers)


def finish_out(live, base, came, across, seq):
    slots, share, count = base.shape
    return pl.pallas_call(
        out_kernel,
        grid=(slots,),
        out_shape=shaped(slots, share, seq),
        in_specs=[
            SCALARS,
            pl.BlockSpec((1, share, count), lambda i: (i, 0, 0)),
            pl.BlockSpec((1, 1, share, count), lambda i: (i, 0, 0, 0)),
            pl.BlockSpec((1, share, count), lambda i: (i, 0, 0)),
        ],
        out_specs=pl.BlockSpec((1, share, seq), lambda i: (i, 0, 0)),
        compiler_params=pltpu.CompilerParams(vmem_limit_bytes=VMEM_LIMIT),
        name="out",
    )(live, base, came, across)


def place(near, far, pos):
    count = 2 * len(near)
    rows, hidden = near[0].shape
    outs = [shaped(count, rows, hidden), shaped(hidden, count * rows)]
    placed, turned = run(place_kernel, outs, [pos, *near, far], "place", 10**6, scalars=1)
    return placed.reshape(count * rows, hidden), turned


def join(near, far):
    rows, half = near.shape
    outs = [shaped(rows, 2 * half), shaped(half // 2, rows)]
    return run(join_kernel, outs, [near, far], "join", 10**6)


def weight_grad(a, b, order, after=()):
    width, count = a[0].shape
    share, hidden = width // 4, b[0].shape[0]
    slots = len(a)
    out = shaped(4, share, hidden)
    moved = sum(math.prod(v.shape) * 2 for v in [*a, *b, out])
    out = pl.pallas_call(
        lambda *refs: weight_grad_kernel(slots, *refs),
        out_shape=out,
        grid_spec=pltpu.PrefetchScalarGridSpec(
            num_scalar_prefetch=1,
            grid=(4,),
            in_specs=[
                *[pl.BlockSpec((share, count), lambda r, order: (r, 0)) for _ in a],
                *[pl.BlockSpec((hidden, count), lambda r, order: (0, 0)) for _ in b],
                *[pl.BlockSpec(memory_space=pl.ANY)] * len(after),
            ],
            out_specs=pl.BlockSpec((1, share, hidden), lambda r, order: (order[r], 0, 0)),
        ),
        compiler_params=pltpu.CompilerParams(vmem_limit_bytes=VMEM_LIMIT),
        cost_estimate=pl.CostEstimate(
            flops=2 * slots * width * hidden * count, bytes_accessed=moved, transcendentals=0
        ),
        name="weight_grad",
    )(order, *a, *b, *after)
    return out.reshape(width, hidden)


def weight_split(a, b, order, odd, after=()):
    width, count = a[0].shape
    share, hidden = width // 4, b[0].shape[0]
    slots = len(a)
    outs = [shaped(4, share // 2, hidden, dtype=F32), shaped(4, share // 2, hidden)]
    moved = sum(math.prod(v.shape) * 2 for v in [*a, *b, *outs])
    return pl.pallas_call(
        lambda *refs: weight_split_kernel(slots, *refs),
        out_shape=outs,
        grid_spec=pltpu.PrefetchScalarGridSpec(
            num_scalar_prefetch=2,
            grid=(4,),
            in_specs=[
                *[pl.BlockSpec((share, count), lambda r, order, odd: (r, 0)) for _ in a],
                *[pl.BlockSpec((hidden, count), lambda r, order, odd: (0, 0)) for _ in b],
                *[pl.BlockSpec(memory_space=pl.ANY)] * len(after),
            ],
            out_specs=[
                pl.BlockSpec((1, share // 2, hidden), lambda r, order, odd: (order[r], 0, 0))
            ]
            * 2,
        ),
        compiler_params=pltpu.CompilerParams(vmem_limit_bytes=VMEM_LIMIT),
        cost_estimate=pl.CostEstimate(
            flops=2 * slots * width * hidden * count, bytes_accessed=moved, transcendentals=0
        ),
        name="weight_grad",
    )(order, odd, *a, *b, *after)


def place_blocks_kernel(order, value, out, turned):
    for r in range(4):
        out[r] = value[order[r]]
    rows = out.shape[0] * out.shape[1]
    turned[...] = out[...].reshape(rows, out.shape[2]).T


def place_blocks(value, t):
    rows, hidden = value.shape
    order = jnp.stack([t ^ m for m in (0, 2, 1, 3)]).astype(jnp.int32)
    placed, turned = run(
        place_blocks_kernel,
        [shaped(4, rows // 4, hidden), shaped(hidden, rows)],
        [order, value.reshape(4, rows // 4, hidden)],
        "place",
        10**6,
        scalars=1,
    )
    return placed.reshape(rows, hidden), turned


def gate(values, after):
    values, _ = lax.optimization_barrier((list(values), list(after)))
    return values


def dp_swap(value, mask):
    size = lax.axis_size("dp")
    return lax.ppermute(value, "dp", [(i, i ^ mask) for i in range(size)])


def gather_dp_whole(shard, t):
    size = lax.axis_size("dp")
    value = lax.all_gather(shard, "dp", axis=0, tiled=True)
    if size != 8:
        value = rel_blocks(value, t)
        return value, value.T
    return place_blocks(value, t)


def gather_first(shard):
    return [shard, *[dp_swap(shard, m) for m in (2, 4, 6)]]


def gather_second(near, far, t):
    pos = []
    for m in range(8):
        k = lax.axis_index("dp") ^ m
        b = t ^ (k >> 1)
        pos.append((((b & 1) << 1) | (b >> 1)) * 2 + (k & 1))
    return place(near, far, jnp.stack(pos).astype(jnp.int32))


def scatter_dp(a, b, t, direct, after=()):
    size = lax.axis_size("dp")
    order = jnp.stack([t ^ m for m in (0, 2, 1, 3)]).astype(jnp.int32)
    if size != 8 or not direct:
        value = weight_grad(a, b, order, after)
        return lax.psum_scatter(value, "dp", scatter_dimension=0, tiled=True).astype(F32)
    me = lax.axis_index("dp")
    keep, send = weight_split(a, b, order ^ (me >> 1), (me & 1).reshape(1).astype(jnp.int32), after)
    total = keep + dp_swap(send, 1).astype(F32)
    out = total[0]
    for j in (1, 2, 3):
        out = out + dp_swap(total[j].astype(LOW), 2 * j).astype(F32)
    return out


def sum_dp(value):
    size = lax.axis_size("dp")
    if size != 8:
        return lax.psum(value, "dp")
    value = value + dp_swap(value, 1)
    return sum((dp_swap(value, m) for m in (2, 4, 6)), value)


def columns(vectors, count=8):
    vectors = [*vectors, *[jnp.zeros_like(vectors[0])] * (count - len(vectors))]
    return jnp.stack(vectors, axis=1)


def local(
    images,
    image_count,
    attn_gain,
    attn_shift,
    query_weight,
    query_bias,
    key_weight,
    value_weight,
    value_bias,
    output_weight,
    output_bias,
    mlp_gain,
    mlp_shift,
    up_weight,
    up_bias,
    down_weight,
    down_bias,
    cotangent,
):
    images, cotangent = images.transpose(0, 2, 1), cotangent.transpose(0, 2, 1)
    slots, share, seq = images.shape
    t = lax.axis_index("tensor")
    count = -(-seq // TILE) * TILE
    zero = jnp.zeros_like(output_bias)
    gains = [rel_blocks(a, t) for a in (attn_gain, attn_shift, mlp_gain, mlp_shift)]
    down_rows = jnp.concatenate([down_bias, zero, zero, zero])
    vec = columns([gains[0], gains[1], gains[1], gains[2], gains[3], down_rows])
    vec_own = vec[:share]
    qkv_bias = columns([jnp.concatenate([query_bias, zero, value_bias])])
    up_b = columns([up_bias])
    live = (jnp.arange(slots) < image_count[0]).astype(F32)

    fast = lax.axis_size("dp") == 8
    qkv_shard = jnp.concatenate([query_weight, key_weight, value_weight], axis=1)
    out_t = output_weight.T
    out_shard = jnp.concatenate([out_t, y_swap(out_t)], axis=1)
    x_own = prepare(images, columns([output_bias]), count)
    x_across = y_swap(*gate([x_own], [out_shard]))
    up_value = lax.all_gather(up_weight, "dp", axis=0, tiled=True)
    cot_own, cot_sums = prepare_grad(cotangent, live, count, [x_own])
    if fast:
        near = gather_first(*gate([qkv_shard], [x_own]))
        near_stack, out_shard = gate([jnp.stack(near), out_shard], near[1:])
        far = dp_swap(near_stack, 1)
        out_near = gather_first(out_shard)
        x_across, x_own2, cot_send = gate([x_across, x_own, cot_own], near[1:])
        (down_shard, cot_send) = gate([down_weight.T, cot_send], [*out_near[1:], x_across])
        down_near = gather_first(down_shard)
        qkv_w, qkv_t = gather_second(near, far, t)
    else:
        x_own2, cot_send = x_own, cot_own
        qkv_w, qkv_t = gather_dp_whole(qkv_shard, t)
    cot_across = y_swap(cot_send)
    x = [x_own, x_across, core_swap(x_own2), core_swap(x_across)]
    fwd, mixes = [], []
    for i in range(slots):
        after = [fwd[i - 1][4]] if i else [cot_sums]
        if i == 0 and fast:
            (out_stack,) = gate([jnp.stack(out_near)], [far])
            out_far = dp_swap(out_stack, 1)
        if i == 2 and fast:
            out_far, down_stack = gate([out_far, jnp.stack(down_near)], after)
            down_far = dp_swap(down_stack, 1)
        fwd.append(attn_fwd(x, i, vec, qkv_t, qkv_bias, seq, after))
        mixes.append([fwd[i][2], y_swap(fwd[i][2])])
    if fast:
        (o_half, _) = gather_second(out_near, out_far, t)
        down_t, down_w = gather_second(down_near, down_far, t)
        up_w, up_t = place_blocks(up_value, t)
    else:
        o_half, _ = gather_dp_whole(out_shard, t)
        down_t, down_w = gather_dp_whole(down_weight.T, t)
        up_w, up_t = gather_dp_whole(up_weight, t)
    o_full, o_mine = join(o_half, core_swap(o_half))
    for m in mixes:
        m.extend([core_swap(m[0]), core_swap(m[1])])
    (cot_across,) = gate([cot_across], [fwd[-1][2]])
    cot = [cot_own, cot_across, core_swap(cot_own), core_swap(cot_across)]

    mlp, back, ends = [], [], []
    norm2_grad = []
    last = [fwd[-1][4]]

    def attention_back(i, after):
        attn_in, qkv, _, stats1, lse = fwd[i]
        norm2, stats2 = mlp[i][1], mlp[i][5]
        ends.append(
            attn_bwd(
                norm2_grad[i], back[i][0], norm2, stats2, vec, o_mine, qkv, lse, qkv_w, attn_in,
                seq, after,
            )
        )

    for i in range(slots):
        buffers = {j: mlp[i - 1][j] for j in (4, 6, 7)} if i else {}
        mlp.append(mlp_fwd(x, mixes[i], i, vec, o_full, up_t, up_b, down_t, seq, buffers, last))
        if i:
            half, across = norm2_grad[i - 1]
            both = (half + across.astype(F32)).astype(LOW)
            (both,) = gate([both], [mlp[i][5]])
            norm2_grad[i - 1] = (half, across, core_swap(both))
        back.append(mlp_bwd(cot, i, mlp[i][3], down_w, up_w, [mlp[i][5]]))
        half = back[i][2] + core_swap(back[i][3]).astype(F32)
        norm2_grad.append((half, y_swap(half[::-1].astype(LOW))))
        last = [half]
    down_grad = scatter_dp([b[0] for b in back], [m[2] for m in mlp], t, True, last).T
    base, keep, send = (mlp[-1][j] for j in (4, 6, 7))
    came = core_swap(*gate([send], last))
    across = y_swap((keep + came[:, 1].astype(F32)).astype(LOW))
    out_buffer = finish_out(live, base, came, across, seq)
    up_grad = scatter_dp([m[0] for m in mlp], [b[1] for b in back], t, False, last)
    for i in range(slots):
        attention_back(i, last)
        last = [ends[i][-1]]
        if i == 0:
            half, across = norm2_grad[-1]
            both = (half + across.astype(F32)).astype(LOW)
            (both,) = gate([both], last)
            norm2_grad[-1] = (half, across, core_swap(both))
    mixed_rows = [f[2] for f in fwd]
    qkv_grad = scatter_dp([f[0] for f in fwd], [e[2] for e in ends], t, True)
    out_grad = scatter_dp([e[0] for e in ends], mixed_rows, t, True).T
    grad_buffer, sums = None, None
    for group in (list(range(slots - 1)), [slots - 1]):
        came = [core_swap(ends[i][5]) for i in group]
        across = y_swap(
            jnp.stack([(ends[i][4] + c[1].astype(F32)).astype(LOW) for i, c in zip(group, came)])
        )
        stats = jnp.stack([ends[i][6] for i in group])
        stats = stats + core_swap(stats)
        stats = stats + y_swap(stats)
        for j, i in enumerate(group):
            grad_buffer, grad_sums = finish_grad(
                [ends[i][1], ends[i][3], came[j], (across, j), (x_own, i), fwd[i][3], (stats, j), vec_own],
                i, grad_buffer, slots, seq,
            )
            now = (grad_sums, ends[i][7], ends[i][8], back[i][-1])
            sums = now if sums is None else jax.tree.map(jnp.add, sums, now)
    sums = (*sums, cot_sums)
    sizes = [2 * share, 3 * share, 3 * share, up_bias.shape[0], share]
    small = jnp.concatenate(
        [
            sums[0][:, :2].T.reshape(-1),
            sums[1][:, :3].T.reshape(-1),
            sums[2][0],
            sums[3][0],
            sums[4][0],
        ]
    )
    small = sum_dp(small)
    parts, at = [], 0
    for size in sizes:
        parts.append(small[at : at + size])
        at += size
    grad_sums, own_sums = parts[0].reshape(2, share), parts[1].reshape(3, share)
    qkv_sums, up_sum, cot_sum = parts[2:]
    return (
        out_buffer.transpose(0, 2, 1),
        grad_buffer.transpose(0, 2, 1),
        grad_sums[0],
        grad_sums[1],
        qkv_grad[:, :share],
        qkv_sums[:share],
        qkv_grad[:, share : 2 * share],
        qkv_grad[:, 2 * share :],
        qkv_sums[2 * share :],
        out_grad,
        own_sums[0],
        own_sums[1],
        own_sums[2],
        up_grad,
        up_sum,
        down_grad,
        cot_sum,
    )


def solution(mesh):
    in_specs = (
        P("dp", None, "tensor"),
        P("dp"),
        P(),
        P(),
        P("dp", "tensor"),
        P("tensor"),
        P("dp", "tensor"),
        P("dp", "tensor"),
        P("tensor"),
        P("tensor", "dp"),
        P("tensor"),
        P(),
        P(),
        P("dp", "tensor"),
        P("tensor"),
        P("tensor", "dp"),
        P("tensor"),
        P("dp", None, "tensor"),
    )
    out_specs = (
        P("dp", None, "tensor"),
        P("dp", None, "tensor"),
        P("tensor"),
        P("tensor"),
        P("dp", "tensor"),
        P("tensor"),
        P("dp", "tensor"),
        P("dp", "tensor"),
        P("tensor"),
        P("tensor", "dp"),
        P("tensor"),
        P("tensor"),
        P("tensor"),
        P("dp", "tensor"),
        P("tensor"),
        P("tensor", "dp"),
        P("tensor"),
    )
    return jax.shard_map(local, mesh=mesh, in_specs=in_specs, out_specs=out_specs, check_vma=False)
```

time: 1490 us -> 581 us (0.39)
  waiting for transfers between devices: 913 us -> 167 us
  Pallas kernels: 0 us -> 259 us
  matrix products: 214 us -> 0 us
  blocking collectives: 188 us -> 0 us
  other arithmetic: 108 us -> 38.6 us
  starting transfers between devices: 3.9 us -> 53.4 us
    reduce_scatter x18 -> x1, waiting for transfers between devices: 696 us -> 0.01 us  [scatter_dp(): lax.psum_scatter(value, 'dp', scatter_dimension=0, tiled=True).astype(F32)]
    pallas_call x0 -> x27, Pallas kernels: none -> 259 us  [the longest x22 212 us: run(): pl.pallas_call(body, grid=(1,), out_shape=tuple(shapes), in_specs=[*[SCAL...]
    dot_general x72 -> x0, matrix products: 214 us -> none  [the longest x3 22.7 us: local(): jnp.einsum('sd,fd->sf', grad_low, down_full, preferred_element_type=jnp.f...]
    all_gather x14 -> x1, waiting for transfers between devices: 212 us -> 0.01 us  [local(): up_value = lax.all_gather(up_weight, 'dp', axis=0, tiled=True)]
    ppermute x0 -> x65, waiting for transfers between devices: none -> 167 us  [the longest x28 136 us: dp_swap(): return lax.ppermute(value, 'dp', [(i, i ^ mask) for i in range(size)])]
    all_gather x4 -> x0, blocking collectives: 127 us -> none  [the longest x1 32.6 us: fetch_weights(): lax.all_gather(value_weight, 'dp', axis=0, tiled=True)]
    psum x3 -> x0, blocking collectives: 60.6 us -> none  [the longest x1 37.6 us: local(): lax.psum((grads_sum[6], grads_sum[7], grads_sum[8], grads_sum[9], grads_s...]
    ppermute x0 -> x65, starting transfers between devices: none -> 53.3 us  [the longest x28 33.8 us: dp_swap(): return lax.ppermute(value, 'dp', [(i, i ^ mask) for i in range(size)])]
  transfers between devices with their start and end apart: 32 -> 67, of which waited for: 22 -> 24; matrix products, arithmetic and copies ran while one was open for 21% -> 12% of each run, Pallas kernels for 0% -> 38%
where the time goes in v1:
time: 581 us; the launch traced here: 570 us
  Pallas kernels  259 us (45%)
  waiting for transfers between devices  167 us (29%)
  starting transfers between devices  53.4 us (9%)
  other arithmetic  38.6 us (7%)
  local copies, waits for them, and re-layouts  36.7 us (6%)
  between operations  15.5 us (3%)
    pallas_call x22, Pallas kernels, run(): pl.pallas_call(body, grid=(1,), out_shape=tuple(shapes), in_specs=[*[SCAL...  212 us
    ppermute x28, waiting for transfers between devices, dp_swap(): return lax.ppermute(value, 'dp', [(i, i ^ mask) for i in range(size)])  136 us
    ppermute x28, starting transfers between devices, dp_swap(): return lax.ppermute(value, 'dp', [(i, i ^ mask) for i in range(size)])  33.8 us
    pallas_call x3, Pallas kernels, weight_split(): pl.pallas_call(lambda *refs: weight_split_kernel(slots, *refs), out_shape...  30.9 us
    ppermute x14, waiting for transfers between devices, y_swap(): return lax.ppermute(value, 'tensor', Y_SWAP)  30.8 us
    ppermute x14, starting transfers between devices, y_swap(): return lax.ppermute(value, 'tensor', Y_SWAP)  16.6 us
    pallas_call x1, Pallas kernels, weight_grad(): pl.pallas_call(lambda *refs: weight_grad_kernel(slots, *refs), out_shape=...  12.5 us
  transfers between devices with their start and end apart: 67, of which 24 were waited for; matrix products, arithmetic and copies ran while one was open for 12% of the time, Pallas kernels for 38%

profile of v1, /device:TPU:8, one launch (start us, length us, event | category | flops | bytes accessed | tf_op | source)
XLA Modules:
  0.0 570.5 jit_solution(11043882751988790775)
XLA Ops:
  7.3 1.6 collective-permute-start
  10.7 2.6 prepare.2.refs_2_.refs_0_.refs_4_
  14.7 2.6 collective-permute-start.3
  17.8 6.0 %collective-permute-done.2.refs_2_ = bf16[144,864]{1,0:T(8,128)(2,1)S(1)} collective-permute-done((bf16[144,864]{1,0:T(8,128)(2,1)S(1)}, bf16[144,864]{1,0:T(8,128)(2,1)S(1)}, u32[]{:S(2)}, u32[]{:S(2)}) %collective-permute-start.2) | collective-permute-done | bytes 248864 | tf_op jit(solution)/shard_map/ppermute | solution.py:544
  23.9 16.8 %collective-permute-done.3.refs_3_ = bf16[144,864]{1,0:T(8,128)(2,1)S(1)} collective-permute-done((bf16[144,864]{1,0:T(8,128)(2,1)S(1)}, bf16[144,864]{1,0:T(8,128)(2,1)S(1)}, u32[]{:S(2)}, u32[]{:S(2)}) %collective-permute-start.3) | collective-permute-done | bytes 248864 | tf_op jit(solution)/shard_map/ppermute | solution.py:544
  40.7 9.5 %collective-permute-done.4.refs_4_ = bf16[144,864]{1,0:T(8,128)(2,1)S(1)} collective-permute-done((bf16[144,864]{1,0:T(8,128)(2,1)S(1)}, bf16[144,864]{1,0:T(8,128)(2,1)S(1)}, u32[]{:S(2)}, u32[]{:S(2)}) %collective-permute-start.4) | collective-permute-done | bytes 248864 | tf_op jit(solution)/shard_map/ppermute | solution.py:544
  54.9 3.0 prepare.3
  58.6 3.0 collective-permute-start.12
  61.6 13.2 %collective-permute-done.11.refs_2_ = bf16[144,576]{1,0:T(8,128)(2,1)S(1)} collective-permute-done((bf16[144,576]{1,0:T(8,128)(2,1)S(1)}, bf16[144,576]{1,0:T(8,128)(2,1)S(1)}, u32[]{:S(2)}, u32[]{:S(2)}) %collective-permute-start.11) | collective-permute-done | bytes 165920 | tf_op jit(solution)/shard_map/ppermute | solution.py:544
  74.8 1.9 collective-permute-start.13
  78.6 14.7 %collective-permute-done.13.refs_4_ = bf16[144,576]{1,0:T(8,128)(2,1)} collective-permute-done((bf16[144,576]{1,0:T(8,128)(2,1)S(1)}, bf16[144,576]{1,0:T(8,128)(2,1)}, u32[]{:S(2)}, u32[]{:S(2)}) %collective-permute-start.13) | collective-permute-done | bytes 165920 | tf_op jit(solution)/shard_map/ppermute | solution.py:544
  94.8 2.0 collective-permute-start.17
  99.6 3.9 place.4
  103.5 2.9 collective-permute-done.15.refs_2_
  106.4 1.6 collective-permute-start.14
  108.1 9.2 %collective-permute-done.16.refs_3_ = bf16[144,1076]{1,0:T(8,128)(2,1)} collective-permute-done((bf16[144,1076]{1,0:T(8,128)(2,1)S(1)}, bf16[144,1076]{1,0:T(8,128)(2,1)}, u32[]{:S(2)}, u32[]{:S(2)}) %collective-permute-start.16) | collective-permute-done | bytes 309920 | tf_op jit(solution)/shard_map/ppermute | solution.py:544
  117.3 1.6 collective-permute-start.26
  118.9 6.1 %collective-permute-done.17.refs_4_ = bf16[144,1076]{1,0:T(8,128)(2,1)} collective-permute-done((bf16[144,1076]{1,0:T(8,128)(2,1)S(1)}, bf16[144,1076]{1,0:T(8,128)(2,1)}, u32[]{:S(2)}, u32[]{:S(2)}) %collective-permute-start.17) | collective-permute-done | bytes 309920 | tf_op jit(solution)/shard_map/ppermute | solution.py:544
  125.0 2.6 pad_maximum_fusion
  127.6 10.0 %attn_fwd.3 = (bf16[1152,768]{1,0:T(8,128)(2,1)}, bf16[12,72,768]{2,1,0:T(8,128)(2,1)}, bf16[288,768]{1,0:T(8,128)(2,1)}, f32[8,768]{1,0:T(8,128)}, f32[8,768]{1,0:T(8,128)}) custom-call(bf16[3,288,768]{2,1,0:T(8,128)(2,1)} %prepare.2.refs_2_.refs_0_.refs_4_, bf16[3,288,768]{2,1,0:T(8,128)(2,1)} %copy-done.7, ...), custom_call_target="tpu_custom_call" | custom-call | flops 2736783360 | bytes 10951680 | tf_op jit(solution)/shard_map/attn_fwd/pallas_call | solution.py:314
  137.6 10.5 %attn_fwd.4 = (bf16[1152,768]{1,0:T(8,128)(2,1)}, bf16[12,72,768]{2,1,0:T(8,128)(2,1)}, bf16[288,768]{1,0:T(8,128)(2,1)}, f32[8,768]{1,0:T(8,128)}, f32[8,768]{1,0:T(8,128)}) custom-call(bf16[3,288,768]{2,1,0:T(8,128)(2,1)} %prepare.2.refs_2_.refs_0_.refs_4_, bf16[3,288,768]{2,1,0:T(8,128)(2,1)} %copy-done.7, ...), custom_call_target="tpu_custom_call" | custom-call | flops 2736783360 | bytes 10951680 | tf_op jit(solution)/shard_map/attn_fwd/pallas_call | solution.py:314
  149.1 3.1 place.5
  152.2 2.7 copy.65
  156.9 10.0 %attn_fwd.5 = (bf16[1152,768]{1,0:T(8,128)(2,1)}, bf16[12,72,768]{2,1,0:T(8,128)(2,1)}, bf16[288,768]{1,0:T(8,128)(2,1)}, f32[8,768]{1,0:T(8,128)}, f32[8,768]{1,0:T(8,128)}) custom-call(bf16[3,288,768]{2,1,0:T(8,128)(2,1)} %prepare.2.refs_2_.refs_0_.refs_4_, bf16[3,288,768]{2,1,0:T(8,128)(2,1)} %copy-done.7, ...), custom_call_target="tpu_custom_call" | custom-call | flops 2736783360 | bytes 10951680 | tf_op jit(solution)/shard_map/attn_fwd/pallas_call | solution.py:314
  167.7 9.9 %collective-permute-done.19.refs_5_ = bf16[4,144,1076]{2,1,0:T(8,128)(2,1)S(1)} collective-permute-done((bf16[4,144,1076]{2,1,0:T(8,128)(2,1)}, bf16[4,144,1076]{2,1,0:T(8,128)(2,1)S(1)}, u32[]{:S(2)}, u32[]{:S(2)}) %collective-permute-start.19) | collective-permute-done | bytes 1239584 | tf_op jit(solution)/shard_map/ppermute | solution.py:544
  179.4 4.3 place.7
  183.7 1.8 copy.66.refs_1_
  185.4 4.3 join.1
  189.7 4.8 place.6
  194.6 19.3 %mlp_fwd.3 = (bf16[1152,768]{1,0:T(8,128)(2,1)}, bf16[1152,768]{1,0:T(8,128)(2,1)}, bf16[1076,768]{1,0:T(8,128)(2,1)}, bf16[1076,768]{1,0:T(8,128)(2,1)}, f32[3,...) custom-call(bf16[3,288,768]{2,1,0:T(8,128)(2,1)} %prepare.2.refs_2_.refs_0_.refs, ...), custom_call_target="tpu_custom_call" | custom-call | flops 5846335488 | bytes 29593216 | tf_op jit(solution)/shard_map/mlp_fwd/pallas_call | solution.py:314
  213.9 11.2 %mlp_bwd.3 = (bf16[1152,768]{1,0:T(8,128)(2,1)}, bf16[1076,768]{1,0:T(8,128)(2,1)}, f32[2,288,768]{2,1,0:T(8,128)}, bf16[2,288,768]{2,1,0:T(8,128)(2,1)}, f32[8,1076]{1,0:T(8,128)}) custom-call(bf16[3,288,768]{2,1,0:T(8,128)(2,1)} %get-tuple-element.165.refs_0_, bf16[3,288,768]{2,1,0:T(8,128)(2,1)} %collective-permute-done.26.refs_1_, ...), custom_call_target="tpu_custom_call" | custom-call | flops 3807903744 | bytes 18030208 | tf_op jit(solution)/shard_map/mlp_bwd/pallas_call | solution.py:314
  226.9 10.7 %collective-permute-done.20.refs_5_ = bf16[288,768]{1,0:T(8,128)(2,1)S(1)} collective-permute-done((bf16[288,768]{1,0:T(8,128)(2,1)S(1)}, bf16[288,768]{1,0:T(8,128)(2,1)S(1)}, u32[]{:S(2)}, u32[]{:S(2)}) %collective-permute-start.20) | collective-permute-done | bytes 442400 | tf_op jit(solution)/shard_map/ppermute | solution.py:26
  237.7 3.1 convert_add_fusion.5.refs_16_.refs_0_
  241.7 19.3 %mlp_fwd.4 = (bf16[1152,768]{1,0:T(8,128)(2,1)}, bf16[1152,768]{1,0:T(8,128)(2,1)}, bf16[1076,768]{1,0:T(8,128)(2,1)}, bf16[1076,768]{1,0:T(8,128)(2,1)}, f32[3,...) custom-call(bf16[3,288,768]{2,1,0:T(8,128)(2,1)} %prepare.2.refs_2_., ...), custom_call_target="tpu_custom_call", output_to_operand_aliasing={{4}: (13, {}), {6}: (14, {}), {7}: (15, {})} | custom-call | flops 5846335488 | bytes 29593216 | tf_op jit(solution)/shard_map/mlp_fwd/pallas_call | solution.py:314
  261.0 11.1 %mlp_bwd.4 = (bf16[1152,768]{1,0:T(8,128)(2,1)}, bf16[1076,768]{1,0:T(8,128)(2,1)}, f32[2,288,768]{2,1,0:T(8,128)}, bf16[2,288,768]{2,1,0:T(8,128)(2,1)}, f32[8,1076]{1,0:T(8,128)}) custom-call(bf16[3,288,768]{2,1,0:T(8,128)(2,1)} %get-tuple-element.165.refs_0_, bf16[3,288,768]{2,1,0:T(8,128)(2,1)} %collective-permute-done.26.refs_1_, ...), custom_call_target="tpu_custom_call" | custom-call | flops 3807903744 | bytes 18030208 | tf_op jit(solution)/shard_map/mlp_bwd/pallas_call | solution.py:314
  273.9 11.1 %collective-permute-done.8.refs_5_ = bf16[288,768]{1,0:T(8,128)(2,1)} collective-permute-done((bf16[288,768]{1,0:T(8,128)(2,1)}, bf16[288,768]{1,0:T(8,128)(2,1)}, u32[]{:S(2)}, u32[]{:S(2)}) %collective-permute-start.8) | collective-permute-done | bytes 442400 | tf_op jit(solution)/shard_map/ppermute | solution.py:26
  287.5 2.6 convert_add_fusion.4.refs_16_.refs_0_
  290.0 19.5 %mlp_fwd.5 = (bf16[1152,768]{1,0:T(8,128)(2,1)}, bf16[1152,768]{1,0:T(8,128)(2,1)}, bf16[1076,768]{1,0:T(8,128)(2,1)}, bf16[1076,768]{1,0:T(8,128)(2,1)}, f32[3,...) custom-call(bf16[3,288,768]{2,1,0:T(8,128)(2,1)} %prepare.2.refs_2_., ...), custom_call_target="tpu_custom_call", output_to_operand_aliasing={{4}: (13, {}), {6}: (14, {}), {7}: (15, {})} | custom-call | flops 5846335488 | bytes 29593216 | tf_op jit(solution)/shard_map/mlp_fwd/pallas_call | solution.py:314
  309.6 11.1 %mlp_bwd.5 = (bf16[1152,768]{1,0:T(8,128)(2,1)}, bf16[1076,768]{1,0:T(8,128)(2,1)}, f32[2,288,768]{2,1,0:T(8,128)}, bf16[2,288,768]{2,1,0:T(8,128)(2,1)}, f32[8,1076]{1,0:T(8,128)}) custom-call(bf16[3,288,768]{2,1,0:T(8,128)(2,1)} %get-tuple-element.165.refs_0_, bf16[3,288,768]{2,1,0:T(8,128)(2,1)} %collective-permute-done.26.refs_1_, ...), custom_call_target="tpu_custom_call" | custom-call | flops 3807903744 | bytes 18030208 | tf_op jit(solution)/shard_map/mlp_bwd/pallas_call | solution.py:314
  325.3 2.3 add_convert_fusion.1
  328.6 2.6 convert_add_fusion.3.refs_12_.refs_0_.refs_7_.refs_8_
  331.1 12.6 %weight_grad.7 = (f32[4,144,1076]{2,1,0:T(8,128)}, bf16[4,144,1076]{2,1,0:T(8,128)(2,1)}) custom-call(s32[4]{0:T(128)} %get-tuple-element.265.refs_0_, s32[1]{0:T(128)} %bitcast.48.refs_1_, bf16[1152,768]{1,0:T(8,128)(2,1)} %get-tuple-element.189.refs_3_.refs_2_, bf16[1152,768]{1,0:T(8,128)(2,1)} %get-tuple-element.202.refs_3_, ...), custom_call_target="tpu_custom_call" | custom-call | flops 5711855616 | bytes 12745728 | tf_op jit(solution)/shard_map/weight_grad/pallas_call | solution.py:492
  346.9 2.3 add_convert_fusion
  349.2 12.5 %weight_grad.6 = bf16[4,288,1076]{2,1,0:T(8,128)(2,1)} custom-call(s32[4]{0:T(128)} %get-tuple-element.266.refs_0_, bf16[1152,768]{1,0:T(8,128)(2,1)} %get-tuple-element.248.refs_1_, bf16[1152,768]{1,0:T(8,128)(2,1)} %get-tuple-element.249.refs_2_, bf16[1152,768]{1,0:T(8,128)(2,1)} %get-tuple-element.250.refs_3_, ...), custom_call_target="tpu_custom_call" | custom-call | flops 5711855616 | bytes 12745728 | tf_op jit(solution)/shard_map/weight_grad/pallas_call | solution.py:464
  363.6 17.9 %attn_bwd.3 = (bf16[1152,768]{1,0:T(8,128)(2,1)}, f32[288,768]{1,0:T(8,128)}, bf16[864,768]{1,0:T(8,128)(2,1)}, f32[288,768]{1,0:T(8,128)}, f32[288,768]{1,0:T(8...) custom-call(f32[2,288,768]{2,1,0:T(8,128)} %convert_add_fusion.5.refs_16_.refs_0_,, ...), custom_call_target="tpu_custom_call" | custom-call | flops 5058330624 | bytes 19611648 | tf_op jit(solution)/shard_map/attn_bwd/pallas_call | solution.py:314
  381.6 1.7 copy.73
  384.2 18.1 %attn_bwd.4 = (bf16[1152,768]{1,0:T(8,128)(2,1)}, f32[288,768]{1,0:T(8,128)}, bf16[864,768]{1,0:T(8,128)(2,1)}, f32[288,768]{1,0:T(8,128)}, f32[288,768]{1,0:T(8...) custom-call(f32[2,288,768]{2,1,0:T(8,128)} %convert_add_fusion.4.refs_16_.refs_0_,, ...), custom_call_target="tpu_custom_call" | custom-call | flops 5058330624 | bytes 19611648 | tf_op jit(solution)/shard_map/attn_bwd/pallas_call | solution.py:314
  407.7 2.4 collective-permute-start.64
  410.9 9.9 %collective-permute-done.62 = bf16[144,1076]{1,0:T(8,128)(2,1)S(1)} collective-permute-done((bf16[144,1076]{1,0:T(8,128)(2,1)S(1)}, bf16[144,1076]{1,0:T(8,128)(2,1)S(1)}, u32[]{:S(2)}, u32[]{:S(2)}) %collective-permute-start.62) | collective-permute-done | bytes 309920 | tf_op jit(solution)/shard_map/ppermute | solution.py:544
  420.8 5.7 %collective-permute-done.63 = bf16[144,1076]{1,0:T(8,128)(2,1)S(1)} collective-permute-done((bf16[144,1076]{1,0:T(8,128)(2,1)S(1)}, bf16[144,1076]{1,0:T(8,128)(2,1)S(1)}, u32[]{:S(2)}, u32[]{:S(2)}) %collective-permute-start.63) | collective-permute-done | bytes 309920 | tf_op jit(solution)/shard_map/ppermute | solution.py:544
  426.5 23.0 %collective-permute-done.64 = bf16[144,1076]{1,0:T(8,128)(2,1)S(1)} collective-permute-done((bf16[144,1076]{1,0:T(8,128)(2,1)S(1)}, bf16[144,1076]{1,0:T(8,128)(2,1)S(1)}, u32[]{:S(2)}, u32[]{:S(2)}) %collective-permute-start.64) | collective-permute-done | bytes 309920 | tf_op jit(solution)/shard_map/ppermute | solution.py:544
  451.4 17.7 %attn_bwd.5 = (bf16[1152,768]{1,0:T(8,128)(2,1)}, f32[288,768]{1,0:T(8,128)}, bf16[864,768]{1,0:T(8,128)(2,1)}, f32[288,768]{1,0:T(8,128)}, f32[288,768]{1,0:T(8...) custom-call(f32[2,288,768]{2,1,0:T(8,128)} %convert_add_fusion.3.refs_12_.refs_0_., ...), custom_call_target="tpu_custom_call" | custom-call | flops 5058330624 | bytes 19611648 | tf_op jit(solution)/shard_map/attn_bwd/pallas_call | solution.py:314
  469.2 7.3 %weight_grad.5 = (f32[4,144,288]{2,1,0:T(8,128)}, bf16[4,144,288]{2,1,0:T(8,128)(2,1)}) custom-call(s32[4]{0:T(128)} %get-tuple-element.265.refs_0_, s32[1]{0:T(128)} %bitcast.48.refs_1_, bf16[1152,768]{1,0:T(8,128)(2,1)} %get-tuple-element.243.refs_2_, bf16[1152,768]{1,0:T(8,128)(2,1)} %get-tuple-element.244.refs_3_, ...), custom_call_target="tpu_custom_call" | custom-call | flops 1528823808 | bytes 7299072 | tf_op jit(solution)/shard_map/weight_grad/pallas_call | solution.py:492
  477.8 11.0 %weight_grad.4 = (f32[4,144,864]{2,1,0:T(8,128)}, bf16[4,144,864]{2,1,0:T(8,128)(2,1)}) custom-call(s32[4]{0:T(128)} %get-tuple-element.265.refs_0_, s32[1]{0:T(128)} %bitcast.48.refs_1_, bf16[1152,768]{1,0:T(8,128)(2,1)} %get-tuple-element.194.refs_11_.refs_2_, bf16[1152,768]{1,0:T(8,128)(2,1)} %get-tuple-element.205.refs_11_.refs_3_, ...), custom_call_target="tpu_custom_call" | custom-call | flops 4586471424 | bytes 11280384 | tf_op jit(solution)/shard_map/weight_grad/pallas_call | solution.py:492
  501.0 2.8 fusion
  503.9 2.5 collective-permute-start.60
  506.5 6.0 %collective-permute-done.53 = bf16[4,144,864]{2,1,0:T(8,128)(2,1)} collective-permute-done((bf16[4,144,864]{2,1,0:T(8,128)(2,1)}, bf16[4,144,864]{2,1,0:T(8,128)(2,1)}, u32[]{:S(2)}, u32[]{:S(2)}) %collective-permute-start.53) | collective-permute-done | bytes 995360 | tf_op jit(solution)/shard_map/ppermute | solution.py:544
  521.1 3.4 copy.74.came
  524.6 3.3 grad.3
  527.9 3.3 grad.4
  531.9 3.3 grad.5
  549.3 6.8 %collective-permute-done.33.across = bf16[3,288,768]{2,1,0:T(8,128)(2,1)S(1)} collective-permute-done((bf16[3,288,768]{2,1,0:T(8,128)(2,1)}, bf16[3,288,768]{2,1,0:T(8,128)(2,1)S(1)}, u32[]{:S(2)}, u32[]{:S(2)}) %collective-permute-start.33) | collective-permute-done | bytes 1327136 | tf_op jit(solution)/shard_map/ppermute | solution.py:26
  557.2 4.4 out.1
  561.5 1.9 convert_element_type.189
  (313 shorter events, 85.3 us)
Async XLA Ops:
  7.2 182.5 %all-gather.2.cloned.1.call-start = ((), (), s32[]{:S(2)}) async-start(), calls=%async_computation.1 | async-start | bytes 2985984 | tf_op jit(solution)/shard_map/all_gather | solution.py:636
  7.3 6.0 %collective-permute-start = (bf16[144,288]{1,0:T(8,128)(2,1)}, bf16[144,288]{1,0:T(8,128)(2,1)S(1)}, u32[]{:S(2)}, u32[]{:S(2)}) collective-permute-start(bf16[144,288]{1,0:T(8,128)(2,1)} %bitcast.154), channel_id=1, source_target_pairs={{0,2},{2,0},{1,3},{3,1},{4,6},{6,4},{5,7},{7,5},{8,10},{10,8},{9,1... | collective-permute-start | bytes 248840 | tf_op jit(solution)/shard_map/ppermute | solution.py:26
  13.4 44.5 %collective-permute-start.1 = (bf16[3,288,768]{2,1,0:T(8,128)(2,1)}, bf16[3,288,768]{2,1,0:T(8,128)(2,1)S(1)}, u32[]{:S(2)}, u32[]{:S(2)}) collective-permute-start(bf16[3,288,768]{2,1,0:T(8,128)(2,1)} %prepare.2.refs_2_.refs_0_.refs_4_), channel_id=1, source_target_pairs={{0,2},{2,0},{1,3},{3,1},{4,6},{6,4},{5,7},{7,5},{8,10},{10,8},{9,1... | collective-permute-start | bytes 3981320 | tf_op jit(solution)/shard_map/ppermute | solution.py:26
  14.2 9.6 %collective-permute-start.2 = (bf16[144,864]{1,0:T(8,128)(2,1)S(1)}, bf16[144,864]{1,0:T(8,128)(2,1)S(1)}, u32[]{:S(2)}, u32[]{:S(2)}) collective-permute-start(bf16[144,864]{1,0:T(8,128)(2,1)S(1)} %pad_maximum_fusion.4.refs_1_), channel_id=1, source_target_pairs={{0,8},{4,12},{8,0},{12,4},{16,24},{20,28},{24,16},{28,20},{1,9},{5... | collective-permute-start | bytes 746504 | tf_op jit(solution)/shard_map/ppermute | solution.py:544
  14.7 25.9 %collective-permute-start.3 = (bf16[144,864]{1,0:T(8,128)(2,1)S(1)}, bf16[144,864]{1,0:T(8,128)(2,1)S(1)}, u32[]{:S(2)}, u32[]{:S(2)}) collective-permute-start(bf16[144,864]{1,0:T(8,128)(2,1)S(1)} %pad_maximum_fusion.4.refs_1_), channel_id=1, source_target_pairs={{0,16},{4,20},{8,24},{12,28},{16,0},{20,4},{24,8},{28,12},{1,17},{... | collective-permute-start | bytes 746504 | tf_op jit(solution)/shard_map/ppermute | solution.py:544
  17.3 32.8 %collective-permute-start.4 = (bf16[144,864]{1,0:T(8,128)(2,1)S(1)}, bf16[144,864]{1,0:T(8,128)(2,1)S(1)}, u32[]{:S(2)}, u32[]{:S(2)}) collective-permute-start(bf16[144,864]{1,0:T(8,128)(2,1)S(1)} %pad_maximum_fusion.4.refs_1_), channel_id=1, source_target_pairs={{0,24},{4,28},{8,16},{12,20},{16,8},{20,12},{24,0},{28,4},{1,25},{... | collective-permute-start | bytes 746504 | tf_op jit(solution)/shard_map/ppermute | solution.py:544
  17.8 543.7 %reduce-scatter.2.cloned.1.call-start = ((), (), s32[]{:S(2)}) async-start(), calls=%async_computation.2 | async-start | bytes 2985984 | tf_op jit(solution)/shard_map/reduce_scatter | solution.py:574
  52.1 42.8 %collective-permute-start.7 = (bf16[4,144,864]{2,1,0:T(8,128)(2,1)}, bf16[4,144,864]{2,1,0:T(8,128)(2,1)}, u32[]{:S(2)}, u32[]{:S(2)}) collective-permute-start(bf16[4,144,864]{2,1,0:T(8,128)(2,1)} %pad_maximum_fusion.1), channel_id=1, source_target_pairs={{0,4},{4,0},{8,12},{12,8},{16,20},{20,16},{24,28},{28,24},{1,5},{5... | collective-permute-start | bytes 2985992 | tf_op jit(solution)/shard_map/ppermute | solution.py:544
  57.9 69.7 %collective-permute-start.6 = (bf16[3,288,768]{2,1,0:T(8,128)(2,1)S(1)}, bf16[3,288,768]{2,1,0:T(8,128)(2,1)}, u32[]{:S(2)}, u32[]{:S(2)}) collective-permute-start(bf16[3,288,768]{2,1,0:T(8,128)(2,1)S(1)} %collective-permute-done.1.refs_1_), channel_id=1, source_target_pairs={{0,1},{1,0},{2,3},{3,2},{4,5},{5,4},{6,7},{7,6},{8,9},{9,8},{10,11... | collective-permute-start | bytes 3981320 | tf_op jit(solution)/shard_map/ppermute | solution.py:30
  58.0 69.6 %collective-permute-start.5 = (bf16[3,288,768]{2,1,0:T(8,128)(2,1)S(1)}, bf16[3,288,768]{2,1,0:T(8,128)(2,1)}, u32[]{:S(2)}, u32[]{:S(2)}) collective-permute-start(bf16[3,288,768]{2,1,0:T(8,128)(2,1)S(1)} %copy-done), channel_id=1, source_target_pairs={{0,1},{1,0},{2,3},{3,2},{4,5},{5,4},{6,7},{7,6},{8,9},{9,8},{10,11... | collective-permute-start | bytes 3981320 | tf_op jit(solution)/shard_map/ppermute | solution.py:30
  58.5 16.3 %collective-permute-start.11 = (bf16[144,576]{1,0:T(8,128)(2,1)S(1)}, bf16[144,576]{1,0:T(8,128)(2,1)S(1)}, u32[]{:S(2)}, u32[]{:S(2)}) collective-permute-start(bf16[144,576]{1,0:T(8,128)(2,1)S(1)} %pad_maximum_fusion.5.refs_1_), channel_id=1, source_target_pairs={{0,8},{4,12},{8,0},{12,4},{16,24},{20,28},{24,16},{28,20},{1,9},{5... | collective-permute-start | bytes 497672 | tf_op jit(solution)/shard_map/ppermute | solution.py:544
  58.6 20.0 %collective-permute-start.12 = (bf16[144,576]{1,0:T(8,128)(2,1)S(1)}, bf16[144,576]{1,0:T(8,128)(2,1)}, u32[]{:S(2)}, u32[]{:S(2)}) collective-permute-start(bf16[144,576]{1,0:T(8,128)(2,1)S(1)} %pad_maximum_fusion.5.refs_1_), channel_id=1, source_target_pairs={{0,16},{4,20},{8,24},{12,28},{16,0},{20,4},{24,8},{28,12},{1,17},{... | collective-permute-start | bytes 497672 | tf_op jit(solution)/shard_map/ppermute | solution.py:544
  74.8 18.5 %collective-permute-start.13 = (bf16[144,576]{1,0:T(8,128)(2,1)S(1)}, bf16[144,576]{1,0:T(8,128)(2,1)}, u32[]{:S(2)}, u32[]{:S(2)}) collective-permute-start(bf16[144,576]{1,0:T(8,128)(2,1)S(1)} %pad_maximum_fusion.5.refs_1_), channel_id=1, source_target_pairs={{0,24},{4,28},{8,16},{12,20},{16,8},{20,12},{24,0},{28,4},{1,25},{... | collective-permute-start | bytes 497672 | tf_op jit(solution)/shard_map/ppermute | solution.py:544
  93.3 13.2 %collective-permute-start.15 = (bf16[144,1076]{1,0:T(8,128)(2,1)S(1)}, bf16[144,1076]{1,0:T(8,128)(2,1)}, u32[]{:S(2)}, u32[]{:S(2)}) collective-permute-start(bf16[144,1076]{1,0:T(8,128)(2,1)S(1)} %bitcast.140), channel_id=1, source_target_pairs={{0,8},{4,12},{8,0},{12,4},{16,24},{20,28},{24,16},{28,20},{1,9},{5... | collective-permute-start | bytes 929672 | tf_op jit(solution)/shard_map/ppermute | solution.py:544
  93.3 24.0 %collective-permute-start.16 = (bf16[144,1076]{1,0:T(8,128)(2,1)S(1)}, bf16[144,1076]{1,0:T(8,128)(2,1)}, u32[]{:S(2)}, u32[]{:S(2)}) collective-permute-start(bf16[144,1076]{1,0:T(8,128)(2,1)S(1)} %bitcast.141), channel_id=1, source_target_pairs={{0,16},{4,20},{8,24},{12,28},{16,0},{20,4},{24,8},{28,12},{1,17},{... | collective-permute-start | bytes 929672 | tf_op jit(solution)/shard_map/ppermute | solution.py:544
  94.8 30.2 %collective-permute-start.17 = (bf16[144,1076]{1,0:T(8,128)(2,1)S(1)}, bf16[144,1076]{1,0:T(8,128)(2,1)}, u32[]{:S(2)}, u32[]{:S(2)}) collective-permute-start(bf16[144,1076]{1,0:T(8,128)(2,1)S(1)} %bitcast.142), channel_id=1, source_target_pairs={{0,24},{4,28},{8,16},{12,20},{16,8},{20,12},{24,0},{28,4},{1,25},{... | collective-permute-start | bytes 929672 | tf_op jit(solution)/shard_map/ppermute | solution.py:544
  106.4 41.6 %collective-permute-start.14 = (bf16[4,144,576]{2,1,0:T(8,128)(2,1)S(1)}, bf16[4,144,576]{2,1,0:T(8,128)(2,1)S(1)}, u32[]{:S(2)}, u32[]{:S(2)}) collective-permute-start(bf16[4,144,576]{2,1,0:T(8,128)(2,1)S(1)} %pad_maximum_fusion.3), channel_id=1, source_target_pairs={{0,4},{4,0},{8,12},{12,8},{16,20},{20,16},{24,28},{28,24},{1,5},{5... | collective-permute-start | bytes 1990664 | tf_op jit(solution)/shard_map/ppermute | solution.py:544
  117.3 49.6 %collective-permute-start.26 = (bf16[3,288,768]{2,1,0:T(8,128)(2,1)}, bf16[3,288,768]{2,1,0:T(8,128)(2,1)}, u32[]{:S(2)}, u32[]{:S(2)}) collective-permute-start(bf16[3,288,768]{2,1,0:T(8,128)(2,1)} %get-tuple-element.165.refs_0_), channel_id=1, source_target_pairs={{0,2},{2,0},{1,3},{3,1},{4,6},{6,4},{5,7},{7,5},{8,10},{10,8},{9,1... | collective-permute-start | bytes 3981320 | tf_op jit(solution)/shard_map/ppermute | solution.py:26
  148.0 29.5 %collective-permute-start.19 = (bf16[4,144,1076]{2,1,0:T(8,128)(2,1)}, bf16[4,144,1076]{2,1,0:T(8,128)(2,1)S(1)}, u32[]{:S(2)}, u32[]{:S(2)}) collective-permute-start(bf16[4,144,1076]{2,1,0:T(8,128)(2,1)} %pad_maximum_fusion), channel_id=1, source_target_pairs={{0,4},{4,0},{8,12},{12,8},{16,20},{20,16},{24,28},{28,24},{1,5},{5... | collective-permute-start | bytes 3718664 | tf_op jit(solution)/shard_map/ppermute | solution.py:544
  154.9 28.7 %collective-permute-start.18 = (bf16[1152,576]{0,1:T(8,128)(2,1)}, bf16[1152,576]{0,1:T(8,128)(2,1)S(1)}, u32[]{:S(2)}, u32[]{:S(2)}) collective-permute-start(bf16[1152,576]{0,1:T(8,128)(2,1)} %copy.65), channel_id=1, source_target_pairs={{0,1},{1,0},{2,3},{3,2},{4,5},{5,4},{6,7},{7,6},{8,9},{9,8},{10,11... | collective-permute-start | bytes 3981320 | tf_op jit(solution)/shard_map/ppermute | solution.py:30
  154.9 58.9 %collective-permute-start.27 = (bf16[3,288,768]{2,1,0:T(8,128)(2,1)}, bf16[3,288,768]{2,1,0:T(8,128)(2,1)}, u32[]{:S(2)}, u32[]{:S(2)}) collective-permute-start(bf16[3,288,768]{2,1,0:T(8,128)(2,1)} %get-tuple-element.165.refs_0_), channel_id=1, source_target_pairs={{0,1},{1,0},{2,3},{3,2},{4,5},{5,4},{6,7},{7,6},{8,9},{9,8},{10,11... | collective-permute-start | bytes 3981320 | tf_op jit(solution)/shard_map/ppermute | solution.py:30
  155.4 12.2 %collective-permute-start.23 = (bf16[288,768]{1,0:T(8,128)(2,1)S(1)}, bf16[288,768]{1,0:T(8,128)(2,1)}, u32[]{:S(2)}, u32[]{:S(2)}) collective-permute-start(bf16[288,768]{1,0:T(8,128)(2,1)S(1)} %copy-done.34), channel_id=1, source_target_pairs={{0,2},{2,0},{1,3},{3,1},{4,6},{6,4},{5,7},{7,5},{8,10},{10,8},{9,1... | collective-permute-start | bytes 1327112 | tf_op jit(solution)/shard_map/ppermute | solution.py:26
  166.9 47.0 %collective-permute-start.28 = (bf16[3,288,768]{2,1,0:T(8,128)(2,1)}, bf16[3,288,768]{2,1,0:T(8,128)(2,1)}, u32[]{:S(2)}, u32[]{:S(2)}) collective-permute-start(bf16[3,288,768]{2,1,0:T(8,128)(2,1)} %collective-permute-done.26.refs_1_), channel_id=1, source_target_pairs={{0,1},{1,0},{2,3},{3,2},{4,5},{5,4},{6,7},{7,6},{8,9},{9,8},{10,11... | collective-permute-start | bytes 3981320 | tf_op jit(solution)/shard_map/ppermute | solution.py:30
  167.7 26.9 %collective-permute-start.24 = (bf16[288,768]{1,0:T(8,128)(2,1)S(1)}, bf16[288,768]{1,0:T(8,128)(2,1)}, u32[]{:S(2)}, u32[]{:S(2)}) collective-permute-start(bf16[288,768]{1,0:T(8,128)(2,1)S(1)} %copy-done.34), channel_id=1, source_target_pairs={{0,1},{1,0},{2,3},{3,2},{4,5},{5,4},{6,7},{7,6},{8,9},{9,8},{10,11... | collective-permute-start | bytes 1327112 | tf_op jit(solution)/shard_map/ppermute | solution.py:30
  177.6 17.0 %collective-permute-start.25 = (bf16[288,768]{1,0:T(8,128)(2,1)}, bf16[288,768]{1,0:T(8,128)(2,1)}, u32[]{:S(2)}, u32[]{:S(2)}) collective-permute-start(bf16[288,768]{1,0:T(8,128)(2,1)} %collective-permute-done.23.refs_5_), channel_id=1, source_target_pairs={{0,1},{1,0},{2,3},{3,2},{4,5},{5,4},{6,7},{7,6},{8,9},{9,8},{10,11... | collective-permute-start | bytes 1327112 | tf_op jit(solution)/shard_map/ppermute | solution.py:30
  225.1 12.6 %collective-permute-start.29 = (bf16[2,288,768]{2,1,0:T(8,128)(2,1)}, bf16[2,288,768]{2,1,0:T(8,128)(2,1)S(1)}, u32[]{:S(2)}, u32[]{:S(2)}) collective-permute-start(bf16[2,288,768]{2,1,0:T(8,128)(2,1)} %get-tuple-element.172), channel_id=1, source_target_pairs={{0,1},{1,0},{2,3},{3,2},{4,5},{5,4},{6,7},{7,6},{8,9},{9,8},{10,11... | collective-permute-start | bytes 2654216 | tf_op jit(solution)/shard_map/ppermute | solution.py:30
  225.5 12.2 %collective-permute-start.20 = (bf16[288,768]{1,0:T(8,128)(2,1)S(1)}, bf16[288,768]{1,0:T(8,128)(2,1)S(1)}, u32[]{:S(2)}, u32[]{:S(2)}) collective-permute-start(bf16[288,768]{1,0:T(8,128)(2,1)S(1)} %copy-done.17), channel_id=1, source_target_pairs={{0,2},{2,0},{1,3},{3,1},{4,6},{6,4},{5,7},{7,5},{8,10},{10,8},{9,1... | collective-permute-start | bytes 1327112 | tf_op jit(solution)/shard_map/ppermute | solution.py:26
  226.9 13.8 %collective-permute-start.21 = (bf16[288,768]{1,0:T(8,128)(2,1)S(1)}, bf16[288,768]{1,0:T(8,128)(2,1)S(1)}, u32[]{:S(2)}, u32[]{:S(2)}) collective-permute-start(bf16[288,768]{1,0:T(8,128)(2,1)S(1)} %copy-done.17), channel_id=1, source_target_pairs={{0,1},{1,0},{2,3},{3,2},{4,5},{5,4},{6,7},{7,6},{8,9},{9,8},{10,11... | collective-permute-start | bytes 1327112 | tf_op jit(solution)/shard_map/ppermute | solution.py:30
  272.1 15.4 %collective-permute-start.30 = (bf16[2,288,768]{2,1,0:T(8,128)(2,1)}, bf16[2,288,768]{2,1,0:T(8,128)(2,1)}, u32[]{:S(2)}, u32[]{:S(2)}) collective-permute-start(bf16[2,288,768]{2,1,0:T(8,128)(2,1)} %get-tuple-element.179), channel_id=1, source_target_pairs={{0,1},{1,0},{2,3},{3,2},{4,5},{5,4},{6,7},{7,6},{8,9},{9,8},{10,11... | collective-permute-start | bytes 2654216 | tf_op jit(solution)/shard_map/ppermute | solution.py:30
  272.4 12.6 %collective-permute-start.8 = (bf16[288,768]{1,0:T(8,128)(2,1)}, bf16[288,768]{1,0:T(8,128)(2,1)}, u32[]{:S(2)}, u32[]{:S(2)}) collective-permute-start(bf16[288,768]{1,0:T(8,128)(2,1)} %get-tuple-element.148.refs_4_.refs_7_), channel_id=1, source_target_pairs={{0,2},{2,0},{1,3},{3,1},{4,6},{6,4},{5,7},{7,5},{8,10},{10,8},{9,1... | collective-permute-start | bytes 1327112 | tf_op jit(solution)/shard_map/ppermute | solution.py:26
  273.9 16.1 %collective-permute-start.9 = (bf16[288,768]{1,0:T(8,128)(2,1)}, bf16[288,768]{1,0:T(8,128)(2,1)}, u32[]{:S(2)}, u32[]{:S(2)}) collective-permute-start(bf16[288,768]{1,0:T(8,128)(2,1)} %get-tuple-element.148.refs_4_.refs_7_), channel_id=1, source_target_pairs={{0,1},{1,0},{2,3},{3,2},{4,5},{5,4},{6,7},{7,6},{8,9},{9,8},{10,11... | collective-permute-start | bytes 1327112 | tf_op jit(solution)/shard_map/ppermute | solution.py:30
  285.0 5.1 collective-permute-start.10
  286.0 39.3 %collective-permute-start.35 = (bf16[2,288,768]{2,1,0:T(8,128)(2,1)}, bf16[2,288,768]{2,1,0:T(8,128)(2,1)}, u32[]{:S(2)}, u32[]{:S(2)}) collective-permute-start(bf16[2,288,768]{2,1,0:T(8,128)(2,1)} %rev.16), channel_id=1, source_target_pairs={{0,2},{2,0},{1,3},{3,1},{4,6},{6,4},{5,7},{7,5},{8,10},{10,8},{9,1... | collective-permute-start | bytes 2654216 | tf_op jit(solution)/shard_map/ppermute | solution.py:26
  320.6 7.9 %collective-permute-start.31 = (bf16[2,288,768]{2,1,0:T(8,128)(2,1)}, bf16[2,288,768]{2,1,0:T(8,128)(2,1)}, u32[]{:S(2)}, u32[]{:S(2)}) collective-permute-start(bf16[2,288,768]{2,1,0:T(8,128)(2,1)} %get-tuple-element.185), channel_id=1, source_target_pairs={{0,1},{1,0},{2,3},{3,2},{4,5},{5,4},{6,7},{7,6},{8,9},{9,8},{10,11... | collective-permute-start | bytes 2654216 | tf_op jit(solution)/shard_map/ppermute | solution.py:30
  324.8 22.2 %collective-permute-start.38 = (bf16[2,288,768]{2,1,0:T(8,128)(2,1)}, bf16[2,288,768]{2,1,0:T(8,128)(2,1)}, u32[]{:S(2)}, u32[]{:S(2)}) collective-permute-start(bf16[2,288,768]{2,1,0:T(8,128)(2,1)} %rev.15), channel_id=1, source_target_pairs={{0,2},{2,0},{1,3},{3,1},{4,6},{6,4},{5,7},{7,5},{8,10},{10,8},{9,1... | collective-permute-start | bytes 2654216 | tf_op jit(solution)/shard_map/ppermute | solution.py:26
  327.6 36.0 %collective-permute-start.36 = (bf16[2,288,768]{2,1,0:T(8,128)(2,1)}, bf16[2,288,768]{2,1,0:T(8,128)(2,1)}, u32[]{:S(2)}, u32[]{:S(2)}) collective-permute-start(bf16[2,288,768]{2,1,0:T(8,128)(2,1)} %add_convert_fusion.1), channel_id=1, source_target_pairs={{0,1},{1,0},{2,3},{3,2},{4,5},{5,4},{6,7},{7,6},{8,9},{9,8},{10,11... | collective-permute-start | bytes 2654216 | tf_op jit(solution)/shard_map/ppermute | solution.py:30
  344.7 61.4 %collective-permute-start.61 = (bf16[4,144,1076]{2,1,0:T(8,128)(2,1)}, bf16[4,144,1076]{2,1,0:T(8,128)(2,1)S(1)}, u32[]{:S(2)}, u32[]{:S(2)}) collective-permute-start(bf16[4,144,1076]{2,1,0:T(8,128)(2,1)} %get-tuple-element.258), channel_id=1, source_target_pairs={{0,4},{4,0},{8,12},{12,8},{16,20},{20,16},{24,28},{28,24},{1,5},{5... | collective-permute-start | bytes 3718664 | tf_op jit(solution)/shard_map/ppermute | solution.py:544
  349.2 34.0 %collective-permute-start.39 = (bf16[2,288,768]{2,1,0:T(8,128)(2,1)}, bf16[2,288,768]{2,1,0:T(8,128)(2,1)S(1)}, u32[]{:S(2)}, u32[]{:S(2)}) collective-permute-start(bf16[2,288,768]{2,1,0:T(8,128)(2,1)} %add_convert_fusion), channel_id=1, source_target_pairs={{0,1},{1,0},{2,3},{3,2},{4,5},{5,4},{6,7},{7,6},{8,9},{9,8},{10,11... | collective-permute-start | bytes 2654216 | tf_op jit(solution)/shard_map/ppermute | solution.py:30
  362.9 40.6 %collective-permute-start.34 = (bf16[2,288,768]{2,1,0:T(8,128)(2,1)S(1)}, bf16[2,288,768]{2,1,0:T(8,128)(2,1)S(1)}, u32[]{:S(2)}, u32[]{:S(2)}) collective-permute-start(bf16[2,288,768]{2,1,0:T(8,128)(2,1)S(1)} %copy-done.29), channel_id=1, source_target_pairs={{0,2},{2,0},{1,3},{3,1},{4,6},{6,4},{5,7},{7,5},{8,10},{10,8},{9,1... | collective-permute-start | bytes 2654216 | tf_op jit(solution)/shard_map/ppermute | solution.py:26
  381.5 26.2 %collective-permute-start.45 = (bf16[2,288,768]{2,1,0:T(8,128)(2,1)}, bf16[2,288,768]{2,1,0:T(8,128)(2,1)S(1)}, u32[]{:S(2)}, u32[]{:S(2)}) collective-permute-start(bf16[2,288,768]{2,1,0:T(8,128)(2,1)} %get-tuple-element.217), channel_id=1, source_target_pairs={{0,1},{1,0},{2,3},{3,2},{4,5},{5,4},{6,7},{7,6},{8,9},{9,8},{10,11... | collective-permute-start | bytes 2654216 | tf_op jit(solution)/shard_map/ppermute | solution.py:30
  404.5 46.0 %collective-permute-start.37 = (bf16[2,288,768]{2,1,0:T(8,128)(2,1)S(1)}, bf16[2,288,768]{2,1,0:T(8,128)(2,1)S(1)}, u32[]{:S(2)}, u32[]{:S(2)}) collective-permute-start(bf16[2,288,768]{2,1,0:T(8,128)(2,1)S(1)} %add_convert_fusion.2), channel_id=1, source_target_pairs={{0,1},{1,0},{2,3},{3,2},{4,5},{5,4},{6,7},{7,6},{8,9},{9,8},{10,11... | collective-permute-start | bytes 2654216 | tf_op jit(solution)/shard_map/ppermute | solution.py:30
  404.6 5.6 collective-permute-start.48
  406.5 14.2 %collective-permute-start.62 = (bf16[144,1076]{1,0:T(8,128)(2,1)S(1)}, bf16[144,1076]{1,0:T(8,128)(2,1)S(1)}, u32[]{:S(2)}, u32[]{:S(2)}) collective-permute-start(bf16[144,1076]{1,0:T(8,128)(2,1)S(1)} %get-tuple-element.267), channel_id=1, source_target_pairs={{0,8},{4,12},{8,0},{12,4},{16,24},{20,28},{24,16},{28,20},{1,9},{5... | collective-permute-start | bytes 929672 | tf_op jit(solution)/shard_map/ppermute | solution.py:544
  406.6 19.9 %collective-permute-start.63 = (bf16[144,1076]{1,0:T(8,128)(2,1)S(1)}, bf16[144,1076]{1,0:T(8,128)(2,1)S(1)}, u32[]{:S(2)}, u32[]{:S(2)}) collective-permute-start(bf16[144,1076]{1,0:T(8,128)(2,1)S(1)} %get-tuple-element.269), channel_id=1, source_target_pairs={{0,16},{4,20},{8,24},{12,28},{16,0},{20,4},{24,8},{28,12},{1,17},{... | collective-permute-start | bytes 929672 | tf_op jit(solution)/shard_map/ppermute | solution.py:544
  407.7 41.8 %collective-permute-start.64 = (bf16[144,1076]{1,0:T(8,128)(2,1)S(1)}, bf16[144,1076]{1,0:T(8,128)(2,1)S(1)}, u32[]{:S(2)}, u32[]{:S(2)}) collective-permute-start(bf16[144,1076]{1,0:T(8,128)(2,1)S(1)} %get-tuple-element.268), channel_id=1, source_target_pairs={{0,24},{4,28},{8,16},{12,20},{16,8},{20,12},{24,0},{28,4},{1,25},{... | collective-permute-start | bytes 929672 | tf_op jit(solution)/shard_map/ppermute | solution.py:544
  410.2 89.8 %collective-permute-start.32 = (bf16[3,2,288,768]{3,2,0,1:T(8,128)(2,1)}, bf16[3,2,288,768]{3,2,0,1:T(8,128)(2,1)}, u32[]{:S(2)}, u32[]{:S(2)}) collective-permute-start(bf16[3,2,288,768]{3,2,0,1:T(8,128)(2,1)} %copy.73), channel_id=1, source_target_pairs={{0,1},{1,0},{2,3},{3,2},{4,5},{5,4},{6,7},{7,6},{8,9},{9,8},{10,11... | collective-permute-start | bytes 7962632 | tf_op jit(solution)/shard_map/ppermute | solution.py:30
  420.8 69.5 %collective-permute-start.44 = (bf16[2,288,768]{2,1,0:T(8,128)(2,1)S(1)}, bf16[2,288,768]{2,1,0:T(8,128)(2,1)S(1)}, u32[]{:S(2)}, u32[]{:S(2)}) collective-permute-start(bf16[2,288,768]{2,1,0:T(8,128)(2,1)S(1)} %copy-done.60), channel_id=1, source_target_pairs={{0,1},{1,0},{2,3},{3,2},{4,5},{5,4},{6,7},{7,6},{8,9},{9,8},{10,11... | collective-permute-start | bytes 2654216 | tf_op jit(solution)/shard_map/ppermute | solution.py:30
  476.5 22.3 %collective-permute-start.57 = (bf16[4,144,288]{2,1,0:T(8,128)(2,1)}, bf16[4,144,288]{2,1,0:T(8,128)(2,1)}, u32[]{:S(2)}, u32[]{:S(2)}) collective-permute-start(bf16[4,144,288]{2,1,0:T(8,128)(2,1)} %get-tuple-element.247), channel_id=1, source_target_pairs={{0,4},{4,0},{8,12},{12,8},{16,20},{20,16},{24,28},{28,24},{1,5},{5... | collective-permute-start | bytes 995336 | tf_op jit(solution)/shard_map/ppermute | solution.py:544
  488.8 23.6 %collective-permute-start.53 = (bf16[4,144,864]{2,1,0:T(8,128)(2,1)}, bf16[4,144,864]{2,1,0:T(8,128)(2,1)}, u32[]{:S(2)}, u32[]{:S(2)}) collective-permute-start(bf16[4,144,864]{2,1,0:T(8,128)(2,1)} %get-tuple-element.242), channel_id=1, source_target_pairs={{0,4},{4,0},{8,12},{12,8},{16,20},{20,16},{24,28},{28,24},{1,5},{5... | collective-permute-start | bytes 2985992 | tf_op jit(solution)/shard_map/ppermute | solution.py:544
  492.2 5.3 collective-permute-start.43
  496.1 22.7 %collective-permute-start.46 = (bf16[2,288,768]{2,1,0:T(8,128)(2,1)}, bf16[2,288,768]{2,1,0:T(8,128)(2,1)S(1)}, u32[]{:S(2)}, u32[]{:S(2)}) collective-permute-start(bf16[2,288,768]{2,1,0:T(8,128)(2,1)} %pad_maximum_fusion.2), channel_id=1, source_target_pairs={{0,2},{2,0},{1,3},{3,1},{4,6},{6,4},{5,7},{7,5},{8,10},{10,8},{9,1... | collective-permute-start | bytes 2654216 | tf_op jit(solution)/shard_map/ppermute | solution.py:26
  497.4 6.4 %collective-permute-start.40 = (bf16[2,288,768]{2,1,0:T(8,128)(2,1)}, bf16[2,288,768]{2,1,0:T(8,128)(2,1)S(1)}, u32[]{:S(2)}, u32[]{:S(2)}) collective-permute-start(bf16[2,288,768]{2,1,0:T(8,128)(2,1)} %get-tuple-element.209), channel_id=1, source_target_pairs={{0,1},{1,0},{2,3},{3,2},{4,5},{5,4},{6,7},{7,6},{8,9},{9,8},{10,11... | collective-permute-start | bytes 2654216 | tf_op jit(solution)/shard_map/ppermute | solution.py:30
  500.0 15.7 %collective-permute-start.58 = (bf16[144,288]{1,0:T(8,128)(2,1)S(1)}, bf16[144,288]{1,0:T(8,128)(2,1)S(1)}, u32[]{:S(2)}, u32[]{:S(2)}) collective-permute-start(bf16[144,288]{1,0:T(8,128)(2,1)S(1)} %get-tuple-element.276), channel_id=1, source_target_pairs={{0,8},{4,12},{8,0},{12,4},{16,24},{20,28},{24,16},{28,20},{1,9},{5... | collective-permute-start | bytes 248840 | tf_op jit(solution)/shard_map/ppermute | solution.py:544
  500.0 16.9 %collective-permute-start.59 = (bf16[144,288]{1,0:T(8,128)(2,1)S(1)}, bf16[144,288]{1,0:T(8,128)(2,1)S(1)}, u32[]{:S(2)}, u32[]{:S(2)}) collective-permute-start(bf16[144,288]{1,0:T(8,128)(2,1)S(1)} %get-tuple-element.278), channel_id=1, source_target_pairs={{0,16},{4,20},{8,24},{12,28},{16,0},{20,4},{24,8},{28,12},{1,17},{... | collective-permute-start | bytes 248840 | tf_op jit(solution)/shard_map/ppermute | solution.py:544
  503.9 13.0 %collective-permute-start.60 = (bf16[144,288]{1,0:T(8,128)(2,1)S(1)}, bf16[144,288]{1,0:T(8,128)(2,1)S(1)}, u32[]{:S(2)}, u32[]{:S(2)}) collective-permute-start(bf16[144,288]{1,0:T(8,128)(2,1)S(1)} %get-tuple-element.277), channel_id=1, source_target_pairs={{0,24},{4,28},{8,16},{12,20},{16,8},{20,12},{24,0},{28,4},{1,25},{... | collective-permute-start | bytes 248840 | tf_op jit(solution)/shard_map/ppermute | solution.py:544
  512.5 18.7 %collective-permute-start.41 = (bf16[1,288,768]{2,1,0:T(8,128)(2,1)S(1)}, bf16[1,288,768]{2,1,0:T(8,128)(2,1)S(1)}, u32[]{:S(2)}, u32[]{:S(2)}) collective-permute-start(bf16[1,288,768]{2,1,0:T(8,128)(2,1)S(1)} %fusion.11), channel_id=1, source_target_pairs={{0,2},{2,0},{1,3},{3,1},{4,6},{6,4},{5,7},{7,5},{8,10},{10,8},{9,1... | collective-permute-start | bytes 1327112 | tf_op jit(solution)/shard_map/ppermute | solution.py:26
  515.7 40.3 %collective-permute-start.33 = (bf16[3,288,768]{2,1,0:T(8,128)(2,1)}, bf16[3,288,768]{2,1,0:T(8,128)(2,1)S(1)}, u32[]{:S(2)}, u32[]{:S(2)}) collective-permute-start(bf16[3,288,768]{2,1,0:T(8,128)(2,1)} %fusion), channel_id=1, source_target_pairs={{0,2},{2,0},{1,3},{3,1},{4,6},{6,4},{5,7},{7,5},{8,10},{10,8},{9,1... | collective-permute-start | bytes 3981320 | tf_op jit(solution)/shard_map/ppermute | solution.py:26
  516.9 22.2 %collective-permute-start.54 = (bf16[144,864]{1,0:T(8,128)(2,1)}, bf16[144,864]{1,0:T(8,128)(2,1)}, u32[]{:S(2)}, u32[]{:S(2)}) collective-permute-start(bf16[144,864]{1,0:T(8,128)(2,1)} %get-tuple-element.270), channel_id=1, source_target_pairs={{0,8},{4,12},{8,0},{12,4},{16,24},{20,28},{24,16},{28,20},{1,9},{5... | collective-permute-start | bytes 746504 | tf_op jit(solution)/shard_map/ppermute | solution.py:544
  516.9 22.2 %collective-permute-start.55 = (bf16[144,864]{1,0:T(8,128)(2,1)}, bf16[144,864]{1,0:T(8,128)(2,1)}, u32[]{:S(2)}, u32[]{:S(2)}) collective-permute-start(bf16[144,864]{1,0:T(8,128)(2,1)} %get-tuple-element.272), channel_id=1, source_target_pairs={{0,16},{4,20},{8,24},{12,28},{16,0},{20,4},{24,8},{28,12},{1,17},{... | collective-permute-start | bytes 746504 | tf_op jit(solution)/shard_map/ppermute | solution.py:544
  518.8 21.4 %collective-permute-start.56 = (bf16[144,864]{1,0:T(8,128)(2,1)}, bf16[144,864]{1,0:T(8,128)(2,1)}, u32[]{:S(2)}, u32[]{:S(2)}) collective-permute-start(bf16[144,864]{1,0:T(8,128)(2,1)} %get-tuple-element.271), channel_id=1, source_target_pairs={{0,24},{4,28},{8,16},{12,20},{16,8},{20,12},{24,0},{28,4},{1,25},{... | collective-permute-start | bytes 746504 | tf_op jit(solution)/shard_map/ppermute | solution.py:544
  538.4 3.8 collective-permute-start.49
  542.2 4.5 collective-permute-start.50
  543.2 4.6 collective-permute-start.51
  544.1 3.9 collective-permute-start.52
  (66 other events, 810.6 us)
Sparse Core Ops, SparseCore 0:
  17.9 75.0 all-gather.1
  361.9 86.7 reduce-scatter.1

commit v2 on v1

--- a/solution.py
+++ b/solution.py
@@ -83,6 +83,19 @@
         out[i, :, :seq] = (x[i].astype(F32) * live[i]).astype(LOW)
         total = total + dot_nt(jnp.ones((8, out.shape[2]), LOW), out[i])
     sums[...] = total
+
+
+def place_pair_kernel(pos, *refs):
+    count = len(refs) - 4
+    far, first, second, turned = refs[count:]
+    cut = first.shape[2]
+    for m in range(count):
+        first[pos[2 * m]] = refs[m][:, :cut]
+        first[pos[2 * m + 1]] = far[m, :, :cut]
+        second[pos[2 * m]] = refs[m][:, cut:]
+        second[pos[2 * m + 1]] = far[m, :, cut:]
+    rows = second.shape[0] * second.shape[1]
+    turned[...] = second[...].reshape(rows, second.shape[2]).T
 
 
 def place_kernel(pos, *refs):
@@ -266,16 +279,53 @@
     out[0] = total.astype(LOW)
 
 
-def weight_split_kernel(count, *refs):
-    odd, a, b = refs[1][0] == 1, refs[2 : count + 2], refs[count + 2 : 2 * count + 2]
+def row_sum(pairs, start):
+    total = None if start is None else start[...]
+    for a, b in pairs:
+        part = dot_nt(a[...], b[...])
+        total = part if total is None else total + part
+    return total
+
+
+def weight_part_kernel(count, *refs):
+    refs[-1][...] = row_sum(list(zip(refs[:count], refs[count : 2 * count])), None)
+
+
+def weight_split_kernel(counts, starts, *refs):
+    odd, refs = refs[1][0] == 1, list(refs[2:])
     keep, send = refs[-2:]
-    total = dot_nt(a[0][...], b[0][...])
-    for i in range(1, count):
-        total = total + dot_nt(a[i][...], b[i][...])
-    half = total.shape[0] // 2
-    top, low = total[:half], total[half:]
-    keep[0] = jnp.where(odd, low, top)
-    send[0] = jnp.where(odd, top, low).astype(LOW)
+    at = 0
+    for count, start in zip(counts, starts):
+        pairs = list(zip(refs[:count], refs[count : 2 * count]))
+        total = row_sum(pairs, refs[2 * count] if start else None)
+        refs = refs[2 * count + start :]
+        half = total.shape[0] // 2
+        top, low = total[:half], total[half:]
+        to = at + total.shape[1]
+        keep[0, :, at:to] = jnp.where(odd, low, top)
+        send[0, :, at:to] = jnp.where(odd, top, low).astype(LOW)
+        at = to
+
+
+TIMES = {
+    "prepare": 2.6,
+    "place": 4.0,
+    "join": 4.0,
+    "attn_fwd": 10.0,
+    "mlp_fwd": 19.5,
+    "mlp_bwd": 11.0,
+    "attn_bwd": 17.7,
+    "weight_grad": 12.4,
+    "weight_part": 7.0,
+    "grad": 3.3,
+}
+RATE = 2e8
+
+
+def cost(name):
+    return pl.CostEstimate(
+        flops=int(TIMES[name] * RATE), bytes_accessed=0, transcendentals=0
+    )
 
 
 def shaped(*dims, dtype=LOW):
@@ -320,7 +370,7 @@
         input_output_aliases={used + j: o for j, o in enumerate(buffers)},
         scratch_shapes=scratch,
         compiler_params=pltpu.CompilerParams(vmem_limit_bytes=VMEM_LIMIT),
-        cost_estimate=pl.CostEstimate(flops=flops, bytes_accessed=moved, transcendentals=0),
+        cost_estimate=cost(name),
         name=name,
     )(*arrays, *buffers.values(), *after)
 
@@ -449,10 +499,24 @@
     return placed.reshape(count * rows, hidden), turned
 
 
-def join(near, far):
+def place_pair(near, far, cut, pos):
+    count = 2 * len(near)
+    rows, hidden = near[0].shape
+    outs = [
+        shaped(count, rows, cut),
+        shaped(count, rows, hidden - cut),
+        shaped(hidden - cut, count * rows),
+    ]
+    first, second, turned = run(
+        place_pair_kernel, outs, [pos, *near, far], "place", 10**6, scalars=1
+    )
+    return first.reshape(count * rows, cut), second.reshape(count * rows, hidden - cut), turned
+
+
+def join(near, far, after=()):
     rows, half = near.shape
     outs = [shaped(rows, 2 * half), shaped(half // 2, rows)]
-    return run(join_kernel, outs, [near, far], "join", 10**6)
+    return run(join_kernel, outs, [near, far], "join", 10**6, after=after)
 
 
 def weight_grad(a, b, order, after=()):
@@ -475,42 +539,68 @@
             out_specs=pl.BlockSpec((1, share, hidden), lambda r, order: (order[r], 0, 0)),
         ),
         compiler_params=pltpu.CompilerParams(vmem_limit_bytes=VMEM_LIMIT),
-        cost_estimate=pl.CostEstimate(
-            flops=2 * slots * width * hidden * count, bytes_accessed=moved, transcendentals=0
-        ),
+        cost_estimate=cost("weight_grad"),
         name="weight_grad",
     )(order, *a, *b, *after)
     return out.reshape(width, hidden)
 
 
-def weight_split(a, b, order, odd, after=()):
+def weight_part(a, b, after=()):
     width, count = a[0].shape
     share, hidden = width // 4, b[0].shape[0]
-    slots = len(a)
-    outs = [shaped(4, share // 2, hidden, dtype=F32), shaped(4, share // 2, hidden)]
-    moved = sum(math.prod(v.shape) * 2 for v in [*a, *b, *outs])
     return pl.pallas_call(
-        lambda *refs: weight_split_kernel(slots, *refs),
+        lambda *refs: weight_part_kernel(len(a), *refs),
+        out_shape=shaped(width, hidden, dtype=F32),
+        grid=(4,),
+        in_specs=[
+            *[pl.BlockSpec((share, count), lambda r: (r, 0)) for _ in a],
+            *[pl.BlockSpec((hidden, count), lambda r: (0, 0)) for _ in b],
+            *[LEFT] * len(after),
+        ],
+        out_specs=pl.BlockSpec((share, hidden), lambda r: (r, 0)),
+        compiler_params=pltpu.CompilerParams(vmem_limit_bytes=VMEM_LIMIT),
+        cost_estimate=cost("weight_part"),
+        name="weight_part",
+    )(*a, *b, *after)
+
+
+def weight_split(groups, order, odd, after=()):
+    width, count = groups[0][0][0].shape
+    share = width // 4
+    args, specs, total = [], [], 0
+    for a, b, start in groups:
+        hidden = b[0].shape[0]
+        args += [*a, *b]
+        specs += [pl.BlockSpec((share, count), lambda r, order, odd: (r, 0)) for _ in a]
+        specs += [pl.BlockSpec((hidden, count), lambda r, order, odd: (0, 0)) for _ in b]
+        if start is not None:
+            args.append(start)
+            specs.append(pl.BlockSpec((share, hidden), lambda r, order, odd: (r, 0)))
+        total += hidden
+    outs = [shaped(4, share // 2, total, dtype=F32), shaped(4, share // 2, total)]
+    counts = [len(g[0]) for g in groups]
+    starts = [int(g[2] is not None) for g in groups]
+    used = len(args) + 2
+
+    def body(*refs):
+        weight_split_kernel(counts, starts, *refs[:used], *refs[used + len(after) :])
+
+    return pl.pallas_call(
+        body,
         out_shape=outs,
         grid_spec=pltpu.PrefetchScalarGridSpec(
             num_scalar_prefetch=2,
             grid=(4,),
-            in_specs=[
-                *[pl.BlockSpec((share, count), lambda r, order, odd: (r, 0)) for _ in a],
-                *[pl.BlockSpec((hidden, count), lambda r, order, odd: (0, 0)) for _ in b],
-                *[pl.BlockSpec(memory_space=pl.ANY)] * len(after),
-            ],
+            in_specs=[*specs, *[LEFT] * len(after)],
             out_specs=[
-                pl.BlockSpec((1, share // 2, hidden), lambda r, order, odd: (order[r], 0, 0))
+                pl.BlockSpec((1, share // 2, total), lambda r, order, odd: (order[r], 0, 0))
             ]
             * 2,
         ),
         compiler_params=pltpu.CompilerParams(vmem_limit_bytes=VMEM_LIMIT),
-        cost_estimate=pl.CostEstimate(
-            flops=2 * slots * width * hidden * count, bytes_accessed=moved, transcendentals=0
-        ),
+        cost_estimate=cost("weight_grad"),
         name="weight_grad",
-    )(order, odd, *a, *b, *after)
+    )(order, odd, *args, *after)
 
 
 def place_blocks_kernel(order, value, out, turned):
@@ -520,7 +610,7 @@
     turned[...] = out[...].reshape(rows, out.shape[2]).T
 
 
-def place_blocks(value, t):
+def place_blocks(value, t, after=()):
     rows, hidden = value.shape
     order = jnp.stack([t ^ m for m in (0, 2, 1, 3)]).astype(jnp.int32)
     placed, turned = run(
@@ -530,13 +620,23 @@
         "place",
         10**6,
         scalars=1,
+        after=after,
     )
     return placed.reshape(rows, hidden), turned
 
 
 def gate(values, after):
-    values, _ = lax.optimization_barrier((list(values), list(after)))
-    return values
+    values, after = list(values), list(after)
+    left = pl.BlockSpec(memory_space=pl.ANY)
+    return pl.pallas_call(
+        lambda *refs: None,
+        out_shape=[jax.ShapeDtypeStruct(v.shape, v.dtype) for v in values],
+        in_specs=[left] * (len(values) + len(after)),
+        out_specs=[left] * len(values),
+        input_output_aliases={i: i for i in range(len(values))},
+        cost_estimate=pl.CostEstimate(flops=0, bytes_accessed=0, transcendentals=0),
+        name="gate",
+    )(*values, *after)
 
 
 def dp_swap(value, mask):
@@ -557,28 +657,53 @@
     return [shard, *[dp_swap(shard, m) for m in (2, 4, 6)]]
 
 
-def gather_second(near, far, t):
+def shard_order(t):
     pos = []
     for m in range(8):
         k = lax.axis_index("dp") ^ m
         b = t ^ (k >> 1)
         pos.append((((b & 1) << 1) | (b >> 1)) * 2 + (k & 1))
-    return place(near, far, jnp.stack(pos).astype(jnp.int32))
-
-
-def scatter_dp(a, b, t, direct, after=()):
-    size = lax.axis_size("dp")
+    return jnp.stack(pos).astype(jnp.int32)
+
+
+def gather_second(near, far, t):
+    return place(near, far, shard_order(t))
+
+
+def gather_pair(near, far, cut, t):
+    return place_pair(near, far, cut, shard_order(t))
+
+
+def weight_whole(a, b, t, after=()):
     order = jnp.stack([t ^ m for m in (0, 2, 1, 3)]).astype(jnp.int32)
-    if size != 8 or not direct:
-        value = weight_grad(a, b, order, after)
-        return lax.psum_scatter(value, "dp", scatter_dimension=0, tiled=True).astype(F32)
+    return weight_grad(a, b, order, after)
+
+
+def scatter_rows(value):
+    return lax.psum_scatter(value, "dp", scatter_dimension=0, tiled=True).astype(F32)
+
+
+def scatter_whole(a, b, t, after=()):
+    return scatter_rows(weight_whole(a, b, t, after))
+
+
+def scatter_split(groups, t, after=()):
+    order = jnp.stack([t ^ m for m in (0, 2, 1, 3)]).astype(jnp.int32)
     me = lax.axis_index("dp")
-    keep, send = weight_split(a, b, order ^ (me >> 1), (me & 1).reshape(1).astype(jnp.int32), after)
-    total = keep + dp_swap(send, 1).astype(F32)
-    out = total[0]
-    for j in (1, 2, 3):
-        out = out + dp_swap(total[j].astype(LOW), 2 * j).astype(F32)
-    return out
+    return weight_split(groups, order ^ (me >> 1), (me & 1).reshape(1).astype(jnp.int32), after)
+
+
+def scatter_first(keep, came):
+    total = keep + came.astype(F32)
+    return total[0], [total[j].astype(LOW) for j in (1, 2, 3)]
+
+
+def scatter_second(sends):
+    return [dp_swap(send, 2 * j) for j, send in zip((1, 2, 3), sends)]
+
+
+def scatter_last(own, came):
+    return own + came[0].astype(F32) + came[1].astype(F32) + came[2].astype(F32)
 
 
 def sum_dp(value):
@@ -631,52 +756,82 @@
     qkv_shard = jnp.concatenate([query_weight, key_weight, value_weight], axis=1)
     out_t = output_weight.T
     out_shard = jnp.concatenate([out_t, y_swap(out_t)], axis=1)
+    up_value = lax.all_gather(up_weight, "dp", axis=0, tiled=True)
     x_own = prepare(images, columns([output_bias]), count)
-    x_across = y_swap(*gate([x_own], [out_shard]))
-    up_value = lax.all_gather(up_weight, "dp", axis=0, tiled=True)
-    cot_own, cot_sums = prepare_grad(cotangent, live, count, [x_own])
+    x_send, qkv_shard = gate([x_own, qkv_shard], [out_shard])
+    x_far, x_across = core_swap(x_send), y_swap(x_send)
     if fast:
-        near = gather_first(*gate([qkv_shard], [x_own]))
-        near_stack, out_shard = gate([jnp.stack(near), out_shard], near[1:])
+        near = gather_first(qkv_shard)
+        cot_own, cot_sums = prepare_grad(cotangent, live, count, [x_own])
+        out_shard = jnp.concatenate([out_shard, down_weight.T], axis=1)
+        *near[1:], out_shard = gate([*near[1:], out_shard], [x_far, cot_sums])
+        near_stack = jnp.stack(near)
         far = dp_swap(near_stack, 1)
         out_near = gather_first(out_shard)
-        x_across, x_own2, cot_send = gate([x_across, x_own, cot_own], near[1:])
-        (down_shard, cot_send) = gate([down_weight.T, cot_send], [*out_near[1:], x_across])
-        down_near = gather_first(down_shard)
+        (x_across,) = gate([x_across], [near_stack])
+        x_wide = core_swap(x_across)
+        (cot_send,) = gate([cot_own], [x_wide])
+        cot_across = y_swap(cot_send)
         qkv_w, qkv_t = gather_second(near, far, t)
     else:
-        x_own2, cot_send = x_own, cot_own
+        x_wide = core_swap(x_across)
+        cot_own, cot_sums = prepare_grad(cotangent, live, count, [x_own])
+        cot_across = y_swap(cot_own)
         qkv_w, qkv_t = gather_dp_whole(qkv_shard, t)
-    cot_across = y_swap(cot_send)
-    x = [x_own, x_across, core_swap(x_own2), core_swap(x_across)]
-    fwd, mixes = [], []
-    for i in range(slots):
-        after = [fwd[i - 1][4]] if i else [cot_sums]
-        if i == 0 and fast:
-            (out_stack,) = gate([jnp.stack(out_near)], [far])
-            out_far = dp_swap(out_stack, 1)
-        if i == 2 and fast:
-            out_far, down_stack = gate([out_far, jnp.stack(down_near)], after)
-            down_far = dp_swap(down_stack, 1)
-        fwd.append(attn_fwd(x, i, vec, qkv_t, qkv_bias, seq, after))
-        mixes.append([fwd[i][2], y_swap(fwd[i][2])])
-    if fast:
-        (o_half, _) = gather_second(out_near, out_far, t)
-        down_t, down_w = gather_second(down_near, down_far, t)
-        up_w, up_t = place_blocks(up_value, t)
-    else:
         o_half, _ = gather_dp_whole(out_shard, t)
         down_t, down_w = gather_dp_whole(down_weight.T, t)
         up_w, up_t = gather_dp_whole(up_weight, t)
+    x = [x_own, x_across, x_far, x_wide]
+
+    def forward(i, after):
+        fwd.append(attn_fwd(x, i, vec, qkv_t, qkv_bias, seq, after))
+        mixes.append([fwd[i][2], y_swap(fwd[i][2])])
+
+    def widen(i):
+        mixes[i].extend([core_swap(mixes[i][0]), core_swap(mixes[i][1])])
+
+    fwd, mixes = [], []
+    forward(0, [cot_sums])
+    if fast:
+        out_near[1:] = gate(out_near[1:], [fwd[0][4]])
+        out_stack = jnp.stack(out_near)
+        out_far = dp_swap(out_stack, 1)
+        forward(1, [fwd[0][4], out_stack])
+    else:
+        forward(1, [fwd[0][4]])
+    (cot_across,) = gate([cot_across], [fwd[1][4]])
+    cot_far, cot_wide = core_swap(cot_own), core_swap(cot_across)
+    forward(2, [fwd[1][4], cot_far])
+    mixes[0][1], mixes[1][1] = gate([mixes[0][1], mixes[1][1]], [fwd[2][4], cot_wide])
+    widen(0)
+    widen(1)
+    if fast:
+        up_w, up_t = place_blocks(up_value, t, [cot_far, cot_wide])
+    widen(2)
+    if fast:
+        (out_far,) = gate([out_far], [v for m in mixes for v in m])
+        o_half, down_t, down_w = gather_pair(out_near, out_far, 2 * share, t)
     o_full, o_mine = join(o_half, core_swap(o_half))
-    for m in mixes:
-        m.extend([core_swap(m[0]), core_swap(m[1])])
-    (cot_across,) = gate([cot_across], [fwd[-1][2]])
-    cot = [cot_own, cot_across, core_swap(cot_own), core_swap(cot_across)]
-
-    mlp, back, ends = [], [], []
-    norm2_grad = []
-    last = [fwd[-1][4]]
+    cot = [cot_own, cot_across, cot_far, cot_wide]
+
+    mlp, back, ends, norm2_grad = [], [], [], []
+
+    def mlp_forward(i, after):
+        buffers = {j: mlp[i - 1][j] for j in (4, 6, 7)} if i else {}
+        mlp.append(mlp_fwd(x, mixes[i], i, vec, o_full, up_t, up_b, down_t, seq, buffers, after))
+
+    def mlp_back(i, after):
+        back.append(mlp_bwd(cot, i, mlp[i][3], down_w, up_w, after))
+        half = back[i][2] + core_swap(back[i][3]).astype(F32)
+        send = half[::-1].astype(LOW)
+        norm2_grad.append([half, y_swap(send)])
+        return send
+
+    def norm2_wide(i):
+        half, across = norm2_grad[i]
+        both = (half + across.astype(F32)).astype(LOW)
+        norm2_grad[i].append(core_swap(both))
+        return both
 
     def attention_back(i, after):
         attn_in, qkv, _, stats1, lse = fwd[i]
@@ -688,51 +843,88 @@
             )
         )
 
+    mlp_forward(0, [])
+    send = mlp_back(0, [mlp[0][5]])
+    mlp_forward(1, [send])
+    norm2_grad[0][1], *_ = gate([norm2_grad[0][1]], [mlp[1][5]])
+    both = norm2_wide(0)
+    send = mlp_back(1, [both])
+    mlp_forward(2, [send, norm2_grad[0][2]])
+    norm2_grad[1][1], mlp_send = gate([norm2_grad[1][1], mlp[2][7]], [mlp[2][5]])
+    both = norm2_wide(1)
+    mlp_came = core_swap(mlp_send)
+    send = mlp_back(2, [both])
+    base, keep = mlp[2][4], mlp[2][6]
+    (mlp_came,) = gate([mlp_came], [send])
+    out_send = (keep + mlp_came[:, 1].astype(F32)).astype(LOW)
+
+    up_rows = weight_whole(
+        [m[0] for m in mlp], [b[1] for b in back], t, [send, norm2_grad[1][2], out_send]
+    )
+    up_grad = scatter_rows(up_rows)
+    terms = [b[0] for b in back], [m[2] for m in mlp]
+    if fast:
+        down_keep, last = scatter_split([(*terms, None)], t, [up_rows])
+        down_x = dp_swap(last, 1)
+    else:
+        last = weight_whole(*terms, t, [up_rows])
+        down_grad = scatter_rows(last)
+    norm2_grad[2][1], out_send = gate([norm2_grad[2][1], out_send], [last])
+    both = norm2_wide(2)
+    (out_send,) = gate([out_send], [both])
+    out_across = y_swap(out_send)
+    attention_back(0, [both, last])
+    came = [core_swap(ends[0][5])]
+    attention_back(1, [ends[0][-1], norm2_grad[2][2]])
+    if fast:
+        (down_x,) = gate([down_x], [ends[1][-1]])
+        down_own, down_sends = scatter_first(down_keep, down_x)
+        down_came = scatter_second(down_sends)
+    came.append(core_swap(*gate([ends[1][5]], [came[0], out_across])))
+    send = jnp.stack([(ends[i][4] + came[i][1].astype(F32)).astype(LOW) for i in (0, 1)])
+    across = [y_swap(send)]
+    qkv_part = weight_part([f[0] for f in fwd[:2]], [e[2] for e in ends], [send])
+    out_part = weight_part([e[0] for e in ends], [f[2] for f in fwd[:2]], [send])
+    attention_back(2, [qkv_part, out_part, up_grad])
+    e = ends[2]
+    stats = jnp.concatenate([v[6] for v in ends])
+    if fast:
+        keep_a, send_a = scatter_split([([fwd[2][0]], [e[2]], qkv_part)], t, [e[-1]])
+        x_a = dp_swap(send_a, 1)
+        part, stats, *down_came = gate([e[5], stats, *down_came], [send_a])
+        down_grad = scatter_last(down_own, down_came)
+    else:
+        qkv_grad = scatter_whole([f[0] for f in fwd], [v[2] for v in ends], t)
+        out_grad = scatter_whole([v[0] for v in ends], [f[2] for f in fwd], t)
+        part = e[5]
+    came_last = core_swap(part)
+    came.append(came_last)
+    send = (e[4] + came_last[1].astype(F32)).astype(LOW)[None]
+    stats = stats + core_swap(stats)
+    across.append(y_swap(send))
+    stats = stats + y_swap(stats)
+    if fast:
+        keep_b, send_b = scatter_split([([e[0]], [fwd[2][2]], out_part)], t, [send])
+        x_b = dp_swap(send_b, 1)
+        (out_across,) = gate([out_across], [send_b])
+        own_a, sends_a = scatter_first(keep_a, x_a)
+        came_a = scatter_second(sends_a)
+        *came_a, x_b = gate([*came_a, x_b], [send_b])
+        own_b, sends_b = scatter_first(keep_b, x_b)
+        came_b = scatter_second(sends_b)
+        qkv_grad = scatter_last(own_a, came_a)
+        out_grad = scatter_last(own_b, came_b)
+    out_buffer = finish_out(live, base, mlp_came, out_across, seq)
+    grad_buffer, sums = None, None
     for i in range(slots):
-        buffers = {j: mlp[i - 1][j] for j in (4, 6, 7)} if i else {}
-        mlp.append(mlp_fwd(x, mixes[i], i, vec, o_full, up_t, up_b, down_t, seq, buffers, last))
-        if i:
-            half, across = norm2_grad[i - 1]
-            both = (half + across.astype(F32)).astype(LOW)
-            (both,) = gate([both], [mlp[i][5]])
-            norm2_grad[i - 1] = (half, across, core_swap(both))
-        back.append(mlp_bwd(cot, i, mlp[i][3], down_w, up_w, [mlp[i][5]]))
-        half = back[i][2] + core_swap(back[i][3]).astype(F32)
-        norm2_grad.append((half, y_swap(half[::-1].astype(LOW))))
-        last = [half]
-    down_grad = scatter_dp([b[0] for b in back], [m[2] for m in mlp], t, True, last).T
-    base, keep, send = (mlp[-1][j] for j in (4, 6, 7))
-    came = core_swap(*gate([send], last))
-    across = y_swap((keep + came[:, 1].astype(F32)).astype(LOW))
-    out_buffer = finish_out(live, base, came, across, seq)
-    up_grad = scatter_dp([m[0] for m in mlp], [b[1] for b in back], t, False, last)
-    for i in range(slots):
-        attention_back(i, last)
-        last = [ends[i][-1]]
-        if i == 0:
-            half, across = norm2_grad[-1]
-            both = (half + across.astype(F32)).astype(LOW)
-            (both,) = gate([both], last)
-            norm2_grad[-1] = (half, across, core_swap(both))
-    mixed_rows = [f[2] for f in fwd]
-    qkv_grad = scatter_dp([f[0] for f in fwd], [e[2] for e in ends], t, True)
-    out_grad = scatter_dp([e[0] for e in ends], mixed_rows, t, True).T
-    grad_buffer, sums = None, None
-    for group in (list(range(slots - 1)), [slots - 1]):
-        came = [core_swap(ends[i][5]) for i in group]
-        across = y_swap(
-            jnp.stack([(ends[i][4] + c[1].astype(F32)).astype(LOW) for i, c in zip(group, came)])
+        grad_buffer, grad_sums = finish_grad(
+            [ends[i][1], ends[i][3], came[i], (across[i // 2], i % 2), (x_own, i), fwd[i][3],
+             stats[8 * i : 8 * i + 8], vec_own],
+            i, grad_buffer, slots, seq,
         )
-        stats = jnp.stack([ends[i][6] for i in group])
-        stats = stats + core_swap(stats)
-        stats = stats + y_swap(stats)
-        for j, i in enumerate(group):
-            grad_buffer, grad_sums = finish_grad(
-                [ends[i][1], ends[i][3], came[j], (across, j), (x_own, i), fwd[i][3], (stats, j), vec_own],
-                i, grad_buffer, slots, seq,
-            )
-            now = (grad_sums, ends[i][7], ends[i][8], back[i][-1])
-            sums = now if sums is None else jax.tree.map(jnp.add, sums, now)
+        now = (grad_sums, ends[i][7], ends[i][8], back[i][-1])
+        sums = now if sums is None else jax.tree.map(jnp.add, sums, now)
+    down_grad, out_grad = down_grad.T, out_grad.T
     sums = (*sums, cot_sums)
     sizes = [2 * share, 3 * share, 3 * share, up_bias.shape[0], share]
     small = jnp.concatenate(
@@ -744,6 +936,8 @@
             sums[4][0],
         ]
     )
+    if fast:
+        (small,) = gate([small], [x_b])
     small = sum_dp(small)
     parts, at = [], 0
     for size in sizes:

time: 581 us -> 563 us (0.969)
  waiting for transfers between devices: 167 us -> 133 us
  local copies, waits for them, and re-layouts: 36.7 us -> 46.4 us
  other arithmetic: 38.6 us -> 46.3 us
  Pallas kernels: 259 us -> 265 us
    ppermute x28 -> x24, waiting for transfers between devices: 136 us -> 99 us  [dp_swap(): return lax.ppermute(value, 'dp', [(i, i ^ mask) for i in range(size)])]
    unnamed x126 -> x140, local copies, waits for them, and re-layouts: 7.65 us -> 23.9 us
    ppermute x23 -> x22, waiting for transfers between devices: 0.06 us -> 10.9 us  [core_swap(): return lax.ppermute(value, 'tensor', CORE_SWAP)]
    pallas_call x3 -> x24, Pallas kernels: 30.9 us -> 39.4 us  [the longest x3 25.8 us: weight_split(): pl.pallas_call(body, out_shape=outs, grid_spec=pltpu.PrefetchScalarGridSp...]
    ppermute x14 -> x13, waiting for transfers between devices: 30.8 us -> 22.9 us  [y_swap(): return lax.ppermute(value, 'tensor', Y_SWAP)]
    another operation x11 -> x8, other arithmetic: 9.75 us -> 15.6 us
    ppermute x28 -> x24, starting transfers between devices: 33.8 us -> 29.9 us  [dp_swap(): return lax.ppermute(value, 'dp', [(i, i ^ mask) for i in range(size)])]
    pallas_call x22 -> x21, Pallas kernels: 212 us -> 209 us  [run(): pl.pallas_call(body, grid=(1,), out_shape=tuple(shapes), in_specs=[*[SCAL...]
  transfers between devices with their start and end apart: 67 -> 61, of which waited for: 24 -> 26; matrix products, arithmetic and copies ran while one was open for 12% -> 12% of each run, Pallas kernels for 38% -> 39%
where the time goes in v2:
time: 563 us; the launch traced here: 555 us
  Pallas kernels  265 us (47%)
  waiting for transfers between devices  133 us (24%)
  starting transfers between devices  48.5 us (9%)
  local copies, waits for them, and re-layouts  46.4 us (8%)
  other arithmetic  46.3 us (8%)
  between operations  15.6 us (3%)
    pallas_call x21, Pallas kernels, run(): pl.pallas_call(body, grid=(1,), out_shape=tuple(shapes), in_specs=[*[SCAL...  209 us
    ppermute x24, waiting for transfers between devices, dp_swap(): return lax.ppermute(value, 'dp', [(i, i ^ mask) for i in range(size)])  99 us
    ppermute x24, starting transfers between devices, dp_swap(): return lax.ppermute(value, 'dp', [(i, i ^ mask) for i in range(size)])  29.9 us
    pallas_call x3, Pallas kernels, weight_split(): pl.pallas_call(body, out_shape=outs, grid_spec=pltpu.PrefetchScalarGridSp...  25.8 us
    unnamed x140, local copies, waits for them, and re-layouts  23.9 us
    ppermute x13, waiting for transfers between devices, y_swap(): return lax.ppermute(value, 'tensor', Y_SWAP)  22.9 us
    ppermute x13, starting transfers between devices, y_swap(): return lax.ppermute(value, 'tensor', Y_SWAP)  14.9 us
    pallas_call x2, Pallas kernels, weight_part(): pl.pallas_call(lambda *refs: weight_part_kernel(len(a), *refs), out_shape...  13.5 us
  transfers between devices with their start and end apart: 61, of which 26 were waited for; matrix products, arithmetic and copies ran while one was open for 12% of the time, Pallas kernels for 39%

profile of v2, /device:TPU:8, one launch (start us, length us, event | category | flops | bytes accessed | tf_op | source)
XLA Modules:
  0.0 555.1 jit_solution(15552882292412862435)
XLA Ops:
  10.6 2.6 prepare.2.refs_2_.refs_0_.refs_4_
  13.3 2.5 copy.114.refs_0_
  17.9 3.0 collective-permute-start.3
  22.6 2.7 prepare.3
  25.3 2.1 concatenate.37.refs_3_
  27.4 1.9 collective-permute-done.2.refs_0_
  29.4 9.6 %collective-permute-done.3.refs_1_ = bf16[144,864]{1,0:T(8,128)(2,1)} collective-permute-done((bf16[144,864]{1,0:T(8,128)(2,1)}, bf16[144,864]{1,0:T(8,128)(2,1)}, u32[]{:S(2)}, u32[]{:S(2)}) %collective-permute-start.3) | collective-permute-done | bytes 248864 | tf_op jit(solution)/shard_map/ppermute | solution.py:644
  38.9 5.5 collective-permute-done.4.refs_2_
  45.5 2.4 pad_maximum_fusion.1.refs_1_
  51.7 2.5 copy.124.refs_0_
  59.8 2.5 collective-permute-start.8
  64.0 15.4 %collective-permute-done.7.refs_5_ = bf16[4,144,864]{2,1,0:T(8,128)(2,1)} collective-permute-done((bf16[4,144,864]{2,1,0:T(8,128)(2,1)}, bf16[4,144,864]{2,1,0:T(8,128)(2,1)}, u32[]{:S(2)}, u32[]{:S(2)}) %collective-permute-start.7) | collective-permute-done | bytes 995360 | tf_op jit(solution)/shard_map/ppermute | solution.py:644
  79.3 3.9 place.3
  83.2 10.0 %attn_fwd.3 = (bf16[1152,768]{1,0:T(8,128)(2,1)}, bf16[12,72,768]{2,1,0:T(8,128)(2,1)}, bf16[288,768]{1,0:T(8,128)(2,1)}, f32[8,768]{1,0:T(8,128)}, f32[8,768]{1,0:T(8,128)}) custom-call(bf16[3,288,768]{2,1,0:T(8,128)(2,1)} %prepare.2.refs_2_.refs_0_.refs_4_, bf16[3,288,768]{2,1,0:T(8,128)(2,1)} %gate.21.refs_1_, bf16[3,288,768]{2,1,0:T(8,128)(2,1)} %copy-done, ...), custom_call_target="tpu_custom_call" | custom-call | flops 2000000000 | tf_op jit(solution)/shard_map/attn_fwd/pallas_call | solution.py:364
  95.1 36.3 %collective-permute-done.9.refs_1_ = bf16[144,1652]{1,0:T(8,128)(2,1)} collective-permute-done((bf16[144,1652]{1,0:T(8,128)(2,1)S(1)}, bf16[144,1652]{1,0:T(8,128)(2,1)}, u32[]{:S(2)}, u32[]{:S(2)}) %collective-permute-start.9) | collective-permute-done | bytes 475808 | tf_op jit(solution)/shard_map/ppermute | solution.py:644
  131.3 2.9 pad_maximum_fusion.refs_8_
  134.9 10.6 %attn_fwd.4 = (bf16[1152,768]{1,0:T(8,128)(2,1)}, bf16[12,72,768]{2,1,0:T(8,128)(2,1)}, bf16[288,768]{1,0:T(8,128)(2,1)}, f32[8,768]{1,0:T(8,128)}, f32[8,768]{1,0:T(8,128)}) custom-call(bf16[3,288,768]{2,1,0:T(8,128)(2,1)} %prepare.2.refs_2_.refs_0_.refs_4_, bf16[3,288,768]{2,1,0:T(8,128)(2,1)} %gate.21.refs_1_, bf16[3,288,768]{2,1,0:T(8,128)(2,1)} %copy-done, ...), custom_call_target="tpu_custom_call" | custom-call | flops 2000000000 | tf_op jit(solution)/shard_map/attn_fwd/pallas_call | solution.py:364
  149.7 10.0 %attn_fwd.5 = (bf16[1152,768]{1,0:T(8,128)(2,1)}, bf16[12,72,768]{2,1,0:T(8,128)(2,1)}, bf16[288,768]{1,0:T(8,128)(2,1)}, f32[8,768]{1,0:T(8,128)}, f32[8,768]{1,0:T(8,128)}) custom-call(bf16[3,288,768]{2,1,0:T(8,128)(2,1)} %prepare.2.refs_2_.refs_0_.refs_4_, bf16[3,288,768]{2,1,0:T(8,128)(2,1)} %gate.21.refs_1_, bf16[3,288,768]{2,1,0:T(8,128)(2,1)} %copy-done, ...), custom_call_target="tpu_custom_call" | custom-call | flops 2000000000 | tf_op jit(solution)/shard_map/attn_fwd/pallas_call | solution.py:364
  161.2 8.0 %collective-permute-done.16.refs_0_ = bf16[288,768]{1,0:T(8,128)(2,1)S(1)} collective-permute-done((bf16[288,768]{1,0:T(8,128)(2,1)S(1)}, bf16[288,768]{1,0:T(8,128)(2,1)S(1)}, u32[]{:S(2)}, u32[]{:S(2)}) %collective-permute-start.16) | collective-permute-done | bytes 442400 | tf_op jit(solution)/shard_map/ppermute | solution.py:26
  169.2 9.1 %collective-permute-done.12.refs_10_.refs_5_ = bf16[288,768]{1,0:T(8,128)(2,1)S(1)} collective-permute-done((bf16[288,768]{1,0:T(8,128)(2,1)}, bf16[288,768]{1,0:T(8,128)(2,1)S(1)}, u32[]{:S(2)}, u32[]{:S(2)}) %collective-permute-start.12) | collective-permute-done | bytes 442400 | tf_op jit(solution)/shard_map/ppermute | solution.py:26
  183.9 5.8 %place.4 = (bf16[8,144,576]{2,1,0:T(8,128)(2,1)}, bf16[8,144,1076]{2,1,0:T(8,128)(2,1)}, bf16[1076,1152]{1,0:T(8,128)(2,1)}) custom-call(s32[8]{0:T(128)} %stack.192.refs_0_, bf16[144,1652]{1,0:T(8,128)(2,1)} %get-tuple-element.153.refs_1_, bf16[144,1652]{1,0:T(8,128)(2,1)} %get-tuple-element.154.refs_2_, bf16[144,1652]{1,0:T(8,128)(2,1)} %get-tuple-element.155.refs_3_, ...), custom_call_target="tpu_custom_call" | custom-call | flops 800000000 | tf_op jit(solution)/shard_map/place/pallas_call | solution.py:364
  189.7 1.9 copy.98
  193.8 4.7 place.5
  198.5 1.9 copy.99.refs_1_
  200.4 4.3 join.1
  204.6 19.4 %mlp_fwd.3 = (bf16[1152,768]{1,0:T(8,128)(2,1)}, bf16[1152,768]{1,0:T(8,128)(2,1)}, bf16[1076,768]{1,0:T(8,128)(2,1)}, bf16[1076,768]{1,0:T(8,128)(2,1)}, f32[3,...) custom-call(bf16[3,288,768]{2,1,0:T(8,128)(2,1)} %prepare.2.refs_2_.refs_0_.refs, ...), custom_call_target="tpu_custom_call" | custom-call | flops 3900000000 | tf_op jit(solution)/shard_map/mlp_fwd/pallas_call | solution.py:364
  224.0 11.2 %mlp_bwd.3 = (bf16[1152,768]{1,0:T(8,128)(2,1)}, bf16[1076,768]{1,0:T(8,128)(2,1)}, f32[2,288,768]{2,1,0:T(8,128)}, bf16[2,288,768]{2,1,0:T(8,128)(2,1)}, f32[8,1076]{1,0:T(8,128)}) custom-call(bf16[3,288,768]{2,1,0:T(8,128)(2,1)} %get-tuple-element.158.refs_0_, bf16[3,288,768]{2,1,0:T(8,128)(2,1)} %gate.24.refs_1_, bf16[3,288,768]{2,1,0:T(8,128)(2,1)} %copy-done.3, ...), custom_call_target="tpu_custom_call" | custom-call | flops 2200000000 | tf_op jit(solution)/shard_map/mlp_bwd/pallas_call | solution.py:364
  235.3 2.5 collective-permute-done.25
  241.2 19.3 %mlp_fwd.4 = (bf16[1152,768]{1,0:T(8,128)(2,1)}, bf16[1152,768]{1,0:T(8,128)(2,1)}, bf16[1076,768]{1,0:T(8,128)(2,1)}, bf16[1076,768]{1,0:T(8,128)(2,1)}, f32[3,...) custom-call(bf16[3,288,768]{2,1,0:T(8,128)(2,1)} %prepare.2.refs_2_., ...), custom_call_target="tpu_custom_call", output_to_operand_aliasing={{4}: (13, {}), {6}: (14, {}), {7}: (15, {})} | custom-call | flops 3900000000 | tf_op jit(solution)/shard_map/mlp_fwd/pallas_call | solution.py:364
  262.4 2.3 add_convert_fusion.2.refs_7_
  264.6 11.5 %mlp_bwd.4 = (bf16[1152,768]{1,0:T(8,128)(2,1)}, bf16[1076,768]{1,0:T(8,128)(2,1)}, f32[2,288,768]{2,1,0:T(8,128)}, bf16[2,288,768]{2,1,0:T(8,128)(2,1)}, f32[8,1076]{1,0:T(8,128)}) custom-call(bf16[3,288,768]{2,1,0:T(8,128)(2,1)} %get-tuple-element.158.refs_0_, bf16[3,288,768]{2,1,0:T(8,128)(2,1)} %gate.24.refs_1_, bf16[3,288,768]{2,1,0:T(8,128)(2,1)} %copy-done.3, ...), custom_call_target="tpu_custom_call" | custom-call | flops 2200000000 | tf_op jit(solution)/shard_map/mlp_bwd/pallas_call | solution.py:364
  276.6 2.7 collective-permute-done.27
  283.5 19.5 %mlp_fwd.5 = (bf16[1152,768]{1,0:T(8,128)(2,1)}, bf16[1152,768]{1,0:T(8,128)(2,1)}, bf16[1076,768]{1,0:T(8,128)(2,1)}, bf16[1076,768]{1,0:T(8,128)(2,1)}, f32[3,...) custom-call(bf16[3,288,768]{2,1,0:T(8,128)(2,1)} %prepare.2.refs_2_., ...), custom_call_target="tpu_custom_call", output_to_operand_aliasing={{4}: (13, {}), {6}: (14, {}), {7}: (15, {})} | custom-call | flops 3900000000 | tf_op jit(solution)/shard_map/mlp_fwd/pallas_call | solution.py:364
  304.8 2.3 add_convert_fusion.1.refs_7_
  307.1 11.0 %mlp_bwd.5 = (bf16[1152,768]{1,0:T(8,128)(2,1)}, bf16[1076,768]{1,0:T(8,128)(2,1)}, f32[2,288,768]{2,1,0:T(8,128)}, bf16[2,288,768]{2,1,0:T(8,128)(2,1)}, f32[8,1076]{1,0:T(8,128)}) custom-call(bf16[3,288,768]{2,1,0:T(8,128)(2,1)} %get-tuple-element.158.refs_0_, bf16[3,288,768]{2,1,0:T(8,128)(2,1)} %gate.24.refs_1_, bf16[3,288,768]{2,1,0:T(8,128)(2,1)} %copy-done.3, ...), custom_call_target="tpu_custom_call" | custom-call | flops 2200000000 | tf_op jit(solution)/shard_map/mlp_bwd/pallas_call | solution.py:364
  318.5 3.5 collective-permute-done.31
  326.3 3.5 fusion.refs_9_.refs_1_
  329.8 12.3 %weight_grad.4 = bf16[4,288,1076]{2,1,0:T(8,128)(2,1)} custom-call(s32[4]{0:T(128)} %get-tuple-element.280.refs_0_, bf16[1152,768]{1,0:T(8,128)(2,1)} %get-tuple-element.200.refs_1_, bf16[1152,768]{1,0:T(8,128)(2,1)} %get-tuple-element.201.refs_2_, bf16[1152,768]{1,0:T(8,128)(2,1)} %get-tuple-element.202.refs_3_, ...), custom_call_target="tpu_custom_call" | custom-call | flops 2480000000 | tf_op jit(solution)/shard_map/weight_grad/pallas_call | solution.py:528
  342.1 12.6 %weight_grad.5 = (f32[4,144,1076]{2,1,0:T(8,128)}, bf16[4,144,1076]{2,1,0:T(8,128)(2,1)}) custom-call(s32[4]{0:T(128)} %get-tuple-element.279.refs_0_, s32[1]{0:T(128)} %bitcast.30.refs_1_, bf16[1152,768]{1,0:T(8,128)(2,1)} %get-tuple-element.194.refs_2_.refs_3_, bf16[1152,768]{1,0:T(8,128)(2,1)} %get-tuple-element.195.refs_3_, ...), custom_call_target="tpu_custom_call" | custom-call | flops 2480000000 | tf_op jit(solution)/shard_map/weight_grad/pallas_call | solution.py:588
  355.7 2.3 add_convert_fusion.refs_1_.refs_12_
  358.0 17.6 %attn_bwd.3 = (bf16[1152,768]{1,0:T(8,128)(2,1)}, f32[288,768]{1,0:T(8,128)}, bf16[864,768]{1,0:T(8,128)(2,1)}, f32[288,768]{1,0:T(8,128)}, f32[288,768]{1,0:T(8...) custom-call(f32[2,288,768]{2,1,0:T(8,128)} %copy-done.7, ...), custom_call_target="tpu_custom_call" | custom-call | flops 3540000000 | tf_op jit(solution)/shard_map/attn_bwd/pallas_call | solution.py:364
  380.8 2.3 fusion.11
  384.0 18.1 %attn_bwd.4 = (bf16[1152,768]{1,0:T(8,128)(2,1)}, f32[288,768]{1,0:T(8,128)}, bf16[864,768]{1,0:T(8,128)(2,1)}, f32[288,768]{1,0:T(8,128)}, f32[288,768]{1,0:T(8...) custom-call(f32[2,288,768]{2,1,0:T(8,128)} %copy-done.6, ...), custom_call_target="tpu_custom_call" | custom-call | flops 3540000000 | tf_op jit(solution)/shard_map/attn_bwd/pallas_call | solution.py:364
  402.1 13.8 %collective-permute-done.38.refs_0_ = bf16[4,144,1076]{2,1,0:T(8,128)(2,1)S(1)} collective-permute-done((bf16[4,144,1076]{2,1,0:T(8,128)(2,1)}, bf16[4,144,1076]{2,1,0:T(8,128)(2,1)S(1)}, u32[]{:S(2)}, u32[]{:S(2)}) %collective-permute-start.38) | collective-permute-done | bytes 1239584 | tf_op jit(solution)/shard_map/ppermute | solution.py:644
  419.4 3.5 fusion.24
  424.0 2.2 collective-permute-start.39
  430.4 5.4 weight_part.3.refs_13_.refs_4_
  435.8 8.1 %weight_part.2.refs_12_.refs_4_ = f32[1152,864]{1,0:T(8,128)} custom-call(bf16[1152,768]{1,0:T(8,128)(2,1)} %get-tuple-element.214.refs_11_.refs_0_, bf16[1152,768]{1,0:T(8,128)(2,1)} %get-tuple-element.215.refs_11_.refs_1_, bf16[864,768]{1,0:T(8,128)(2,1)} %get-tuple-element.218.refs_2_, bf16[864,768]{1,0:T(8,128)(2,1)} %get-tuple-element.222.refs_3_, ...), custom_call_target="tpu_custom_call" | custom-call | flops 1400000000 | tf_op jit(solution)/shard_map/weight_part/pallas_call | solution.py:551
  444.0 1.9 convert_element_type.172.refs_14_
  445.8 17.5 %attn_bwd.5 = (bf16[1152,768]{1,0:T(8,128)(2,1)}, f32[288,768]{1,0:T(8,128)}, bf16[864,768]{1,0:T(8,128)(2,1)}, f32[288,768]{1,0:T(8,128)}, f32[288,768]{1,0:T(8...) custom-call(f32[2,288,768]{2,1,0:T(8,128)} %copy-done.5, ...), custom_call_target="tpu_custom_call" | custom-call | flops 3540000000 | tf_op jit(solution)/shard_map/attn_bwd/pallas_call | solution.py:364
  463.3 7.4 %weight_grad.6 = (f32[4,144,864]{2,1,0:T(8,128)}, bf16[4,144,864]{2,1,0:T(8,128)(2,1)}) custom-call(s32[4]{0:T(128)} %get-tuple-element.279.refs_0_, s32[1]{0:T(128)} %bitcast.30.refs_1_, bf16[1152,768]{1,0:T(8,128)(2,1)} %get-tuple-element.213.refs_11_.refs_2_, bf16[864,768]{1,0:T(8,128)(2,1)} %get-tuple-element.237.refs_3_, ...), custom_call_target="tpu_custom_call" | custom-call | flops 2480000000 | tf_op jit(solution)/shard_map/weight_grad/pallas_call | solution.py:588
  474.1 2.3 fusion.7
  478.4 2.6 collective-permute-done.45
  481.1 2.3 fusion.13.refs_5_
  483.5 5.8 %weight_grad.7 = (f32[4,144,288]{2,1,0:T(8,128)}, bf16[4,144,288]{2,1,0:T(8,128)(2,1)}) custom-call(s32[4]{0:T(128)} %get-tuple-element.279.refs_0_, s32[1]{0:T(128)} %bitcast.30.refs_1_, bf16[1152,768]{1,0:T(8,128)(2,1)} %get-tuple-element.229.refs_2_, bf16[288,768]{1,0:T(8,128)(2,1)} %get-tuple-element.159.refs_9_.refs_4_.refs_3_, ...), custom_call_target="tpu_custom_call" | custom-call | flops 2480000000 | tf_op jit(solution)/shard_map/weight_grad/pallas_call | solution.py:588
  490.0 6.8 %collective-permute-done.47 = bf16[4,144,864]{2,1,0:T(8,128)(2,1)} collective-permute-done((bf16[4,144,864]{2,1,0:T(8,128)(2,1)}, bf16[4,144,864]{2,1,0:T(8,128)(2,1)}, u32[]{:S(2)}, u32[]{:S(2)}) %collective-permute-start.47) | collective-permute-done | bytes 995360 | tf_op jit(solution)/shard_map/ppermute | solution.py:644
  496.8 2.8 fusion.23
  500.5 2.9 collective-permute-start.48
  506.5 3.3 grad.3
  509.7 3.3 grad.4
  514.0 4.4 out.1
  518.8 4.4 collective-permute-done.50.refs_2_
  525.6 2.2 collective-permute-start.57
  531.0 3.3 grad.5
  (332 shorter events, 97.5 us)
Async XLA Ops:
  7.2 186.6 %all-gather.2.cloned.1.call-start = ((), (), s32[]{:S(2)}) async-start(), calls=%async_computation.1 | async-start | bytes 2985984 | tf_op jit(solution)/shard_map/all_gather | solution.py:759
  7.2 9.4 %collective-permute-start = (bf16[144,288]{1,0:T(8,128)(2,1)}, bf16[144,288]{1,0:T(8,128)(2,1)S(1)}, u32[]{:S(2)}, u32[]{:S(2)}) collective-permute-start(bf16[144,288]{1,0:T(8,128)(2,1)} %bitcast.141), channel_id=1, source_target_pairs={{0,2},{2,0},{1,3},{3,1},{4,6},{6,4},{5,7},{7,5},{8,10},{10,8},{9,1... | collective-permute-start | bytes 248840 | tf_op jit(solution)/shard_map/ppermute | solution.py:26
  17.4 27.0 %collective-permute-start.5 = (bf16[3,288,768]{2,1,0:T(8,128)(2,1)}, bf16[3,288,768]{2,1,0:T(8,128)(2,1)S(1)}, u32[]{:S(2)}, u32[]{:S(2)}) collective-permute-start(bf16[3,288,768]{2,1,0:T(8,128)(2,1)} %get-tuple-element.145), channel_id=1, source_target_pairs={{0,1},{1,0},{2,3},{3,2},{4,5},{5,4},{6,7},{7,6},{8,9},{9,8},{10,11... | collective-permute-start | bytes 3981320 | tf_op jit(solution)/shard_map/ppermute | solution.py:30
  17.4 31.8 %collective-permute-start.1 = (bf16[3,288,768]{2,1,0:T(8,128)(2,1)}, bf16[3,288,768]{2,1,0:T(8,128)(2,1)S(1)}, u32[]{:S(2)}, u32[]{:S(2)}) collective-permute-start(bf16[3,288,768]{2,1,0:T(8,128)(2,1)} %get-tuple-element.145), channel_id=1, source_target_pairs={{0,2},{2,0},{1,3},{3,1},{4,6},{6,4},{5,7},{7,5},{8,10},{10,8},{9,1... | collective-permute-start | bytes 3981320 | tf_op jit(solution)/shard_map/ppermute | solution.py:26
  17.9 11.4 %collective-permute-start.2 = (bf16[144,864]{1,0:T(8,128)(2,1)}, bf16[144,864]{1,0:T(8,128)(2,1)S(1)}, u32[]{:S(2)}, u32[]{:S(2)}) collective-permute-start(bf16[144,864]{1,0:T(8,128)(2,1)} %get-tuple-element.146.refs_1_), channel_id=1, source_target_pairs={{0,8},{4,12},{8,0},{12,4},{16,24},{20,28},{24,16},{28,20},{1,9},{5... | collective-permute-start | bytes 746504 | tf_op jit(solution)/shard_map/ppermute | solution.py:644
  17.9 21.0 %collective-permute-start.3 = (bf16[144,864]{1,0:T(8,128)(2,1)}, bf16[144,864]{1,0:T(8,128)(2,1)}, u32[]{:S(2)}, u32[]{:S(2)}) collective-permute-start(bf16[144,864]{1,0:T(8,128)(2,1)} %get-tuple-element.146.refs_1_), channel_id=1, source_target_pairs={{0,16},{4,20},{8,24},{12,28},{16,0},{20,4},{24,8},{28,12},{1,17},{... | collective-permute-start | bytes 746504 | tf_op jit(solution)/shard_map/ppermute | solution.py:644
  20.9 23.5 %collective-permute-start.4 = (bf16[144,864]{1,0:T(8,128)(2,1)}, bf16[144,864]{1,0:T(8,128)(2,1)}, u32[]{:S(2)}, u32[]{:S(2)}) collective-permute-start(bf16[144,864]{1,0:T(8,128)(2,1)} %get-tuple-element.146.refs_1_), channel_id=1, source_target_pairs={{0,24},{4,28},{8,16},{12,20},{16,8},{20,12},{24,0},{28,4},{1,25},{... | collective-permute-start | bytes 746504 | tf_op jit(solution)/shard_map/ppermute | solution.py:644
  50.2 4.1 collective-permute-start.6
  50.2 29.1 %collective-permute-start.7 = (bf16[4,144,864]{2,1,0:T(8,128)(2,1)}, bf16[4,144,864]{2,1,0:T(8,128)(2,1)}, u32[]{:S(2)}, u32[]{:S(2)}) collective-permute-start(bf16[4,144,864]{2,1,0:T(8,128)(2,1)} %pad_maximum_fusion.1.refs_1_), channel_id=1, source_target_pairs={{0,4},{4,0},{8,12},{12,8},{16,20},{20,16},{24,28},{28,24},{1,5},{5... | collective-permute-start | bytes 2985992 | tf_op jit(solution)/shard_map/ppermute | solution.py:644
  55.4 90.1 %collective-permute-start.18 = (bf16[3,288,768]{2,1,0:T(8,128)(2,1)}, bf16[3,288,768]{2,1,0:T(8,128)(2,1)S(1)}, u32[]{:S(2)}, u32[]{:S(2)}) collective-permute-start(bf16[3,288,768]{2,1,0:T(8,128)(2,1)} %gate.23), channel_id=1, source_target_pairs={{0,2},{2,0},{1,3},{3,1},{4,6},{6,4},{5,7},{7,5},{8,10},{10,8},{9,1... | collective-permute-start | bytes 3981320 | tf_op jit(solution)/shard_map/ppermute | solution.py:26
  55.9 388.0 %reduce-scatter.2.cloned.1.call-start = ((), (), s32[]{:S(2)}) async-start(), calls=%async_computation.2 | async-start | bytes 2985984 | tf_op jit(solution)/shard_map/reduce_scatter | solution.py:683
  58.1 35.8 %collective-permute-start.10 = (bf16[144,1652]{1,0:T(8,128)(2,1)S(1)}, bf16[144,1652]{1,0:T(8,128)(2,1)}, u32[]{:S(2)}, u32[]{:S(2)}) collective-permute-start(bf16[144,1652]{1,0:T(8,128)(2,1)S(1)} %copy-done.15), channel_id=1, source_target_pairs={{0,24},{4,28},{8,16},{12,20},{16,8},{20,12},{24,0},{28,4},{1,25},{... | collective-permute-start | bytes 1427336 | tf_op jit(solution)/shard_map/ppermute | solution.py:644
  59.8 35.3 %collective-permute-start.8 = (bf16[144,1652]{1,0:T(8,128)(2,1)S(1)}, bf16[144,1652]{1,0:T(8,128)(2,1)}, u32[]{:S(2)}, u32[]{:S(2)}) collective-permute-start(bf16[144,1652]{1,0:T(8,128)(2,1)S(1)} %copy-done.15), channel_id=1, source_target_pairs={{0,8},{4,12},{8,0},{12,4},{16,24},{20,28},{24,16},{28,20},{1,9},{5... | collective-permute-start | bytes 1427336 | tf_op jit(solution)/shard_map/ppermute | solution.py:644
  62.2 69.1 %collective-permute-start.9 = (bf16[144,1652]{1,0:T(8,128)(2,1)S(1)}, bf16[144,1652]{1,0:T(8,128)(2,1)}, u32[]{:S(2)}, u32[]{:S(2)}) collective-permute-start(bf16[144,1652]{1,0:T(8,128)(2,1)S(1)} %copy-done.15), channel_id=1, source_target_pairs={{0,16},{4,20},{8,24},{12,28},{16,0},{20,4},{24,8},{28,12},{1,17},{... | collective-permute-start | bytes 1427336 | tf_op jit(solution)/shard_map/ppermute | solution.py:644
  79.3 69.3 %collective-permute-start.11 = (bf16[3,288,768]{2,1,0:T(8,128)(2,1)}, bf16[3,288,768]{2,1,0:T(8,128)(2,1)S(1)}, u32[]{:S(2)}, u32[]{:S(2)}) collective-permute-start(bf16[3,288,768]{2,1,0:T(8,128)(2,1)} %get-tuple-element.158.refs_0_), channel_id=1, source_target_pairs={{0,1},{1,0},{2,3},{3,2},{4,5},{5,4},{6,7},{7,6},{8,9},{9,8},{10,11... | collective-permute-start | bytes 3981320 | tf_op jit(solution)/shard_map/ppermute | solution.py:30
  134.2 46.7 %collective-permute-start.15 = (bf16[4,144,1652]{2,1,0:T(8,128)(2,1)}, bf16[4,144,1652]{2,1,0:T(8,128)(2,1)}, u32[]{:S(2)}, u32[]{:S(2)}) collective-permute-start(bf16[4,144,1652]{2,1,0:T(8,128)(2,1)} %pad_maximum_fusion.refs_8_), channel_id=1, source_target_pairs={{0,4},{4,0},{8,12},{12,8},{16,20},{20,16},{24,28},{28,24},{1,5},{5... | collective-permute-start | bytes 5709320 | tf_op jit(solution)/shard_map/ppermute | solution.py:644
  146.5 31.8 %collective-permute-start.19 = (bf16[3,288,768]{2,1,0:T(8,128)(2,1)}, bf16[3,288,768]{2,1,0:T(8,128)(2,1)S(1)}, u32[]{:S(2)}, u32[]{:S(2)}) collective-permute-start(bf16[3,288,768]{2,1,0:T(8,128)(2,1)} %gate.24.refs_1_), channel_id=1, source_target_pairs={{0,1},{1,0},{2,3},{3,2},{4,5},{5,4},{6,7},{7,6},{8,9},{9,8},{10,11... | collective-permute-start | bytes 3981320 | tf_op jit(solution)/shard_map/ppermute | solution.py:30
  146.5 14.6 %collective-permute-start.17 = (bf16[288,768]{1,0:T(8,128)(2,1)}, bf16[288,768]{1,0:T(8,128)(2,1)S(1)}, u32[]{:S(2)}, u32[]{:S(2)}) collective-permute-start(bf16[288,768]{1,0:T(8,128)(2,1)} %get-tuple-element.161.refs_5_.refs_4_.refs_3_), channel_id=1, source_target_pairs={{0,2},{2,0},{1,3},{3,1},{4,6},{6,4},{5,7},{7,5},{8,10},{10,8},{9,1... | collective-permute-start | bytes 1327112 | tf_op jit(solution)/shard_map/ppermute | solution.py:26
  148.1 21.1 %collective-permute-start.16 = (bf16[288,768]{1,0:T(8,128)(2,1)S(1)}, bf16[288,768]{1,0:T(8,128)(2,1)S(1)}, u32[]{:S(2)}, u32[]{:S(2)}) collective-permute-start(bf16[288,768]{1,0:T(8,128)(2,1)S(1)} %copy-done.19), channel_id=1, source_target_pairs={{0,2},{2,0},{1,3},{3,1},{4,6},{6,4},{5,7},{7,5},{8,10},{10,8},{9,1... | collective-permute-start | bytes 1327112 | tf_op jit(solution)/shard_map/ppermute | solution.py:26
  159.6 18.7 %collective-permute-start.12 = (bf16[288,768]{1,0:T(8,128)(2,1)}, bf16[288,768]{1,0:T(8,128)(2,1)S(1)}, u32[]{:S(2)}, u32[]{:S(2)}) collective-permute-start(bf16[288,768]{1,0:T(8,128)(2,1)} %get-tuple-element.159.refs_9_.refs_4_.refs_3_), channel_id=1, source_target_pairs={{0,2},{2,0},{1,3},{3,1},{4,6},{6,4},{5,7},{7,5},{8,10},{10,8},{9,1... | collective-permute-start | bytes 1327112 | tf_op jit(solution)/shard_map/ppermute | solution.py:26
  161.2 18.3 %collective-permute-start.13 = (bf16[288,768]{1,0:T(8,128)(2,1)}, bf16[288,768]{1,0:T(8,128)(2,1)S(1)}, u32[]{:S(2)}, u32[]{:S(2)}) collective-permute-start(bf16[288,768]{1,0:T(8,128)(2,1)} %get-tuple-element.159.refs_9_.refs_4_.refs_3_), channel_id=1, source_target_pairs={{0,1},{1,0},{2,3},{3,2},{4,5},{5,4},{6,7},{7,6},{8,9},{9,8},{10,11... | collective-permute-start | bytes 1327112 | tf_op jit(solution)/shard_map/ppermute | solution.py:30
  169.2 11.5 %collective-permute-start.22 = (bf16[288,768]{1,0:T(8,128)(2,1)}, bf16[288,768]{1,0:T(8,128)(2,1)}, u32[]{:S(2)}, u32[]{:S(2)}) collective-permute-start(bf16[288,768]{1,0:T(8,128)(2,1)} %get-tuple-element.161.refs_5_.refs_4_.refs_3_), channel_id=1, source_target_pairs={{0,1},{1,0},{2,3},{3,2},{4,5},{5,4},{6,7},{7,6},{8,9},{9,8},{10,11... | collective-permute-start | bytes 1327112 | tf_op jit(solution)/shard_map/ppermute | solution.py:30
  178.3 2.5 collective-permute-start.20
  178.3 2.5 collective-permute-start.14
  180.2 2.1 collective-permute-start.21
  180.7 2.3 collective-permute-start.23
  191.7 6.8 %collective-permute-start.24 = (bf16[1152,576]{0,1:T(8,128)(2,1)S(1)}, bf16[1152,576]{0,1:T(8,128)(2,1)S(1)}, u32[]{:S(2)}, u32[]{:S(2)}) collective-permute-start(bf16[1152,576]{0,1:T(8,128)(2,1)S(1)} %copy.98), channel_id=1, source_target_pairs={{0,1},{1,0},{2,3},{3,2},{4,5},{5,4},{6,7},{7,6},{8,9},{9,8},{10,11... | collective-permute-start | bytes 3981320 | tf_op jit(solution)/shard_map/ppermute | solution.py:30
  235.2 2.6 collective-permute-start.25
  239.5 22.8 %copy-start.7 = (f32[2,288,768]{2,1,0:T(8,128)}, f32[2,288,768]{2,1,0:T(8,128)S(1)}, u32[]{:S(2)}) copy-start(f32[2,288,768]{2,1,0:T(8,128)S(1)} %convert_add_fusion.5.refs_0_) | copy-start | bytes 5308420
  239.6 21.8 %collective-permute-start.26 = (bf16[2,288,768]{2,1,0:T(8,128)(2,1)S(1)}, bf16[2,288,768]{2,1,0:T(8,128)(2,1)S(1)}, u32[]{:S(2)}, u32[]{:S(2)}) collective-permute-start(bf16[2,288,768]{2,1,0:T(8,128)(2,1)S(1)} %rev.17.refs_16_), channel_id=1, source_target_pairs={{0,2},{2,0},{1,3},{3,1},{4,6},{6,4},{5,7},{7,5},{8,10},{10,8},{9,1... | collective-permute-start | bytes 2654216 | tf_op jit(solution)/shard_map/ppermute | solution.py:26
  276.1 3.2 collective-permute-start.27
  276.1 7.4 %collective-permute-start.28 = (bf16[2,288,768]{2,1,0:T(8,128)(2,1)S(1)}, bf16[2,288,768]{2,1,0:T(8,128)(2,1)}, u32[]{:S(2)}, u32[]{:S(2)}) collective-permute-start(bf16[2,288,768]{2,1,0:T(8,128)(2,1)S(1)} %copy-done.24), channel_id=1, source_target_pairs={{0,1},{1,0},{2,3},{3,2},{4,5},{5,4},{6,7},{7,6},{8,9},{9,8},{10,11... | collective-permute-start | bytes 2654216 | tf_op jit(solution)/shard_map/ppermute | solution.py:30
  280.9 23.9 %copy-start.6 = (f32[2,288,768]{2,1,0:T(8,128)}, f32[2,288,768]{2,1,0:T(8,128)S(1)}, u32[]{:S(2)}) copy-start(f32[2,288,768]{2,1,0:T(8,128)S(1)} %convert_add_fusion.4.refs_0_) | copy-start | bytes 5308420
  282.0 21.9 %collective-permute-start.29 = (bf16[2,288,768]{2,1,0:T(8,128)(2,1)}, bf16[2,288,768]{2,1,0:T(8,128)(2,1)S(1)}, u32[]{:S(2)}, u32[]{:S(2)}) collective-permute-start(bf16[2,288,768]{2,1,0:T(8,128)(2,1)} %rev.16.refs_16_), channel_id=1, source_target_pairs={{0,2},{2,0},{1,3},{3,1},{4,6},{6,4},{5,7},{7,5},{8,10},{10,8},{9,1... | collective-permute-start | bytes 2654216 | tf_op jit(solution)/shard_map/ppermute | solution.py:26
  304.8 21.5 %collective-permute-start.30 = (bf16[3,2,288,768]{3,2,1,0:T(8,128)(2,1)}, bf16[3,2,288,768]{3,2,1,0:T(8,128)(2,1)}, u32[]{:S(2)}, u32[]{:S(2)}) collective-permute-start(bf16[3,2,288,768]{3,2,1,0:T(8,128)(2,1)} %get-tuple-element.188), channel_id=1, source_target_pairs={{0,1},{1,0},{2,3},{3,2},{4,5},{5,4},{6,7},{7,6},{8,9},{9,8},{10,11... | collective-permute-start | bytes 7962632 | tf_op jit(solution)/shard_map/ppermute | solution.py:30
  318.0 4.0 collective-permute-start.31
  318.5 11.3 %collective-permute-start.33 = (bf16[2,288,768]{2,1,0:T(8,128)(2,1)}, bf16[2,288,768]{2,1,0:T(8,128)(2,1)}, u32[]{:S(2)}, u32[]{:S(2)}) collective-permute-start(bf16[2,288,768]{2,1,0:T(8,128)(2,1)} %add_convert_fusion.1.refs_7_), channel_id=1, source_target_pairs={{0,1},{1,0},{2,3},{3,2},{4,5},{5,4},{6,7},{7,6},{8,9},{9,8},{10,11... | collective-permute-start | bytes 2654216 | tf_op jit(solution)/shard_map/ppermute | solution.py:30
  323.7 32.0 %copy-start.5 = (f32[2,288,768]{2,1,0:T(8,128)}, f32[2,288,768]{2,1,0:T(8,128)S(1)}, u32[]{:S(2)}) copy-start(f32[2,288,768]{2,1,0:T(8,128)S(1)} %convert_add_fusion.3.refs_0_) | copy-start | bytes 5308420
  324.8 29.9 %collective-permute-start.32 = (bf16[2,288,768]{2,1,0:T(8,128)(2,1)}, bf16[2,288,768]{2,1,0:T(8,128)(2,1)S(1)}, u32[]{:S(2)}, u32[]{:S(2)}) collective-permute-start(bf16[2,288,768]{2,1,0:T(8,128)(2,1)} %rev.15.refs_1_.refs_7_), channel_id=1, source_target_pairs={{0,2},{2,0},{1,3},{3,1},{4,6},{6,4},{5,7},{7,5},{8,10},{10,8},{9,1... | collective-permute-start | bytes 2654216 | tf_op jit(solution)/shard_map/ppermute | solution.py:26
  375.6 5.2 collective-permute-start.36
  375.7 41.3 %collective-permute-start.34 = (bf16[3,288,768]{2,1,0:T(8,128)(2,1)}, bf16[3,288,768]{2,1,0:T(8,128)(2,1)S(1)}, u32[]{:S(2)}, u32[]{:S(2)}) collective-permute-start(bf16[3,288,768]{2,1,0:T(8,128)(2,1)} %gate.31), channel_id=1, source_target_pairs={{0,2},{2,0},{1,3},{3,1},{4,6},{6,4},{5,7},{7,5},{8,10},{10,8},{9,1... | collective-permute-start | bytes 3981320 | tf_op jit(solution)/shard_map/ppermute | solution.py:26
  376.2 39.7 %collective-permute-start.38 = (bf16[4,144,1076]{2,1,0:T(8,128)(2,1)}, bf16[4,144,1076]{2,1,0:T(8,128)(2,1)S(1)}, u32[]{:S(2)}, u32[]{:S(2)}) collective-permute-start(bf16[4,144,1076]{2,1,0:T(8,128)(2,1)} %get-tuple-element.206.refs_2_.refs_13_), channel_id=1, source_target_pairs={{0,4},{4,0},{8,12},{12,8},{16,20},{20,16},{24,28},{28,24},{1,5},{5... | collective-permute-start | bytes 3718664 | tf_op jit(solution)/shard_map/ppermute | solution.py:644
  377.6 5.5 collective-permute-start.35
  418.1 9.6 %collective-permute-start.37 = (bf16[2,288,768]{2,1,0:T(8,128)(2,1)}, bf16[2,288,768]{2,1,0:T(8,128)(2,1)S(1)}, u32[]{:S(2)}, u32[]{:S(2)}) collective-permute-start(bf16[2,288,768]{2,1,0:T(8,128)(2,1)} %gate.32), channel_id=1, source_target_pairs={{0,1},{1,0},{2,3},{3,2},{4,5},{5,4},{6,7},{7,6},{8,9},{9,8},{10,11... | collective-permute-start | bytes 2654216 | tf_op jit(solution)/shard_map/ppermute | solution.py:30
  424.0 48.8 %collective-permute-start.39 = (bf16[144,1076]{1,0:T(8,128)(2,1)}, bf16[144,1076]{1,0:T(8,128)(2,1)S(1)}, u32[]{:S(2)}, u32[]{:S(2)}) collective-permute-start(bf16[144,1076]{1,0:T(8,128)(2,1)} %get-tuple-element.283), channel_id=1, source_target_pairs={{0,8},{4,12},{8,0},{12,4},{16,24},{20,28},{24,16},{28,20},{1,9},{5... | collective-permute-start | bytes 929672 | tf_op jit(solution)/shard_map/ppermute | solution.py:644
  426.2 46.6 %collective-permute-start.40 = (bf16[144,1076]{1,0:T(8,128)(2,1)}, bf16[144,1076]{1,0:T(8,128)(2,1)}, u32[]{:S(2)}, u32[]{:S(2)}) collective-permute-start(bf16[144,1076]{1,0:T(8,128)(2,1)} %get-tuple-element.282), channel_id=1, source_target_pairs={{0,16},{4,20},{8,24},{12,28},{16,0},{20,4},{24,8},{28,12},{1,17},{... | collective-permute-start | bytes 929672 | tf_op jit(solution)/shard_map/ppermute | solution.py:644
  426.9 45.9 %collective-permute-start.41 = (bf16[144,1076]{1,0:T(8,128)(2,1)}, bf16[144,1076]{1,0:T(8,128)(2,1)}, u32[]{:S(2)}, u32[]{:S(2)}) collective-permute-start(bf16[144,1076]{1,0:T(8,128)(2,1)} %get-tuple-element.281), channel_id=1, source_target_pairs={{0,24},{4,28},{8,16},{12,20},{16,8},{20,12},{24,0},{28,4},{1,25},{... | collective-permute-start | bytes 929672 | tf_op jit(solution)/shard_map/ppermute | solution.py:644
  428.6 76.9 %collective-permute-start.46 = (bf16[2,288,768]{2,1,0:T(8,128)(2,1)S(1)}, bf16[2,288,768]{2,1,0:T(8,128)(2,1)S(1)}, u32[]{:S(2)}, u32[]{:S(2)}) collective-permute-start(bf16[2,288,768]{2,1,0:T(8,128)(2,1)S(1)} %pad_maximum_fusion.2.refs_4_), channel_id=1, source_target_pairs={{0,2},{2,0},{1,3},{3,1},{4,6},{6,4},{5,7},{7,5},{8,10},{10,8},{9,1... | collective-permute-start | bytes 2654216 | tf_op jit(solution)/shard_map/ppermute | solution.py:26
  470.7 26.1 %collective-permute-start.47 = (bf16[4,144,864]{2,1,0:T(8,128)(2,1)}, bf16[4,144,864]{2,1,0:T(8,128)(2,1)}, u32[]{:S(2)}, u32[]{:S(2)}) collective-permute-start(bf16[4,144,864]{2,1,0:T(8,128)(2,1)} %get-tuple-element.239.refs_5_), channel_id=1, source_target_pairs={{0,4},{4,0},{8,12},{12,8},{16,20},{20,16},{24,28},{28,24},{1,5},{5... | collective-permute-start | bytes 2985992 | tf_op jit(solution)/shard_map/ppermute | solution.py:644
  473.5 7.6 %collective-permute-start.42 = (bf16[2,288,768]{2,1,0:T(8,128)(2,1)}, bf16[2,288,768]{2,1,0:T(8,128)(2,1)S(1)}, u32[]{:S(2)}, u32[]{:S(2)}) collective-permute-start(bf16[2,288,768]{2,1,0:T(8,128)(2,1)} %get-tuple-element.240), channel_id=1, source_target_pairs={{0,1},{1,0},{2,3},{3,2},{4,5},{5,4},{6,7},{7,6},{8,9},{9,8},{10,11... | collective-permute-start | bytes 2654216 | tf_op jit(solution)/shard_map/ppermute | solution.py:30
  473.6 3.1 collective-permute-start.44
  476.7 4.4 collective-permute-start.45
  489.3 29.1 %collective-permute-start.51 = (bf16[4,144,288]{2,1,0:T(8,128)(2,1)}, bf16[4,144,288]{2,1,0:T(8,128)(2,1)S(1)}, u32[]{:S(2)}, u32[]{:S(2)}) collective-permute-start(bf16[4,144,288]{2,1,0:T(8,128)(2,1)} %get-tuple-element.241.refs_1_.refs_4_), channel_id=1, source_target_pairs={{0,4},{4,0},{8,12},{12,8},{16,20},{20,16},{24,28},{28,24},{1,5},{5... | collective-permute-start | bytes 995336 | tf_op jit(solution)/shard_map/ppermute | solution.py:644
  500.5 17.8 %collective-permute-start.48 = (bf16[144,864]{1,0:T(8,128)(2,1)}, bf16[144,864]{1,0:T(8,128)(2,1)S(1)}, u32[]{:S(2)}, u32[]{:S(2)}) collective-permute-start(bf16[144,864]{1,0:T(8,128)(2,1)} %get-tuple-element.286), channel_id=1, source_target_pairs={{0,8},{4,12},{8,0},{12,4},{16,24},{20,28},{24,16},{28,20},{1,9},{5... | collective-permute-start | bytes 746504 | tf_op jit(solution)/shard_map/ppermute | solution.py:644
  503.5 15.3 %collective-permute-start.49 = (bf16[144,864]{1,0:T(8,128)(2,1)}, bf16[144,864]{1,0:T(8,128)(2,1)S(1)}, u32[]{:S(2)}, u32[]{:S(2)}) collective-permute-start(bf16[144,864]{1,0:T(8,128)(2,1)} %get-tuple-element.285), channel_id=1, source_target_pairs={{0,16},{4,20},{8,24},{12,28},{16,0},{20,4},{24,8},{28,12},{1,17},{... | collective-permute-start | bytes 746504 | tf_op jit(solution)/shard_map/ppermute | solution.py:644
  503.7 19.5 %collective-permute-start.50 = (bf16[144,864]{1,0:T(8,128)(2,1)}, bf16[144,864]{1,0:T(8,128)(2,1)S(1)}, u32[]{:S(2)}, u32[]{:S(2)}) collective-permute-start(bf16[144,864]{1,0:T(8,128)(2,1)} %get-tuple-element.284), channel_id=1, source_target_pairs={{0,24},{4,28},{8,16},{12,20},{16,8},{20,12},{24,0},{28,4},{1,25},{... | collective-permute-start | bytes 746504 | tf_op jit(solution)/shard_map/ppermute | solution.py:644
  513.1 17.1 %collective-permute-start.43 = (bf16[1,288,768]{2,1,0:T(8,128)(2,1)S(1)}, bf16[1,288,768]{2,1,0:T(8,128)(2,1)S(1)}, u32[]{:S(2)}, u32[]{:S(2)}) collective-permute-start(bf16[1,288,768]{2,1,0:T(8,128)(2,1)S(1)} %copy-done.48), channel_id=1, source_target_pairs={{0,2},{2,0},{1,3},{3,1},{4,6},{6,4},{5,7},{7,5},{8,10},{10,8},{9,1... | collective-permute-start | bytes 1327112 | tf_op jit(solution)/shard_map/ppermute | solution.py:26
  525.5 17.5 %collective-permute-start.56 = (bf16[144,288]{1,0:T(8,128)(2,1)S(1)}, bf16[144,288]{1,0:T(8,128)(2,1)S(1)}, u32[]{:S(2)}, u32[]{:S(2)}) collective-permute-start(bf16[144,288]{1,0:T(8,128)(2,1)S(1)} %get-tuple-element.290), channel_id=1, source_target_pairs={{0,8},{4,12},{8,0},{12,4},{16,24},{20,28},{24,16},{28,20},{1,9},{5... | collective-permute-start | bytes 248840 | tf_op jit(solution)/shard_map/ppermute | solution.py:644
  525.6 18.8 %collective-permute-start.57 = (bf16[144,288]{1,0:T(8,128)(2,1)S(1)}, bf16[144,288]{1,0:T(8,128)(2,1)S(1)}, u32[]{:S(2)}, u32[]{:S(2)}) collective-permute-start(bf16[144,288]{1,0:T(8,128)(2,1)S(1)} %get-tuple-element.292), channel_id=1, source_target_pairs={{0,16},{4,20},{8,24},{12,28},{16,0},{20,4},{24,8},{28,12},{1,17},{... | collective-permute-start | bytes 248840 | tf_op jit(solution)/shard_map/ppermute | solution.py:644
  527.7 16.6 %collective-permute-start.58 = (bf16[144,288]{1,0:T(8,128)(2,1)S(1)}, bf16[144,288]{1,0:T(8,128)(2,1)S(1)}, u32[]{:S(2)}, u32[]{:S(2)}) collective-permute-start(bf16[144,288]{1,0:T(8,128)(2,1)S(1)} %get-tuple-element.291), channel_id=1, source_target_pairs={{0,24},{4,28},{8,16},{12,20},{16,8},{20,12},{24,0},{28,4},{1,25},{... | collective-permute-start | bytes 248840 | tf_op jit(solution)/shard_map/ppermute | solution.py:644
  536.2 3.9 collective-permute-start.52
  540.8 4.3 collective-permute-start.53
  541.8 4.6 collective-permute-start.54
  543.0 3.7 collective-permute-start.55
  (66 other events, 274.7 us)
Sparse Core Ops, SparseCore 0:
  56.0 76.9 all-gather.1
  342.2 79.2 reduce-scatter.1

commit v3 on v2

--- a/solution.py
+++ b/solution.py
@@ -909,11 +909,6 @@
         (out_across,) = gate([out_across], [send_b])
         own_a, sends_a = scatter_first(keep_a, x_a)
         came_a = scatter_second(sends_a)
-        *came_a, x_b = gate([*came_a, x_b], [send_b])
-        own_b, sends_b = scatter_first(keep_b, x_b)
-        came_b = scatter_second(sends_b)
-        qkv_grad = scatter_last(own_a, came_a)
-        out_grad = scatter_last(own_b, came_b)
     out_buffer = finish_out(live, base, mlp_came, out_across, seq)
     grad_buffer, sums = None, None
     for i in range(slots):
@@ -924,6 +919,12 @@
         )
         now = (grad_sums, ends[i][7], ends[i][8], back[i][-1])
         sums = now if sums is None else jax.tree.map(jnp.add, sums, now)
+    if fast:
+        *came_a, x_b = gate([*came_a, x_b], [send_b, grad_sums])
+        own_b, sends_b = scatter_first(keep_b, x_b)
+        came_b = scatter_second(sends_b)
+        qkv_grad = scatter_last(own_a, came_a)
+        out_grad = scatter_last(own_b, came_b)
     down_grad, out_grad = down_grad.T, out_grad.T
     sums = (*sums, cot_sums)
     sizes = [2 * share, 3 * share, 3 * share, up_bias.shape[0], share]

time: 563 us -> 558 us (level)
    unnamed x140 -> x144, local copies, waits for them, and re-layouts: 23.9 us -> 23 us
  transfers between devices with their start and end apart: 61 -> 61, of which waited for: 26 -> 25; matrix products, arithmetic and copies ran while one was open for 12% -> 12% of each run, Pallas kernels for 39% -> 40%
where the time goes in v3:
time: 558 us; the launch traced here: 550 us
  Pallas kernels  265 us (47%)
  waiting for transfers between devices  131 us (23%)
  starting transfers between devices  47.5 us (9%)
  local copies, waits for them, and re-layouts  46 us (8%)
  other arithmetic  44.6 us (8%)
  between operations  15.6 us (3%)
    pallas_call x21, Pallas kernels, run(): pl.pallas_call(body, grid=(1,), out_shape=tuple(shapes), in_specs=[*[SCAL...  209 us
    ppermute x24, waiting for transfers between devices, dp_swap(): return lax.ppermute(value, 'dp', [(i, i ^ mask) for i in range(size)])  96.8 us
    ppermute x24, starting transfers between devices, dp_swap(): return lax.ppermute(value, 'dp', [(i, i ^ mask) for i in range(size)])  29.3 us
    pallas_call x3, Pallas kernels, weight_split(): pl.pallas_call(body, out_shape=outs, grid_spec=pltpu.PrefetchScalarGridSp...  25.8 us
    unnamed x144, local copies, waits for them, and re-layouts  23 us
    ppermute x13, waiting for transfers between devices, y_swap(): return lax.ppermute(value, 'tensor', Y_SWAP)  22.9 us
    ppermute x13, starting transfers between devices, y_swap(): return lax.ppermute(value, 'tensor', Y_SWAP)  14.4 us
    pallas_call x2, Pallas kernels, weight_part(): pl.pallas_call(lambda *refs: weight_part_kernel(len(a), *refs), out_shape...  13.5 us
  transfers between devices with their start and end apart: 61, of which 25 were waited for; matrix products, arithmetic and copies ran while one was open for 12% of the time, Pallas kernels for 40%

profile of v3, /device:TPU:8, one launch (start us, length us, event | category | flops | bytes accessed | tf_op | source)
XLA Modules:
  0.0 549.7 jit_solution(8240661764046819943)
XLA Ops:
  10.6 2.6 prepare.2.refs_2_.refs_0_.refs_4_
  13.3 2.5 copy.114.refs_0_
  17.9 3.0 collective-permute-start.3
  22.6 2.7 prepare.3
  25.3 2.1 concatenate.37.refs_3_
  27.4 2.0 collective-permute-done.2.refs_0_
  29.4 9.6 %collective-permute-done.3.refs_1_ = bf16[144,864]{1,0:T(8,128)(2,1)} collective-permute-done((bf16[144,864]{1,0:T(8,128)(2,1)}, bf16[144,864]{1,0:T(8,128)(2,1)}, u32[]{:S(2)}, u32[]{:S(2)}) %collective-permute-start.3) | collective-permute-done | bytes 248864 | tf_op jit(solution)/shard_map/ppermute | solution.py:644
  38.9 5.5 collective-permute-done.4.refs_2_
  45.5 2.4 pad_maximum_fusion.1.refs_1_
  51.7 2.5 copy.124.refs_0_
  59.8 2.5 collective-permute-start.8
  64.0 15.4 %collective-permute-done.7.refs_5_ = bf16[4,144,864]{2,1,0:T(8,128)(2,1)} collective-permute-done((bf16[4,144,864]{2,1,0:T(8,128)(2,1)}, bf16[4,144,864]{2,1,0:T(8,128)(2,1)}, u32[]{:S(2)}, u32[]{:S(2)}) %collective-permute-start.7) | collective-permute-done | bytes 995360 | tf_op jit(solution)/shard_map/ppermute | solution.py:644
  79.3 3.9 place.3
  83.2 10.0 %attn_fwd.3 = (bf16[1152,768]{1,0:T(8,128)(2,1)}, bf16[12,72,768]{2,1,0:T(8,128)(2,1)}, bf16[288,768]{1,0:T(8,128)(2,1)}, f32[8,768]{1,0:T(8,128)}, f32[8,768]{1,0:T(8,128)}) custom-call(bf16[3,288,768]{2,1,0:T(8,128)(2,1)} %prepare.2.refs_2_.refs_0_.refs_4_, bf16[3,288,768]{2,1,0:T(8,128)(2,1)} %gate.21.refs_1_, bf16[3,288,768]{2,1,0:T(8,128)(2,1)} %copy-done, ...), custom_call_target="tpu_custom_call" | custom-call | flops 2000000000 | tf_op jit(solution)/shard_map/attn_fwd/pallas_call | solution.py:364
  95.2 36.2 %collective-permute-done.9.refs_1_ = bf16[144,1652]{1,0:T(8,128)(2,1)} collective-permute-done((bf16[144,1652]{1,0:T(8,128)(2,1)S(1)}, bf16[144,1652]{1,0:T(8,128)(2,1)}, u32[]{:S(2)}, u32[]{:S(2)}) %collective-permute-start.9) | collective-permute-done | bytes 475808 | tf_op jit(solution)/shard_map/ppermute | solution.py:644
  131.4 2.9 pad_maximum_fusion.refs_8_
  135.0 10.6 %attn_fwd.4 = (bf16[1152,768]{1,0:T(8,128)(2,1)}, bf16[12,72,768]{2,1,0:T(8,128)(2,1)}, bf16[288,768]{1,0:T(8,128)(2,1)}, f32[8,768]{1,0:T(8,128)}, f32[8,768]{1,0:T(8,128)}) custom-call(bf16[3,288,768]{2,1,0:T(8,128)(2,1)} %prepare.2.refs_2_.refs_0_.refs_4_, bf16[3,288,768]{2,1,0:T(8,128)(2,1)} %gate.21.refs_1_, bf16[3,288,768]{2,1,0:T(8,128)(2,1)} %copy-done, ...), custom_call_target="tpu_custom_call" | custom-call | flops 2000000000 | tf_op jit(solution)/shard_map/attn_fwd/pallas_call | solution.py:364
  149.7 10.0 %attn_fwd.5 = (bf16[1152,768]{1,0:T(8,128)(2,1)}, bf16[12,72,768]{2,1,0:T(8,128)(2,1)}, bf16[288,768]{1,0:T(8,128)(2,1)}, f32[8,768]{1,0:T(8,128)}, f32[8,768]{1,0:T(8,128)}) custom-call(bf16[3,288,768]{2,1,0:T(8,128)(2,1)} %prepare.2.refs_2_.refs_0_.refs_4_, bf16[3,288,768]{2,1,0:T(8,128)(2,1)} %gate.21.refs_1_, bf16[3,288,768]{2,1,0:T(8,128)(2,1)} %copy-done, ...), custom_call_target="tpu_custom_call" | custom-call | flops 2000000000 | tf_op jit(solution)/shard_map/attn_fwd/pallas_call | solution.py:364
  161.2 8.0 %collective-permute-done.16.refs_0_ = bf16[288,768]{1,0:T(8,128)(2,1)S(1)} collective-permute-done((bf16[288,768]{1,0:T(8,128)(2,1)S(1)}, bf16[288,768]{1,0:T(8,128)(2,1)S(1)}, u32[]{:S(2)}, u32[]{:S(2)}) %collective-permute-start.16) | collective-permute-done | bytes 442400 | tf_op jit(solution)/shard_map/ppermute | solution.py:26
  169.3 9.1 %collective-permute-done.12.refs_10_.refs_5_ = bf16[288,768]{1,0:T(8,128)(2,1)S(1)} collective-permute-done((bf16[288,768]{1,0:T(8,128)(2,1)}, bf16[288,768]{1,0:T(8,128)(2,1)S(1)}, u32[]{:S(2)}, u32[]{:S(2)}) %collective-permute-start.12) | collective-permute-done | bytes 442400 | tf_op jit(solution)/shard_map/ppermute | solution.py:26
  183.9 5.8 %place.4 = (bf16[8,144,576]{2,1,0:T(8,128)(2,1)}, bf16[8,144,1076]{2,1,0:T(8,128)(2,1)}, bf16[1076,1152]{1,0:T(8,128)(2,1)}) custom-call(s32[8]{0:T(128)} %stack.192.refs_0_, bf16[144,1652]{1,0:T(8,128)(2,1)} %get-tuple-element.153.refs_1_, bf16[144,1652]{1,0:T(8,128)(2,1)} %get-tuple-element.154.refs_2_, bf16[144,1652]{1,0:T(8,128)(2,1)} %get-tuple-element.155.refs_3_, ...), custom_call_target="tpu_custom_call" | custom-call | flops 800000000 | tf_op jit(solution)/shard_map/place/pallas_call | solution.py:364
  189.8 1.9 copy.98
  193.9 4.7 place.5
  198.5 1.9 copy.99.refs_1_
  200.4 4.3 join.1
  204.7 19.3 %mlp_fwd.3 = (bf16[1152,768]{1,0:T(8,128)(2,1)}, bf16[1152,768]{1,0:T(8,128)(2,1)}, bf16[1076,768]{1,0:T(8,128)(2,1)}, bf16[1076,768]{1,0:T(8,128)(2,1)}, f32[3,...) custom-call(bf16[3,288,768]{2,1,0:T(8,128)(2,1)} %prepare.2.refs_2_.refs_0_.refs, ...), custom_call_target="tpu_custom_call" | custom-call | flops 3900000000 | tf_op jit(solution)/shard_map/mlp_fwd/pallas_call | solution.py:364
  224.0 11.2 %mlp_bwd.3 = (bf16[1152,768]{1,0:T(8,128)(2,1)}, bf16[1076,768]{1,0:T(8,128)(2,1)}, f32[2,288,768]{2,1,0:T(8,128)}, bf16[2,288,768]{2,1,0:T(8,128)(2,1)}, f32[8,1076]{1,0:T(8,128)}) custom-call(bf16[3,288,768]{2,1,0:T(8,128)(2,1)} %get-tuple-element.158.refs_0_, bf16[3,288,768]{2,1,0:T(8,128)(2,1)} %gate.24.refs_1_, bf16[3,288,768]{2,1,0:T(8,128)(2,1)} %copy-done.3, ...), custom_call_target="tpu_custom_call" | custom-call | flops 2200000000 | tf_op jit(solution)/shard_map/mlp_bwd/pallas_call | solution.py:364
  235.3 2.5 collective-permute-done.25
  241.3 19.3 %mlp_fwd.4 = (bf16[1152,768]{1,0:T(8,128)(2,1)}, bf16[1152,768]{1,0:T(8,128)(2,1)}, bf16[1076,768]{1,0:T(8,128)(2,1)}, bf16[1076,768]{1,0:T(8,128)(2,1)}, f32[3,...) custom-call(bf16[3,288,768]{2,1,0:T(8,128)(2,1)} %prepare.2.refs_2_., ...), custom_call_target="tpu_custom_call", output_to_operand_aliasing={{4}: (13, {}), {6}: (14, {}), {7}: (15, {})} | custom-call | flops 3900000000 | tf_op jit(solution)/shard_map/mlp_fwd/pallas_call | solution.py:364
  262.4 2.3 add_convert_fusion.2.refs_7_
  264.6 11.4 %mlp_bwd.4 = (bf16[1152,768]{1,0:T(8,128)(2,1)}, bf16[1076,768]{1,0:T(8,128)(2,1)}, f32[2,288,768]{2,1,0:T(8,128)}, bf16[2,288,768]{2,1,0:T(8,128)(2,1)}, f32[8,1076]{1,0:T(8,128)}) custom-call(bf16[3,288,768]{2,1,0:T(8,128)(2,1)} %get-tuple-element.158.refs_0_, bf16[3,288,768]{2,1,0:T(8,128)(2,1)} %gate.24.refs_1_, bf16[3,288,768]{2,1,0:T(8,128)(2,1)} %copy-done.3, ...), custom_call_target="tpu_custom_call" | custom-call | flops 2200000000 | tf_op jit(solution)/shard_map/mlp_bwd/pallas_call | solution.py:364
  276.6 2.7 collective-permute-done.27
  283.5 19.5 %mlp_fwd.5 = (bf16[1152,768]{1,0:T(8,128)(2,1)}, bf16[1152,768]{1,0:T(8,128)(2,1)}, bf16[1076,768]{1,0:T(8,128)(2,1)}, bf16[1076,768]{1,0:T(8,128)(2,1)}, f32[3,...) custom-call(bf16[3,288,768]{2,1,0:T(8,128)(2,1)} %prepare.2.refs_2_., ...), custom_call_target="tpu_custom_call", output_to_operand_aliasing={{4}: (13, {}), {6}: (14, {}), {7}: (15, {})} | custom-call | flops 3900000000 | tf_op jit(solution)/shard_map/mlp_fwd/pallas_call | solution.py:364
  304.8 2.3 add_convert_fusion.1.refs_7_
  307.1 11.0 %mlp_bwd.5 = (bf16[1152,768]{1,0:T(8,128)(2,1)}, bf16[1076,768]{1,0:T(8,128)(2,1)}, f32[2,288,768]{2,1,0:T(8,128)}, bf16[2,288,768]{2,1,0:T(8,128)(2,1)}, f32[8,1076]{1,0:T(8,128)}) custom-call(bf16[3,288,768]{2,1,0:T(8,128)(2,1)} %get-tuple-element.158.refs_0_, bf16[3,288,768]{2,1,0:T(8,128)(2,1)} %gate.24.refs_1_, bf16[3,288,768]{2,1,0:T(8,128)(2,1)} %copy-done.3, ...), custom_call_target="tpu_custom_call" | custom-call | flops 2200000000 | tf_op jit(solution)/shard_map/mlp_bwd/pallas_call | solution.py:364
  318.6 3.5 collective-permute-done.31
  326.4 3.5 fusion.refs_9_.refs_1_
  329.9 12.3 %weight_grad.4 = bf16[4,288,1076]{2,1,0:T(8,128)(2,1)} custom-call(s32[4]{0:T(128)} %get-tuple-element.280.refs_0_, bf16[1152,768]{1,0:T(8,128)(2,1)} %get-tuple-element.200.refs_1_, bf16[1152,768]{1,0:T(8,128)(2,1)} %get-tuple-element.201.refs_2_, bf16[1152,768]{1,0:T(8,128)(2,1)} %get-tuple-element.202.refs_3_, ...), custom_call_target="tpu_custom_call" | custom-call | flops 2480000000 | tf_op jit(solution)/shard_map/weight_grad/pallas_call | solution.py:528
  342.2 12.6 %weight_grad.5 = (f32[4,144,1076]{2,1,0:T(8,128)}, bf16[4,144,1076]{2,1,0:T(8,128)(2,1)}) custom-call(s32[4]{0:T(128)} %get-tuple-element.279.refs_0_, s32[1]{0:T(128)} %bitcast.30.refs_1_, bf16[1152,768]{1,0:T(8,128)(2,1)} %get-tuple-element.194.refs_2_.refs_3_, bf16[1152,768]{1,0:T(8,128)(2,1)} %get-tuple-element.195.refs_3_, ...), custom_call_target="tpu_custom_call" | custom-call | flops 2480000000 | tf_op jit(solution)/shard_map/weight_grad/pallas_call | solution.py:588
  355.7 2.3 add_convert_fusion.refs_1_.refs_12_
  358.0 17.6 %attn_bwd.3 = (bf16[1152,768]{1,0:T(8,128)(2,1)}, f32[288,768]{1,0:T(8,128)}, bf16[864,768]{1,0:T(8,128)(2,1)}, f32[288,768]{1,0:T(8,128)}, f32[288,768]{1,0:T(8...) custom-call(f32[2,288,768]{2,1,0:T(8,128)} %copy-done.7, ...), custom_call_target="tpu_custom_call" | custom-call | flops 3540000000 | tf_op jit(solution)/shard_map/attn_bwd/pallas_call | solution.py:364
  381.4 2.3 fusion.11
  384.6 18.0 %attn_bwd.4 = (bf16[1152,768]{1,0:T(8,128)(2,1)}, f32[288,768]{1,0:T(8,128)}, bf16[864,768]{1,0:T(8,128)(2,1)}, f32[288,768]{1,0:T(8,128)}, f32[288,768]{1,0:T(8...) custom-call(f32[2,288,768]{2,1,0:T(8,128)} %copy-done.6, ...), custom_call_target="tpu_custom_call" | custom-call | flops 3540000000 | tf_op jit(solution)/shard_map/attn_bwd/pallas_call | solution.py:364
  402.6 13.7 %collective-permute-done.38.refs_0_ = bf16[4,144,1076]{2,1,0:T(8,128)(2,1)S(1)} collective-permute-done((bf16[4,144,1076]{2,1,0:T(8,128)(2,1)}, bf16[4,144,1076]{2,1,0:T(8,128)(2,1)S(1)}, u32[]{:S(2)}, u32[]{:S(2)}) %collective-permute-start.38) | collective-permute-done | bytes 1239584 | tf_op jit(solution)/shard_map/ppermute | solution.py:644
  419.9 3.5 fusion.24
  424.4 2.1 collective-permute-start.39
  430.2 5.4 weight_part.3.refs_13_.refs_4_
  435.7 8.1 %weight_part.2.refs_12_.refs_4_ = f32[1152,864]{1,0:T(8,128)} custom-call(bf16[1152,768]{1,0:T(8,128)(2,1)} %get-tuple-element.214.refs_11_.refs_0_, bf16[1152,768]{1,0:T(8,128)(2,1)} %get-tuple-element.215.refs_11_.refs_1_, bf16[864,768]{1,0:T(8,128)(2,1)} %get-tuple-element.218.refs_2_, bf16[864,768]{1,0:T(8,128)(2,1)} %get-tuple-element.222.refs_3_, ...), custom_call_target="tpu_custom_call" | custom-call | flops 1400000000 | tf_op jit(solution)/shard_map/weight_part/pallas_call | solution.py:551
  445.6 17.6 %attn_bwd.5 = (bf16[1152,768]{1,0:T(8,128)(2,1)}, f32[288,768]{1,0:T(8,128)}, bf16[864,768]{1,0:T(8,128)(2,1)}, f32[288,768]{1,0:T(8,128)}, f32[288,768]{1,0:T(8...) custom-call(f32[2,288,768]{2,1,0:T(8,128)} %copy-done.5, ...), custom_call_target="tpu_custom_call" | custom-call | flops 3540000000 | tf_op jit(solution)/shard_map/attn_bwd/pallas_call | solution.py:364
  463.2 7.4 %weight_grad.6 = (f32[4,144,864]{2,1,0:T(8,128)}, bf16[4,144,864]{2,1,0:T(8,128)(2,1)}) custom-call(s32[4]{0:T(128)} %get-tuple-element.279.refs_0_, s32[1]{0:T(128)} %bitcast.30.refs_1_, bf16[1152,768]{1,0:T(8,128)(2,1)} %get-tuple-element.213.refs_11_.refs_2_, bf16[864,768]{1,0:T(8,128)(2,1)} %get-tuple-element.237.refs_3_, ...), custom_call_target="tpu_custom_call" | custom-call | flops 2480000000 | tf_op jit(solution)/shard_map/weight_grad/pallas_call | solution.py:588
  474.1 2.3 fusion.7
  478.5 2.6 collective-permute-done.45
  481.2 2.3 fusion.13.refs_5_
  484.4 5.8 %weight_grad.7 = (f32[4,144,288]{2,1,0:T(8,128)}, bf16[4,144,288]{2,1,0:T(8,128)(2,1)}) custom-call(s32[4]{0:T(128)} %get-tuple-element.279.refs_0_, s32[1]{0:T(128)} %bitcast.30.refs_1_, bf16[1152,768]{1,0:T(8,128)(2,1)} %get-tuple-element.229.refs_2_, bf16[288,768]{1,0:T(8,128)(2,1)} %get-tuple-element.159.refs_9_.refs_4_.refs_3_, ...), custom_call_target="tpu_custom_call" | custom-call | flops 2480000000 | tf_op jit(solution)/shard_map/weight_grad/pallas_call | solution.py:588
  490.8 5.9 %collective-permute-done.47 = bf16[4,144,864]{2,1,0:T(8,128)(2,1)} collective-permute-done((bf16[4,144,864]{2,1,0:T(8,128)(2,1)}, bf16[4,144,864]{2,1,0:T(8,128)(2,1)}, u32[]{:S(2)}, u32[]{:S(2)}) %collective-permute-start.47) | collective-permute-done | bytes 995360 | tf_op jit(solution)/shard_map/ppermute | solution.py:644
  496.7 2.8 fusion.23
  500.4 2.5 collective-permute-start.48
  505.0 3.3 grad.3
  508.3 3.3 grad.4
  511.6 4.4 out.1
  516.7 3.3 grad.5
  520.1 3.0 collective-permute-done.50.refs_2_
  525.6 2.2 collective-permute-start.57
  533.4 1.9 collective-permute-start.54
  (336 shorter events, 95.2 us)
Async XLA Ops:
  7.2 186.7 %all-gather.2.cloned.1.call-start = ((), (), s32[]{:S(2)}) async-start(), calls=%async_computation.1 | async-start | bytes 2985984 | tf_op jit(solution)/shard_map/all_gather | solution.py:759
  7.2 9.4 %collective-permute-start = (bf16[144,288]{1,0:T(8,128)(2,1)}, bf16[144,288]{1,0:T(8,128)(2,1)S(1)}, u32[]{:S(2)}, u32[]{:S(2)}) collective-permute-start(bf16[144,288]{1,0:T(8,128)(2,1)} %bitcast.141), channel_id=1, source_target_pairs={{0,2},{2,0},{1,3},{3,1},{4,6},{6,4},{5,7},{7,5},{8,10},{10,8},{9,1... | collective-permute-start | bytes 248840 | tf_op jit(solution)/shard_map/ppermute | solution.py:26
  17.4 27.0 %collective-permute-start.5 = (bf16[3,288,768]{2,1,0:T(8,128)(2,1)}, bf16[3,288,768]{2,1,0:T(8,128)(2,1)S(1)}, u32[]{:S(2)}, u32[]{:S(2)}) collective-permute-start(bf16[3,288,768]{2,1,0:T(8,128)(2,1)} %get-tuple-element.145), channel_id=1, source_target_pairs={{0,1},{1,0},{2,3},{3,2},{4,5},{5,4},{6,7},{7,6},{8,9},{9,8},{10,11... | collective-permute-start | bytes 3981320 | tf_op jit(solution)/shard_map/ppermute | solution.py:30
  17.4 31.8 %collective-permute-start.1 = (bf16[3,288,768]{2,1,0:T(8,128)(2,1)}, bf16[3,288,768]{2,1,0:T(8,128)(2,1)S(1)}, u32[]{:S(2)}, u32[]{:S(2)}) collective-permute-start(bf16[3,288,768]{2,1,0:T(8,128)(2,1)} %get-tuple-element.145), channel_id=1, source_target_pairs={{0,2},{2,0},{1,3},{3,1},{4,6},{6,4},{5,7},{7,5},{8,10},{10,8},{9,1... | collective-permute-start | bytes 3981320 | tf_op jit(solution)/shard_map/ppermute | solution.py:26
  17.9 11.4 %collective-permute-start.2 = (bf16[144,864]{1,0:T(8,128)(2,1)}, bf16[144,864]{1,0:T(8,128)(2,1)S(1)}, u32[]{:S(2)}, u32[]{:S(2)}) collective-permute-start(bf16[144,864]{1,0:T(8,128)(2,1)} %get-tuple-element.146.refs_1_), channel_id=1, source_target_pairs={{0,8},{4,12},{8,0},{12,4},{16,24},{20,28},{24,16},{28,20},{1,9},{5... | collective-permute-start | bytes 746504 | tf_op jit(solution)/shard_map/ppermute | solution.py:644
  17.9 21.0 %collective-permute-start.3 = (bf16[144,864]{1,0:T(8,128)(2,1)}, bf16[144,864]{1,0:T(8,128)(2,1)}, u32[]{:S(2)}, u32[]{:S(2)}) collective-permute-start(bf16[144,864]{1,0:T(8,128)(2,1)} %get-tuple-element.146.refs_1_), channel_id=1, source_target_pairs={{0,16},{4,20},{8,24},{12,28},{16,0},{20,4},{24,8},{28,12},{1,17},{... | collective-permute-start | bytes 746504 | tf_op jit(solution)/shard_map/ppermute | solution.py:644
  21.0 23.5 %collective-permute-start.4 = (bf16[144,864]{1,0:T(8,128)(2,1)}, bf16[144,864]{1,0:T(8,128)(2,1)}, u32[]{:S(2)}, u32[]{:S(2)}) collective-permute-start(bf16[144,864]{1,0:T(8,128)(2,1)} %get-tuple-element.146.refs_1_), channel_id=1, source_target_pairs={{0,24},{4,28},{8,16},{12,20},{16,8},{20,12},{24,0},{28,4},{1,25},{... | collective-permute-start | bytes 746504 | tf_op jit(solution)/shard_map/ppermute | solution.py:644
  50.2 4.1 collective-permute-start.6
  50.2 29.1 %collective-permute-start.7 = (bf16[4,144,864]{2,1,0:T(8,128)(2,1)}, bf16[4,144,864]{2,1,0:T(8,128)(2,1)}, u32[]{:S(2)}, u32[]{:S(2)}) collective-permute-start(bf16[4,144,864]{2,1,0:T(8,128)(2,1)} %pad_maximum_fusion.1.refs_1_), channel_id=1, source_target_pairs={{0,4},{4,0},{8,12},{12,8},{16,20},{20,16},{24,28},{28,24},{1,5},{5... | collective-permute-start | bytes 2985992 | tf_op jit(solution)/shard_map/ppermute | solution.py:644
  55.4 90.1 %collective-permute-start.18 = (bf16[3,288,768]{2,1,0:T(8,128)(2,1)}, bf16[3,288,768]{2,1,0:T(8,128)(2,1)S(1)}, u32[]{:S(2)}, u32[]{:S(2)}) collective-permute-start(bf16[3,288,768]{2,1,0:T(8,128)(2,1)} %gate.23), channel_id=1, source_target_pairs={{0,2},{2,0},{1,3},{3,1},{4,6},{6,4},{5,7},{7,5},{8,10},{10,8},{9,1... | collective-permute-start | bytes 3981320 | tf_op jit(solution)/shard_map/ppermute | solution.py:26
  56.0 387.8 %reduce-scatter.2.cloned.1.call-start = ((), (), s32[]{:S(2)}) async-start(), calls=%async_computation.2 | async-start | bytes 2985984 | tf_op jit(solution)/shard_map/reduce_scatter | solution.py:683
  58.2 35.8 %collective-permute-start.10 = (bf16[144,1652]{1,0:T(8,128)(2,1)S(1)}, bf16[144,1652]{1,0:T(8,128)(2,1)}, u32[]{:S(2)}, u32[]{:S(2)}) collective-permute-start(bf16[144,1652]{1,0:T(8,128)(2,1)S(1)} %copy-done.15), channel_id=1, source_target_pairs={{0,24},{4,28},{8,16},{12,20},{16,8},{20,12},{24,0},{28,4},{1,25},{... | collective-permute-start | bytes 1427336 | tf_op jit(solution)/shard_map/ppermute | solution.py:644
  59.8 35.3 %collective-permute-start.8 = (bf16[144,1652]{1,0:T(8,128)(2,1)S(1)}, bf16[144,1652]{1,0:T(8,128)(2,1)}, u32[]{:S(2)}, u32[]{:S(2)}) collective-permute-start(bf16[144,1652]{1,0:T(8,128)(2,1)S(1)} %copy-done.15), channel_id=1, source_target_pairs={{0,8},{4,12},{8,0},{12,4},{16,24},{20,28},{24,16},{28,20},{1,9},{5... | collective-permute-start | bytes 1427336 | tf_op jit(solution)/shard_map/ppermute | solution.py:644
  62.3 69.1 %collective-permute-start.9 = (bf16[144,1652]{1,0:T(8,128)(2,1)S(1)}, bf16[144,1652]{1,0:T(8,128)(2,1)}, u32[]{:S(2)}, u32[]{:S(2)}) collective-permute-start(bf16[144,1652]{1,0:T(8,128)(2,1)S(1)} %copy-done.15), channel_id=1, source_target_pairs={{0,16},{4,20},{8,24},{12,28},{16,0},{20,4},{24,8},{28,12},{1,17},{... | collective-permute-start | bytes 1427336 | tf_op jit(solution)/shard_map/ppermute | solution.py:644
  79.3 69.3 %collective-permute-start.11 = (bf16[3,288,768]{2,1,0:T(8,128)(2,1)}, bf16[3,288,768]{2,1,0:T(8,128)(2,1)S(1)}, u32[]{:S(2)}, u32[]{:S(2)}) collective-permute-start(bf16[3,288,768]{2,1,0:T(8,128)(2,1)} %get-tuple-element.158.refs_0_), channel_id=1, source_target_pairs={{0,1},{1,0},{2,3},{3,2},{4,5},{5,4},{6,7},{7,6},{8,9},{9,8},{10,11... | collective-permute-start | bytes 3981320 | tf_op jit(solution)/shard_map/ppermute | solution.py:30
  134.3 46.7 %collective-permute-start.15 = (bf16[4,144,1652]{2,1,0:T(8,128)(2,1)}, bf16[4,144,1652]{2,1,0:T(8,128)(2,1)}, u32[]{:S(2)}, u32[]{:S(2)}) collective-permute-start(bf16[4,144,1652]{2,1,0:T(8,128)(2,1)} %pad_maximum_fusion.refs_8_), channel_id=1, source_target_pairs={{0,4},{4,0},{8,12},{12,8},{16,20},{20,16},{24,28},{28,24},{1,5},{5... | collective-permute-start | bytes 5709320 | tf_op jit(solution)/shard_map/ppermute | solution.py:644
  146.6 31.8 %collective-permute-start.19 = (bf16[3,288,768]{2,1,0:T(8,128)(2,1)}, bf16[3,288,768]{2,1,0:T(8,128)(2,1)S(1)}, u32[]{:S(2)}, u32[]{:S(2)}) collective-permute-start(bf16[3,288,768]{2,1,0:T(8,128)(2,1)} %gate.24.refs_1_), channel_id=1, source_target_pairs={{0,1},{1,0},{2,3},{3,2},{4,5},{5,4},{6,7},{7,6},{8,9},{9,8},{10,11... | collective-permute-start | bytes 3981320 | tf_op jit(solution)/shard_map/ppermute | solution.py:30
  146.6 14.6 %collective-permute-start.17 = (bf16[288,768]{1,0:T(8,128)(2,1)}, bf16[288,768]{1,0:T(8,128)(2,1)S(1)}, u32[]{:S(2)}, u32[]{:S(2)}) collective-permute-start(bf16[288,768]{1,0:T(8,128)(2,1)} %get-tuple-element.161.refs_5_.refs_4_.refs_3_), channel_id=1, source_target_pairs={{0,2},{2,0},{1,3},{3,1},{4,6},{6,4},{5,7},{7,5},{8,10},{10,8},{9,1... | collective-permute-start | bytes 1327112 | tf_op jit(solution)/shard_map/ppermute | solution.py:26
  148.1 21.1 %collective-permute-start.16 = (bf16[288,768]{1,0:T(8,128)(2,1)S(1)}, bf16[288,768]{1,0:T(8,128)(2,1)S(1)}, u32[]{:S(2)}, u32[]{:S(2)}) collective-permute-start(bf16[288,768]{1,0:T(8,128)(2,1)S(1)} %copy-done.19), channel_id=1, source_target_pairs={{0,2},{2,0},{1,3},{3,1},{4,6},{6,4},{5,7},{7,5},{8,10},{10,8},{9,1... | collective-permute-start | bytes 1327112 | tf_op jit(solution)/shard_map/ppermute | solution.py:26
  159.7 18.7 %collective-permute-start.12 = (bf16[288,768]{1,0:T(8,128)(2,1)}, bf16[288,768]{1,0:T(8,128)(2,1)S(1)}, u32[]{:S(2)}, u32[]{:S(2)}) collective-permute-start(bf16[288,768]{1,0:T(8,128)(2,1)} %get-tuple-element.159.refs_9_.refs_4_.refs_3_), channel_id=1, source_target_pairs={{0,2},{2,0},{1,3},{3,1},{4,6},{6,4},{5,7},{7,5},{8,10},{10,8},{9,1... | collective-permute-start | bytes 1327112 | tf_op jit(solution)/shard_map/ppermute | solution.py:26
  161.2 18.3 %collective-permute-start.13 = (bf16[288,768]{1,0:T(8,128)(2,1)}, bf16[288,768]{1,0:T(8,128)(2,1)S(1)}, u32[]{:S(2)}, u32[]{:S(2)}) collective-permute-start(bf16[288,768]{1,0:T(8,128)(2,1)} %get-tuple-element.159.refs_9_.refs_4_.refs_3_), channel_id=1, source_target_pairs={{0,1},{1,0},{2,3},{3,2},{4,5},{5,4},{6,7},{7,6},{8,9},{9,8},{10,11... | collective-permute-start | bytes 1327112 | tf_op jit(solution)/shard_map/ppermute | solution.py:30
  169.3 11.5 %collective-permute-start.22 = (bf16[288,768]{1,0:T(8,128)(2,1)}, bf16[288,768]{1,0:T(8,128)(2,1)}, u32[]{:S(2)}, u32[]{:S(2)}) collective-permute-start(bf16[288,768]{1,0:T(8,128)(2,1)} %get-tuple-element.161.refs_5_.refs_4_.refs_3_), channel_id=1, source_target_pairs={{0,1},{1,0},{2,3},{3,2},{4,5},{5,4},{6,7},{7,6},{8,9},{9,8},{10,11... | collective-permute-start | bytes 1327112 | tf_op jit(solution)/shard_map/ppermute | solution.py:30
  178.4 2.4 collective-permute-start.20
  178.4 2.5 collective-permute-start.14
  180.3 2.1 collective-permute-start.21
  180.8 2.3 collective-permute-start.23
  191.7 6.8 %collective-permute-start.24 = (bf16[1152,576]{0,1:T(8,128)(2,1)S(1)}, bf16[1152,576]{0,1:T(8,128)(2,1)S(1)}, u32[]{:S(2)}, u32[]{:S(2)}) collective-permute-start(bf16[1152,576]{0,1:T(8,128)(2,1)S(1)} %copy.98), channel_id=1, source_target_pairs={{0,1},{1,0},{2,3},{3,2},{4,5},{5,4},{6,7},{7,6},{8,9},{9,8},{10,11... | collective-permute-start | bytes 3981320 | tf_op jit(solution)/shard_map/ppermute | solution.py:30
  235.2 2.6 collective-permute-start.25
  239.5 22.8 %copy-start.7 = (f32[2,288,768]{2,1,0:T(8,128)}, f32[2,288,768]{2,1,0:T(8,128)S(1)}, u32[]{:S(2)}) copy-start(f32[2,288,768]{2,1,0:T(8,128)S(1)} %convert_add_fusion.5.refs_0_) | copy-start | bytes 5308420
  239.7 21.8 %collective-permute-start.26 = (bf16[2,288,768]{2,1,0:T(8,128)(2,1)S(1)}, bf16[2,288,768]{2,1,0:T(8,128)(2,1)S(1)}, u32[]{:S(2)}, u32[]{:S(2)}) collective-permute-start(bf16[2,288,768]{2,1,0:T(8,128)(2,1)S(1)} %rev.17.refs_16_), channel_id=1, source_target_pairs={{0,2},{2,0},{1,3},{3,1},{4,6},{6,4},{5,7},{7,5},{8,10},{10,8},{9,1... | collective-permute-start | bytes 2654216 | tf_op jit(solution)/shard_map/ppermute | solution.py:26
  276.1 3.2 collective-permute-start.27
  276.1 7.4 %collective-permute-start.28 = (bf16[2,288,768]{2,1,0:T(8,128)(2,1)S(1)}, bf16[2,288,768]{2,1,0:T(8,128)(2,1)}, u32[]{:S(2)}, u32[]{:S(2)}) collective-permute-start(bf16[2,288,768]{2,1,0:T(8,128)(2,1)S(1)} %copy-done.24), channel_id=1, source_target_pairs={{0,1},{1,0},{2,3},{3,2},{4,5},{5,4},{6,7},{7,6},{8,9},{9,8},{10,11... | collective-permute-start | bytes 2654216 | tf_op jit(solution)/shard_map/ppermute | solution.py:30
  280.9 23.9 %copy-start.6 = (f32[2,288,768]{2,1,0:T(8,128)}, f32[2,288,768]{2,1,0:T(8,128)S(1)}, u32[]{:S(2)}) copy-start(f32[2,288,768]{2,1,0:T(8,128)S(1)} %convert_add_fusion.4.refs_0_) | copy-start | bytes 5308420
  282.0 21.9 %collective-permute-start.29 = (bf16[2,288,768]{2,1,0:T(8,128)(2,1)}, bf16[2,288,768]{2,1,0:T(8,128)(2,1)S(1)}, u32[]{:S(2)}, u32[]{:S(2)}) collective-permute-start(bf16[2,288,768]{2,1,0:T(8,128)(2,1)} %rev.16.refs_16_), channel_id=1, source_target_pairs={{0,2},{2,0},{1,3},{3,1},{4,6},{6,4},{5,7},{7,5},{8,10},{10,8},{9,1... | collective-permute-start | bytes 2654216 | tf_op jit(solution)/shard_map/ppermute | solution.py:26
  304.8 21.6 %collective-permute-start.30 = (bf16[3,2,288,768]{3,2,1,0:T(8,128)(2,1)}, bf16[3,2,288,768]{3,2,1,0:T(8,128)(2,1)}, u32[]{:S(2)}, u32[]{:S(2)}) collective-permute-start(bf16[3,2,288,768]{3,2,1,0:T(8,128)(2,1)} %get-tuple-element.188), channel_id=1, source_target_pairs={{0,1},{1,0},{2,3},{3,2},{4,5},{5,4},{6,7},{7,6},{8,9},{9,8},{10,11... | collective-permute-start | bytes 7962632 | tf_op jit(solution)/shard_map/ppermute | solution.py:30
  318.1 4.0 collective-permute-start.31
  318.6 11.3 %collective-permute-start.33 = (bf16[2,288,768]{2,1,0:T(8,128)(2,1)}, bf16[2,288,768]{2,1,0:T(8,128)(2,1)}, u32[]{:S(2)}, u32[]{:S(2)}) collective-permute-start(bf16[2,288,768]{2,1,0:T(8,128)(2,1)} %add_convert_fusion.1.refs_7_), channel_id=1, source_target_pairs={{0,1},{1,0},{2,3},{3,2},{4,5},{5,4},{6,7},{7,6},{8,9},{9,8},{10,11... | collective-permute-start | bytes 2654216 | tf_op jit(solution)/shard_map/ppermute | solution.py:30
  323.7 32.0 %copy-start.5 = (f32[2,288,768]{2,1,0:T(8,128)}, f32[2,288,768]{2,1,0:T(8,128)S(1)}, u32[]{:S(2)}) copy-start(f32[2,288,768]{2,1,0:T(8,128)S(1)} %convert_add_fusion.3.refs_0_) | copy-start | bytes 5308420
  324.9 29.9 %collective-permute-start.32 = (bf16[2,288,768]{2,1,0:T(8,128)(2,1)}, bf16[2,288,768]{2,1,0:T(8,128)(2,1)S(1)}, u32[]{:S(2)}, u32[]{:S(2)}) collective-permute-start(bf16[2,288,768]{2,1,0:T(8,128)(2,1)} %rev.15.refs_1_.refs_7_), channel_id=1, source_target_pairs={{0,2},{2,0},{1,3},{3,1},{4,6},{6,4},{5,7},{7,5},{8,10},{10,8},{9,1... | collective-permute-start | bytes 2654216 | tf_op jit(solution)/shard_map/ppermute | solution.py:26
  375.6 5.7 %collective-permute-start.36 = (bf16[2,288,768]{2,1,0:T(8,128)(2,1)}, bf16[2,288,768]{2,1,0:T(8,128)(2,1)S(1)}, u32[]{:S(2)}, u32[]{:S(2)}) collective-permute-start(bf16[2,288,768]{2,1,0:T(8,128)(2,1)} %get-tuple-element.224), channel_id=1, source_target_pairs={{0,1},{1,0},{2,3},{3,2},{4,5},{5,4},{6,7},{7,6},{8,9},{9,8},{10,11... | collective-permute-start | bytes 2654216 | tf_op jit(solution)/shard_map/ppermute | solution.py:30
  375.8 41.6 %collective-permute-start.34 = (bf16[3,288,768]{2,1,0:T(8,128)(2,1)}, bf16[3,288,768]{2,1,0:T(8,128)(2,1)S(1)}, u32[]{:S(2)}, u32[]{:S(2)}) collective-permute-start(bf16[3,288,768]{2,1,0:T(8,128)(2,1)} %gate.31), channel_id=1, source_target_pairs={{0,2},{2,0},{1,3},{3,1},{4,6},{6,4},{5,7},{7,5},{8,10},{10,8},{9,1... | collective-permute-start | bytes 3981320 | tf_op jit(solution)/shard_map/ppermute | solution.py:26
  376.2 40.1 %collective-permute-start.38 = (bf16[4,144,1076]{2,1,0:T(8,128)(2,1)}, bf16[4,144,1076]{2,1,0:T(8,128)(2,1)S(1)}, u32[]{:S(2)}, u32[]{:S(2)}) collective-permute-start(bf16[4,144,1076]{2,1,0:T(8,128)(2,1)} %get-tuple-element.206.refs_2_.refs_13_), channel_id=1, source_target_pairs={{0,4},{4,0},{8,12},{12,8},{16,20},{20,16},{24,28},{28,24},{1,5},{5... | collective-permute-start | bytes 3718664 | tf_op jit(solution)/shard_map/ppermute | solution.py:644
  377.6 6.1 %collective-permute-start.35 = (bf16[2,288,768]{2,1,0:T(8,128)(2,1)S(1)}, bf16[2,288,768]{2,1,0:T(8,128)(2,1)S(1)}, u32[]{:S(2)}, u32[]{:S(2)}) collective-permute-start(bf16[2,288,768]{2,1,0:T(8,128)(2,1)S(1)} %copy-done.10), channel_id=1, source_target_pairs={{0,1},{1,0},{2,3},{3,2},{4,5},{5,4},{6,7},{7,6},{8,9},{9,8},{10,11... | collective-permute-start | bytes 2654216 | tf_op jit(solution)/shard_map/ppermute | solution.py:30
  418.5 9.4 %collective-permute-start.37 = (bf16[2,288,768]{2,1,0:T(8,128)(2,1)}, bf16[2,288,768]{2,1,0:T(8,128)(2,1)S(1)}, u32[]{:S(2)}, u32[]{:S(2)}) collective-permute-start(bf16[2,288,768]{2,1,0:T(8,128)(2,1)} %gate.32), channel_id=1, source_target_pairs={{0,1},{1,0},{2,3},{3,2},{4,5},{5,4},{6,7},{7,6},{8,9},{9,8},{10,11... | collective-permute-start | bytes 2654216 | tf_op jit(solution)/shard_map/ppermute | solution.py:30
  424.4 48.4 %collective-permute-start.39 = (bf16[144,1076]{1,0:T(8,128)(2,1)}, bf16[144,1076]{1,0:T(8,128)(2,1)S(1)}, u32[]{:S(2)}, u32[]{:S(2)}) collective-permute-start(bf16[144,1076]{1,0:T(8,128)(2,1)} %get-tuple-element.283), channel_id=1, source_target_pairs={{0,8},{4,12},{8,0},{12,4},{16,24},{20,28},{24,16},{28,20},{1,9},{5... | collective-permute-start | bytes 929672 | tf_op jit(solution)/shard_map/ppermute | solution.py:644
  426.5 46.4 %collective-permute-start.40 = (bf16[144,1076]{1,0:T(8,128)(2,1)}, bf16[144,1076]{1,0:T(8,128)(2,1)}, u32[]{:S(2)}, u32[]{:S(2)}) collective-permute-start(bf16[144,1076]{1,0:T(8,128)(2,1)} %get-tuple-element.282), channel_id=1, source_target_pairs={{0,16},{4,20},{8,24},{12,28},{16,0},{20,4},{24,8},{28,12},{1,17},{... | collective-permute-start | bytes 929672 | tf_op jit(solution)/shard_map/ppermute | solution.py:644
  427.1 45.7 %collective-permute-start.41 = (bf16[144,1076]{1,0:T(8,128)(2,1)}, bf16[144,1076]{1,0:T(8,128)(2,1)}, u32[]{:S(2)}, u32[]{:S(2)}) collective-permute-start(bf16[144,1076]{1,0:T(8,128)(2,1)} %get-tuple-element.281), channel_id=1, source_target_pairs={{0,24},{4,28},{8,16},{12,20},{16,8},{20,12},{24,0},{28,4},{1,25},{... | collective-permute-start | bytes 929672 | tf_op jit(solution)/shard_map/ppermute | solution.py:644
  428.9 74.9 %collective-permute-start.46 = (bf16[2,288,768]{2,1,0:T(8,128)(2,1)S(1)}, bf16[2,288,768]{2,1,0:T(8,128)(2,1)S(1)}, u32[]{:S(2)}, u32[]{:S(2)}) collective-permute-start(bf16[2,288,768]{2,1,0:T(8,128)(2,1)S(1)} %pad_maximum_fusion.2.refs_4_), channel_id=1, source_target_pairs={{0,2},{2,0},{1,3},{3,1},{4,6},{6,4},{5,7},{7,5},{8,10},{10,8},{9,1... | collective-permute-start | bytes 2654216 | tf_op jit(solution)/shard_map/ppermute | solution.py:26
  470.7 26.1 %collective-permute-start.47 = (bf16[4,144,864]{2,1,0:T(8,128)(2,1)}, bf16[4,144,864]{2,1,0:T(8,128)(2,1)}, u32[]{:S(2)}, u32[]{:S(2)}) collective-permute-start(bf16[4,144,864]{2,1,0:T(8,128)(2,1)} %get-tuple-element.239.refs_5_), channel_id=1, source_target_pairs={{0,4},{4,0},{8,12},{12,8},{16,20},{20,16},{24,28},{28,24},{1,5},{5... | collective-permute-start | bytes 2985992 | tf_op jit(solution)/shard_map/ppermute | solution.py:644
  473.6 3.1 collective-permute-start.44
  473.6 7.5 %collective-permute-start.42 = (bf16[2,288,768]{2,1,0:T(8,128)(2,1)}, bf16[2,288,768]{2,1,0:T(8,128)(2,1)S(1)}, u32[]{:S(2)}, u32[]{:S(2)}) collective-permute-start(bf16[2,288,768]{2,1,0:T(8,128)(2,1)} %get-tuple-element.240), channel_id=1, source_target_pairs={{0,1},{1,0},{2,3},{3,2},{4,5},{5,4},{6,7},{7,6},{8,9},{9,8},{10,11... | collective-permute-start | bytes 2654216 | tf_op jit(solution)/shard_map/ppermute | solution.py:30
  476.7 4.4 collective-permute-start.45
  483.5 32.4 %collective-permute-start.43 = (bf16[1,288,768]{2,1,0:T(8,128)(2,1)}, bf16[1,288,768]{2,1,0:T(8,128)(2,1)S(1)}, u32[]{:S(2)}, u32[]{:S(2)}) collective-permute-start(bf16[1,288,768]{2,1,0:T(8,128)(2,1)} %fusion.13.refs_5_), channel_id=1, source_target_pairs={{0,2},{2,0},{1,3},{3,1},{4,6},{6,4},{5,7},{7,5},{8,10},{10,8},{9,1... | collective-permute-start | bytes 1327112 | tf_op jit(solution)/shard_map/ppermute | solution.py:26
  490.3 29.8 %collective-permute-start.51 = (bf16[4,144,288]{2,1,0:T(8,128)(2,1)}, bf16[4,144,288]{2,1,0:T(8,128)(2,1)S(1)}, u32[]{:S(2)}, u32[]{:S(2)}) collective-permute-start(bf16[4,144,288]{2,1,0:T(8,128)(2,1)} %get-tuple-element.241.refs_1_.refs_4_), channel_id=1, source_target_pairs={{0,4},{4,0},{8,12},{12,8},{16,20},{20,16},{24,28},{28,24},{1,5},{5... | collective-permute-start | bytes 995336 | tf_op jit(solution)/shard_map/ppermute | solution.py:644
  500.4 19.6 %collective-permute-start.48 = (bf16[144,864]{1,0:T(8,128)(2,1)}, bf16[144,864]{1,0:T(8,128)(2,1)S(1)}, u32[]{:S(2)}, u32[]{:S(2)}) collective-permute-start(bf16[144,864]{1,0:T(8,128)(2,1)} %get-tuple-element.286), channel_id=1, source_target_pairs={{0,8},{4,12},{8,0},{12,4},{16,24},{20,28},{24,16},{28,20},{1,9},{5... | collective-permute-start | bytes 746504 | tf_op jit(solution)/shard_map/ppermute | solution.py:644
  502.9 17.1 %collective-permute-start.49 = (bf16[144,864]{1,0:T(8,128)(2,1)}, bf16[144,864]{1,0:T(8,128)(2,1)S(1)}, u32[]{:S(2)}, u32[]{:S(2)}) collective-permute-start(bf16[144,864]{1,0:T(8,128)(2,1)} %get-tuple-element.285), channel_id=1, source_target_pairs={{0,16},{4,20},{8,24},{12,28},{16,0},{20,4},{24,8},{28,12},{1,17},{... | collective-permute-start | bytes 746504 | tf_op jit(solution)/shard_map/ppermute | solution.py:644
  503.8 19.3 %collective-permute-start.50 = (bf16[144,864]{1,0:T(8,128)(2,1)}, bf16[144,864]{1,0:T(8,128)(2,1)S(1)}, u32[]{:S(2)}, u32[]{:S(2)}) collective-permute-start(bf16[144,864]{1,0:T(8,128)(2,1)} %get-tuple-element.284), channel_id=1, source_target_pairs={{0,24},{4,28},{8,16},{12,20},{16,8},{20,12},{24,0},{28,4},{1,25},{... | collective-permute-start | bytes 746504 | tf_op jit(solution)/shard_map/ppermute | solution.py:644
  525.4 15.0 %collective-permute-start.56 = (bf16[144,288]{1,0:T(8,128)(2,1)S(1)}, bf16[144,288]{1,0:T(8,128)(2,1)S(1)}, u32[]{:S(2)}, u32[]{:S(2)}) collective-permute-start(bf16[144,288]{1,0:T(8,128)(2,1)S(1)} %get-tuple-element.290), channel_id=1, source_target_pairs={{0,8},{4,12},{8,0},{12,4},{16,24},{20,28},{24,16},{28,20},{1,9},{5... | collective-permute-start | bytes 248840 | tf_op jit(solution)/shard_map/ppermute | solution.py:644
  525.6 14.8 %collective-permute-start.57 = (bf16[144,288]{1,0:T(8,128)(2,1)S(1)}, bf16[144,288]{1,0:T(8,128)(2,1)S(1)}, u32[]{:S(2)}, u32[]{:S(2)}) collective-permute-start(bf16[144,288]{1,0:T(8,128)(2,1)S(1)} %get-tuple-element.292), channel_id=1, source_target_pairs={{0,16},{4,20},{8,24},{12,28},{16,0},{20,4},{24,8},{28,12},{1,17},{... | collective-permute-start | bytes 248840 | tf_op jit(solution)/shard_map/ppermute | solution.py:644
  528.7 3.9 collective-permute-start.52
  532.6 4.6 collective-permute-start.53
  533.4 5.0 collective-permute-start.54
  535.3 3.7 collective-permute-start.55
  537.2 4.7 collective-permute-start.58
  (68 other events, 283.5 us)
Sparse Core Ops, SparseCore 0:
  56.1 76.9 all-gather.1
  342.3 79.0 reduce-scatter.1
